TPU v7x, 32 devices: a whole 2x2x4 slice. The times are simulated.
32 devices in a mesh: seq: 8 (over y, x, core), dp: 4 (over z).
Axes of the slice: x: 2, y: 2, z: 4, core: 2. Of those that a mesh axis runs over, the one named last changes fastest.
Arguments:
- tokens: bfloat16 [12, 1024, 1024], P('dp', 'seq'), may hold values from -6 to 6
- first_values: bfloat16 [12, 1024, 1024], P('dp', 'seq'), may hold values from -6 to 6
- out_grad: bfloat16 [12, 1024, 1024], P('dp', 'seq'), may hold values from -6 to 6
- lengths: int32 [12], P('dp'), may hold values from 1 to 1024, as said below
- norm1_gain: bfloat16 [1024], P(('seq', 'dp')), may hold values from 0.099609375 to 1.8984375
- qkv_weight: bfloat16 [1024, 3072], P(('seq', 'dp')), may hold values from -0.1875 to 0.1875
- out_weight: bfloat16 [1024, 1024], P(('seq', 'dp')), may hold values from -1.5 to 1.5
- norm2_gain: bfloat16 [1024], P(('seq', 'dp')), may hold values from 0.099609375 to 1.8984375
- gate_weight: bfloat16 [1024, 2816], P(('seq', 'dp')), may hold values from -0.1875 to 0.1875
- up_weight: bfloat16 [1024, 2816], P(('seq', 'dp')), may hold values from -0.1875 to 0.1875
- down_weight: bfloat16 [2816, 1024], P(('seq', 'dp')), may hold values from -0.109375 to 0.109375
Outputs:
- output: bfloat16 [12, 1024, 1024], P('dp', 'seq')
- tokens_grad: float32 [12, 1024, 1024], P('dp', 'seq')
- first_values_grad: float32 [12, 1024, 1024], P('dp', 'seq')
- norm1_gain_grad: float32 [1024], P(('seq', 'dp'))
- qkv_weight_grad: float32 [1024, 3072], P(('seq', 'dp'))
- out_weight_grad: float32 [1024, 1024], P(('seq', 'dp'))
- norm2_gain_grad: float32 [1024], P(('seq', 'dp'))
- gate_weight_grad: float32 [1024, 2816], P(('seq', 'dp'))
- up_weight_grad: float32 [1024, 2816], P(('seq', 'dp'))
- down_weight_grad: float32 [2816, 1024], P(('seq', 'dp'))
Inputs may be any that keep to these rules, and one draw needn't show every extreme that they name: `lengths`: real tokens of a slot; within each index of dp one of its 3 slots, drawn from the seed, is full.
All inputs are finite; a program needn't handle non-finite values.
Results may differ from a plain program's by a relative error of at most 0.025.
Values may be sent and summed in bfloat16 or wider, within the bound.
No kernel may reach another device: no remote copies, remote signals or barrier semaphores. Data moves between devices by JAX's collectives and lax.ppermute only.
A program may use at most 320 MiB of HBM per device.

v0:
```python
import functools

import jax
import jax.numpy as jnp
import numpy as np
from jax import lax
from jax.experimental import pallas as pl
from jax.experimental.pallas import tpu as pltpu
from jax.sharding import PartitionSpec as P

HEADS = 16
HEAD_DIM = 64
EPSILON = 1e-06
CORES = 2
OUTER = 2
BLOCK = 256
NEG = -1e30
F32 = jnp.float32
BF16 = jnp.bfloat16
MIB = 1024 * 1024
FREE = pl.CostEstimate(flops=0, bytes_accessed=0, transcendentals=0)


def lasting(us):
    return pl.CostEstimate(flops=0, bytes_accessed=int(us * 3.69e6), transcendentals=0)


def vmem(mib, scale=1):
    return pltpu.CompilerParams(vmem_limit_bytes=int(min(60, mib * max(scale, 1))) * MIB)


def held_in_hbm(*arrays):
    return [pltpu.with_memory_space_constraint(a, pltpu.HBM) for a in arrays]


class Copies:
    def __init__(self, sems):
        self.sems, self.used, self.waiting = sems, 0, {}

    def start(self, name, src, dst):
        copy = pltpu.make_async_copy(src, dst, self.sems.at[self.used])
        self.used += 1
        copy.start()
        self.waiting.setdefault(name, []).append(copy)

    def wait(self, *names):
        for name in names or list(self.waiting):
            for copy in self.waiting.pop(name, []):
                copy.wait()


def corner(a):
    block = (1,) * (a.ndim - 2) + (min(16, a.shape[-2]), min(128, a.shape[-1]))
    return pl.BlockSpec(block, lambda *_: (0,) * a.ndim)


def dot_nn(a, b):
    return lax.dot_general(a, b, (((1,), (0,)), ((), ())), preferred_element_type=F32)


def dot_nt(a, b):
    return lax.dot_general(a, b, (((1,), (1,)), ((), ())), preferred_element_type=F32)


def dot_tn(a, b):
    return lax.dot_general(a, b, (((0,), (0,)), ((), ())), preferred_element_type=F32)


def turned(u):
    half = HEAD_DIM // 2
    width = u.shape[1]
    if width % 128:
        parts = []
        for h in range(width // HEAD_DIM):
            lo = h * HEAD_DIM
            parts += [u[:, lo + half : lo + HEAD_DIM], u[:, lo : lo + half]]
        return jnp.concatenate(parts, axis=1)
    lane = lax.broadcasted_iota(jnp.int32, u.shape, 1) % HEAD_DIM
    return jnp.where(lane < half, pltpu.roll(u, width - half, 1), pltpu.roll(u, half, 1))


def head_mask(shape, h):
    lane = lax.broadcasted_iota(jnp.int32, shape, 1)
    return (lane >= h * HEAD_DIM) & (lane < (h + 1) * HEAD_DIM)


def own_head(u, h):
    if u.shape[1] == HEAD_DIM:
        return u
    return jnp.where(head_mask(u.shape, h), u, jnp.zeros_like(u))


def join_heads(parts):
    out = parts[0]
    for h in range(1, len(parts)):
        out = jnp.where(head_mask(out.shape, h), parts[h], out)
    return out


def fill_rows(seat, refs, order, dest):
    rows = refs[0].shape[1]
    for ref, (m, lane) in zip(refs, order):
        at = pl.multiple_of((seat ^ m) * rows, rows)
        dest[pl.ds(at, rows), lane : lane + ref.shape[2]] = ref[0]


def attn_fwd_kernel(
    order, seat_ref, len_ref, w_ref, cos_ref, sin_ref, *refs,
):
    xs = refs[: len(order)]
    spread = len(refs) - len(order) - 6
    qkv_out, ot_out = refs[len(order) : len(order) + 2]
    sends = refs[len(order) + 2 : len(order) + 2 + spread]
    lse_out, r1_out, xbuf, vt = refs[-4:]
    slot = pl.program_id(0)
    seat = seat_ref[0]
    length = len_ref[slot]
    total = xbuf.shape[0]
    width = w_ref.shape[0]
    wide = w_ref.shape[1] // 3
    heads = wide // HEAD_DIM
    blocks = total // BLOCK
    fill_rows(seat, xs, order, xbuf)
    for b in range(blocks):
        at = slice(b * BLOCK, (b + 1) * BLOCK)
        x = xbuf[at, :width]
        xf = x.astype(F32)
        r1 = lax.rsqrt(jnp.mean(xf * xf, axis=1, keepdims=True) + EPSILON)
        qkv = dot_nn(x, w_ref[...]) * r1
        cosine = cos_ref[at, :]
        sine = sin_ref[at, :]
        q = qkv[:, :wide]
        k = qkv[:, wide : 2 * wide]
        v = qkv[:, 2 * wide :]
        q = (q * cosine + turned(q) * sine) * (HEAD_DIM**-0.5)
        k = k * cosine + turned(k) * sine
        first = xbuf[at, width : width + wide]
        second = xbuf[at, width + wide :]
        v1 = jnp.where(seat % CORES == 0, first, second).astype(F32)
        vm = 0.5 * v + 0.5 * v1
        qkv_out[0, at, :wide] = q.astype(BF16)
        qkv_out[0, at, wide : 2 * wide] = k.astype(BF16)
        qkv_out[0, at, 2 * wide :] = vm.astype(BF16)
        vt[:, at] = vm.T.astype(BF16)
        r1_out[0, at, :] = jnp.broadcast_to(r1, (BLOCK, r1_out.shape[2]))
    for b in range(blocks):
        at = slice(b * BLOCK, (b + 1) * BLOCK)
        count = (b + 1) * BLOCK
        q = qkv_out[0, at, :wide]
        query = b * BLOCK + lax.broadcasted_iota(jnp.int32, (1, BLOCK), 1)
        last = jnp.minimum(query, length - 1)
        key = lax.broadcasted_iota(jnp.int32, (count, BLOCK), 0)
        allowed = key <= last
        ots = []
        for h in range(heads):
            k = own_head(qkv_out[0, :count, wide : 2 * wide], h)
            scores = jnp.where(allowed, dot_nt(k, q), NEG)
            top = jnp.max(scores, axis=0, keepdims=True)
            weights = jnp.exp(scores - top)
            total_w = jnp.sum(weights, axis=0, keepdims=True)
            ot = dot_nn(vt[h * HEAD_DIM : (h + 1) * HEAD_DIM, :count], weights.astype(BF16))
            ots.append(ot / total_w)
            lse_out[0, h : h + 1, at] = top + jnp.log(total_w)
        ot = jnp.concatenate(ots, axis=0)
        ot_out[0, :, at] = ot
        o = ot.T.astype(BF16)
        for x in range(spread):
            sends[x ^ (b % spread)][(b // spread) * spread + x, 0] = o


def chunk_specs(xs, order, lanes):
    return [
        pl.BlockSpec((1, x.shape[1], min(x.shape[2], lanes - lane)), lambda i: (i, 0, 0))
        for x, (_, lane) in zip(xs, order)
    ]


def attn_fwd(seat, lengths, xs, w, cosine, sine, order, ready):
    micro, rows, lanes = xs[0].shape
    width = w.shape[0]
    total = cosine.shape[0]
    spread = total // rows // (OUTER * CORES)
    wide = w.shape[1] // 3
    heads = wide // HEAD_DIM
    smem = pl.BlockSpec(memory_space=pltpu.SMEM)
    whole = lambda a: pl.BlockSpec(a.shape, lambda i: (0,) * a.ndim)
    pairs = total * total // 2 * micro * wide
    return pl.pallas_call(
        functools.partial(attn_fwd_kernel, order),
        grid=(micro,),
        in_specs=[smem, smem, whole(w), whole(cosine), whole(sine)]
        + chunk_specs(xs, order, lanes)
        + [corner(a) for a in ready],
        out_specs=[
            pl.BlockSpec((1, total, 3 * wide), lambda i: (i, 0, 0)),
            pl.BlockSpec((1, wide, total), lambda i: (i, 0, 0)),
        ]
        + [pl.BlockSpec((OUTER * spread, 1, BLOCK, wide), lambda i: (0, i, 0, 0))] * spread
        + [
            pl.BlockSpec((1, heads, total), lambda i: (i, 0, 0)),
            pl.BlockSpec((1, total, 128), lambda i: (i, 0, 0)),
        ],
        out_shape=[
            pltpu.HBM((micro, total, 3 * wide), BF16),
            pltpu.HBM((micro, wide, total), F32),
        ]
        + [pltpu.HBM((OUTER * spread, micro, BLOCK, wide), BF16)] * spread
        + [
            pltpu.HBM((micro, heads, total), F32),
            pltpu.HBM((micro, total, 128), F32),
        ],
        scratch_shapes=[pltpu.VMEM((total, lanes), BF16), pltpu.VMEM((wide, total), BF16)],
        compiler_params=vmem(30, total / 1024),
        cost_estimate=lasting(20),
        name="attn_fwd",
    )(seat, lengths, *held_in_hbm(w, cosine, sine, *xs), *ready)


def attn_bwd_kernel(
    order, sent, seat_ref, len_ref, do_ref, cos_ref, sin_ref, qkv_ref, ot_ref, lse_ref, r1_ref,
    *refs,
):
    xs = refs[: len(order)]
    outs = refs[-6 - CORES : -6]
    dw_out, xbuf, dobuf, dqt, ebuf, dw = refs[-6:]
    slot = pl.program_id(0)
    seat = seat_ref[0]
    rows = do_ref.shape[2]
    length = len_ref[slot]
    total = xbuf.shape[0]
    wide = do_ref.shape[3]
    heads = wide // HEAD_DIM
    blocks = total // BLOCK
    fill_rows(seat, xs, order, xbuf)
    for j in range(do_ref.shape[0]):
        dobuf[j * rows : (j + 1) * rows, :] = do_ref[j, 0]
    dot_t = dobuf[...].astype(F32).T
    deltas = []
    for h in range(heads):
        part = slice(h * HEAD_DIM, (h + 1) * HEAD_DIM)
        deltas.append(jnp.sum(dot_t[part, :] * ot_ref[0, part, :], axis=0, keepdims=True))
    dqt[...] = jnp.zeros_like(dqt)
    for b in range(blocks):
        at = slice(b * BLOCK, (b + 1) * BLOCK)
        later = slice(b * BLOCK, total)
        count = total - b * BLOCK
        k = qkv_ref[0, at, wide : 2 * wide]
        v = qkv_ref[0, at, 2 * wide :]
        kt = k.astype(F32).T.astype(BF16)
        q = qkv_ref[0, later, :wide]
        d_o = dobuf[later, :]
        query = b * BLOCK + lax.broadcasted_iota(jnp.int32, (1, count), 1)
        last = jnp.minimum(query, length - 1)
        key = b * BLOCK + lax.broadcasted_iota(jnp.int32, (BLOCK, count), 0)
        allowed = key <= last
        dks, dvs = [], []
        for h in range(heads):
            part = slice(h * HEAD_DIM, (h + 1) * HEAD_DIM)
            scores = jnp.where(allowed, dot_nt(own_head(k, h), q), NEG)
            weights = jnp.exp(scores - lse_ref[0, h : h + 1, later])
            d_weights = dot_nt(own_head(v, h), d_o)
            ds = (weights * (d_weights - deltas[h][:, later])).astype(BF16)
            dvs.append(dot_nn(weights.astype(BF16), d_o))
            dks.append(dot_nn(ds, q))
            dqt[part, later] += dot_nn(kt[part, :], ds)
        cosine = cos_ref[at, :]
        sine = sin_ref[at, :]
        r1 = r1_ref[0, at, 0:1]
        dk = join_heads(dks)
        dk = dk * cosine - turned(dk) * sine
        dv = 0.5 * join_heads(dvs)
        ebuf[at, 3 * wide :] = dv.astype(BF16)
        ebuf[at, wide : 2 * wide] = (dk * r1).astype(BF16)
        ebuf[at, 2 * wide : 3 * wide] = (dv * r1).astype(BF16)
    for b in range(blocks):
        at = slice(b * BLOCK, (b + 1) * BLOCK)
        dq = dqt[:, at].T * (HEAD_DIM**-0.5)
        dq = dq * cos_ref[at, :] - turned(dq) * sin_ref[at, :]
        ebuf[at, :wide] = (dq * r1_ref[0, at, 0:1]).astype(BF16)
    for low, out in enumerate(outs):
        for j, m in enumerate(sent):
            at = pl.multiple_of((seat ^ m ^ low) * rows, rows)
            out[j, 0] = ebuf[pl.ds(at, rows), :]
    grown = dot_tn(xbuf[...], ebuf[:, : 3 * wide])

    @pl.when(slot == 0)
    def _():
        dw[...] = grown

    @pl.when(slot > 0)
    def _():
        dw[...] += grown

    @pl.when(slot == pl.num_programs(0) - 1)
    def _():
        dw_out[...] = dw[...].astype(BF16)


def attn_bwd(seat, lengths, xs, wshape, d_o, cosine, sine, qkv, ot, lse, r1, order, sent, ready):
    micro, rows = xs[0].shape[:2]
    width = wshape[0]
    total = cosine.shape[0]
    wide = wshape[1] // 3
    heads = wide // HEAD_DIM
    smem = pl.BlockSpec(memory_space=pltpu.SMEM)
    whole = lambda a: pl.BlockSpec(a.shape, lambda i: (0,) * a.ndim)
    vspec = pl.BlockSpec((d_o.shape[0], 1, rows, wide), lambda i: (0, i, 0, 0))
    zshapes = [pltpu.HBM((len(sent), micro, rows, 4 * wide), BF16)] * CORES
    pairs = total * total // 2 * micro * wide
    return pl.pallas_call(
        functools.partial(attn_bwd_kernel, order, sent),
        grid=(micro,),
        in_specs=[
            smem, smem, vspec, whole(cosine), whole(sine),
            pl.BlockSpec((1, total, 3 * wide), lambda i: (i, 0, 0)),
            pl.BlockSpec((1, wide, total), lambda i: (i, 0, 0)),
            pl.BlockSpec((1, heads, total), lambda i: (i, 0, 0)),
            pl.BlockSpec((1, total, 128), lambda i: (i, 0, 0)),
        ]
        + chunk_specs(xs, order, width)
        + [corner(a) for a in ready],
        out_specs=[
            pl.BlockSpec((len(sent), 1, rows, 4 * wide), lambda i: (0, i, 0, 0))
        ]
        * CORES
        + [pl.BlockSpec(wshape, lambda i: (0, 0))],
        out_shape=zshapes + [pltpu.HBM(wshape, BF16)],
        scratch_shapes=[
            pltpu.VMEM((total, width), BF16),
            pltpu.VMEM((total, wide), BF16),
            pltpu.VMEM((wide, total), F32),
            pltpu.VMEM((total, 4 * wide), BF16),
            pltpu.VMEM(wshape, F32),
        ],
        compiler_params=vmem(40, total / 1024),
        cost_estimate=lasting(20),
        name="attn_bwd",
    )(seat, lengths, *held_in_hbm(d_o, cosine, sine, qkv, ot, lse, r1, *xs), *ready)


def ff_kernel(
    own, parts, seat_ref, xa, xb, oa, ob, pair, down_mine, down_far, wout_mine, wout_theirs, *refs,
):
    cotangents, refs = (refs[:parts], refs[parts : 2 * parts]), refs[2 * parts :]
    za, zb_lo, zb_hi, fa, fb, hn_out, hid_out, dgate_out, dup_out = refs[:9]
    refs = refs[9:]
    if own:
        y_out, o_out, wout_out = refs[:3]
        refs = refs[3:]
    x_buf, g_buf, oa_buf, ob_buf, wout, wg, wu, wd, z_buf, f_buf, hn, hid, dgate, dup, y_buf, o_buf, sems = refs
    seat = seat_ref[0]
    core = seat % CORES
    micro, rows = xa.shape[:2]
    width = wout.shape[0]
    many = micro * rows
    depth, outer, group, held, slab2 = pair.shape
    slab = slab2 // 2
    spread = group // CORES
    tall = down_mine.shape[1]
    half = seat // group
    copies = Copies(sems)

    for low in range(CORES):
        there = pl.ds(pl.multiple_of((core ^ low) * rows, rows), rows)
        copies.start("o", oa.at[:, :, there, :], oa_buf.at[low])
        copies.start("o", ob.at[:, :, there, :], ob_buf.at[low])
    for rc, ref in enumerate((wout_mine, wout_theirs)):
        for rx in range(spread):
            for ry in range(outer):
                other = seat ^ (ry * group + rx * CORES + rc)
                for d in range(depth):
                    to = pl.ds(pl.multiple_of((other * depth + d) * held, held), held)
                    copies.start("wout", ref.at[rx, ry, d], wout.at[to, :])
    copies.start("x", xa.at[:, :, pl.ds(0, width)], x_buf.at[0])
    copies.start("x", xb.at[:, :, pl.ds(0, width)], x_buf.at[1])
    for part, dest in ((0, wg), (1, wu)):
        for y in range(outer):
            for q in range(group):
                for d in range(depth):
                    to = ((y * group + q) * depth + d) * held
                    copies.start(
                        "wg" if part == 0 else "wu",
                        pair.at[d, y, q, :, pl.ds(part * slab, slab)],
                        dest.at[pl.ds(to, held), :],
                    )
    for low, some in enumerate(cotangents):
        base = 0
        for ref in some:
            copies.start("g", ref, g_buf.at[low, pl.ds(base, ref.shape[0])])
            base += ref.shape[0]
    for ry, ref in enumerate((down_mine, down_far)):
        for d in range(depth):
            to = pl.ds(pl.multiple_of(((half ^ ry) * depth + d) * tall, tall), tall)
            copies.start("wd", ref.at[d], wd.at[to, :])

    copies.wait("o")
    for low in range(CORES):
        for j in range(oa_buf.shape[1]):
            a = oa_buf[low, j].reshape(many, oa_buf.shape[4])
            b = ob_buf[low, j].reshape(many, oa_buf.shape[4])
            wide = a.shape[1]
            here = slice(low * many, (low + 1) * many)
            o_buf[here, (2 * j) * wide : (2 * j + 1) * wide] = jnp.where(core == 0, a, b)
            o_buf[here, (2 * j + 1) * wide : (2 * j + 2) * wide] = jnp.where(core == 0, b, a)
    copies.wait("wout", "x")
    if own:
        copies.start("out", wout, wout_out)
        copies.start("out", o_buf, o_out)
    y = x_buf[...].reshape(2 * many, width).astype(F32) + dot_nn(o_buf[...], wout[...])
    r2 = lax.rsqrt(jnp.mean(y * y, axis=1, keepdims=True) + EPSILON)
    hn[...] = (y * r2).astype(BF16)
    if own:
        y_buf[...] = y[:many]
        copies.start("out", y_buf, y_out)
    copies.start("out", hn, hn_out)
    copies.wait("wg")
    gate = dot_nn(hn[...], wg[...])
    copies.wait("wu")
    up = dot_nn(hn[...], wu[...])
    sigma = jax.nn.sigmoid(gate)
    act = gate * sigma
    hid[...] = (act * up).astype(BF16)
    copies.start("out", hid, hid_out)
    copies.wait("g", "wd")
    dhid = dot_nt(g_buf[...].reshape(2 * many, width), wd[...])
    dgate[...] = (dhid * up * (sigma + act * (1.0 - sigma))).astype(BF16)
    dup[...] = (dhid * act).astype(BF16)
    copies.start("out", dgate, dgate_out)
    copies.start("out", dup, dup_out)
    z_buf[...] = (dot_nt(dgate[...], wg[...]) + dot_nt(dup[...], wu[...])).astype(BF16)
    copies.start("out", z_buf.at[pl.ds(0, many)], za)
    copies.start("out", z_buf.at[pl.ds(many, many // 2)], zb_lo)
    copies.start("out", z_buf.at[pl.ds(many + many // 2, many // 2)], zb_hi)
    f_buf[...] = dot_nn(hid[...], wd[...]).astype(BF16)
    copies.start("out", f_buf.at[pl.ds(0, many)], fa)
    copies.start("out", f_buf.at[pl.ds(many, many)], fb)
    copies.wait()


def feed_forward(seat, xa, xb, ga, gb, oa, ob, weights, own):
    pair, down_mine, down_far, wout_mine, wout_theirs = weights
    micro, rows = xa.shape[:2]
    width = ga[0].shape[2]
    many = micro * rows
    depth, outer, group, held, slab2 = pair.shape
    fan = slab2 // 2
    wide = oa.shape[3]
    outs = [(many, width), (many // 2, width), (many // 2, width), (many, width), (many, width)]
    outs = [pltpu.HBM(s, BF16) for s in outs + [(2 * many, width)] + [(2 * many, fan)] * 3]
    if own:
        outs += [
            pltpu.HBM((many, width), F32), pltpu.HBM((2 * many, width), BF16),
            pltpu.HBM((width, width), BF16),
        ]
    o_shape = (CORES, oa.shape[0], micro, rows, wide)
    scratch = [
        ((2, micro, rows, width), BF16), ((2, micro, rows, width), BF16), (o_shape, BF16),
        (o_shape, BF16), ((width, width), BF16), ((width, fan), BF16), ((width, fan), BF16),
        ((fan, width), BF16), ((2 * many, width), BF16), ((2 * many, width), BF16),
        ((2 * many, width), BF16), ((2 * many, fan), BF16), ((2 * many, fan), BF16),
        ((2 * many, fan), BF16), ((many, width), F32), ((2 * many, width), BF16),
    ]
    many_copies = 32 + 4 * outer * group * depth
    anywhere = pl.BlockSpec(memory_space=pl.ANY)
    return pl.pallas_call(
        functools.partial(ff_kernel, own, len(ga)),
        grid=(1,),
        in_specs=[pl.BlockSpec(memory_space=pltpu.SMEM)]
        + [anywhere] * (9 + 2 * len(ga)),
        out_specs=[anywhere] * len(outs),
        out_shape=outs,
        scratch_shapes=[pltpu.VMEM(s, t) for s, t in scratch]
        + [pltpu.SemaphoreType.DMA((many_copies,))],
        compiler_params=vmem(56),
        cost_estimate=lasting(16),
        name="ff_own" if own else "ff_near",
    )(seat, *held_in_hbm(xa, xb, oa, ob, *weights, *ga, *gb))


def ff_grads_kernel(sizes, group, spread, seat_ref, *refs):
    sets = []
    for size in sizes:
        sets.append(refs[:size])
        refs = refs[size:]
    o_ref, dyb_ref, dyb_theirs, fa, fb = refs[:5]
    refs = refs[5:]
    pair_out, down_mine, wout_own = refs[:3]
    parcels = refs[3 : 2 + 2 * spread]
    dwg, dwu, dwd, dwo = refs[2 + 2 * spread :]
    seat = seat_ref[0]
    outer = seat // group
    core = seat % CORES
    chip = seat // CORES
    depth, blocks, held, slab2 = pair_out.shape
    slab = slab2 // 2
    tall = down_mine.shape[1]
    many, width = dyb_ref.shape
    for n, (hn, hid, dgate, dup, *gs) in enumerate(sets):
        g = jnp.concatenate([r[...].reshape(-1, width) for r in gs], axis=0)
        new = dot_tn(hn[...], dgate[...]), dot_tn(hn[...], dup[...]), dot_tn(hid[...], g)
        for scratch, value in zip((dwg, dwu, dwd), new):
            if n == 0:
                scratch[...] = value
            else:
                scratch[...] += value
    for k in range(blocks):
        for d in range(depth):
            at = slice((k * depth + d) * held, (k * depth + d + 1) * held)
            pair_out[d, k, :, :slab] = dwg[at, :].astype(BF16)
            pair_out[d, k, :, slab:] = dwu[at, :].astype(BF16)
    far = parcels[spread - 1]
    for d in range(depth):
        pieces = []
        for k in range(OUTER):
            at = slice((k * depth + d) * tall, (k * depth + d + 1) * tall)
            pieces.append(dwd[at, :].astype(BF16))
        down_mine[d] = jnp.where(outer == 0, pieces[0], pieces[1])
        far[d * tall : (d + 1) * tall, :] = jnp.where(outer == 0, pieces[1], pieces[0])
    dyb = jnp.concatenate([dyb_ref[...], dyb_theirs[...]], axis=0)
    rows = depth * held
    for c in range(2 * spread):
        a = o_ref[:, (2 * c) * rows : (2 * c + 1) * rows]
        b = o_ref[:, (2 * c + 1) * rows : (2 * c + 2) * rows]
        dwo[c * rows : (c + 1) * rows, :] = dot_tn(jnp.where(core == 0, a, b), dyb)
    for j in range(2 * spread):
        at = pl.ds(pl.multiple_of((chip ^ j) * rows, rows), rows)
        value = dwo[at, :].astype(BF16)
        if j == 0:
            wout_own[...] = value
        else:
            out = parcels[j - 1]
            out[out.shape[0] - rows :, :] = value
    for j in range(spread - 1):
        parcels[j][:many, :] = (fa[j].astype(F32) + fb[j].astype(F32)).astype(BF16)


def ff_grads(seat, sets, o_both, dyb, dyb_theirs, fa, fb, pair_shape, tall, spread):
    def fixed(shape):
        return pl.BlockSpec(shape, lambda i: (0,) * len(shape), pipeline_mode=pl.Buffered(1))

    args = [a for arrays in sets for a in arrays]
    last = [o_both, dyb, dyb_theirs, fa, fb]
    args += last
    specs = [fixed(a.shape) for a in args]
    depth, _, held, slab2 = pair_shape
    many, width = dyb.shape
    fan = slab2 // 2
    rows = depth * held
    parcels = [(many + rows, width)] * (spread - 1) + [(depth * tall + rows, width)]
    parcels += [(rows, width)] * (spread - 1)
    outs = [pair_shape, (depth, tall, width), (rows, width)] + parcels
    return pl.pallas_call(
        functools.partial(ff_grads_kernel, [len(s) for s in sets], spread * CORES, spread),
        grid=(1,),
        in_specs=[pl.BlockSpec(memory_space=pltpu.SMEM)] + specs,
        out_specs=[fixed(s) for s in outs],
        out_shape=[pltpu.HBM(s, BF16) for s in outs],
        scratch_shapes=[
            pltpu.VMEM((width, fan), F32), pltpu.VMEM((width, fan), F32),
            pltpu.VMEM((fan, width), F32), pltpu.VMEM((2 * spread * rows, width), F32),
        ],
        compiler_params=vmem(56),
        cost_estimate=lasting(14),
        name="ff_grads",
    )(seat, *args)


def pieces_at(values, index):
    step = 1
    while step < len(values):
        flip = (index // step) % 2 == 1
        values = [jnp.where(flip, values[k ^ step], values[k]) for k in range(len(values))]
        step *= 2
    return values


def payloads(seat, tokens, first_values, spread, wide):
    micro, rows, width = tokens.shape
    lanes = CORES * wide

    def kernel(seat_ref, x_ref, *refs):
        firsts, outs = refs[: 2 * spread], refs[2 * spread :]
        for out in outs:
            out[0, :, :width] = x_ref[0]
        for j in range(spread):
            outs[1][0, :, width + j * lanes : width + (j + 1) * lanes] = firsts[spread + j][0]
            outs[j and 1 + j][0, :, width:] = firsts[j][0]

    def part(j):
        return pl.BlockSpec((1, rows, lanes), lambda i, s: (i, 0, (s[0] // CORES) ^ j))

    sizes = [width + lanes, width + spread * lanes] + [width + lanes] * (spread - 1)
    return pl.pallas_call(
        kernel,
        grid_spec=pltpu.PrefetchScalarGridSpec(
            num_scalar_prefetch=1,
            grid=(micro,),
            in_specs=[pl.BlockSpec((1, rows, width), lambda i, s: (i, 0, 0))]
            + [part(j) for j in range(2 * spread)],
            out_specs=[pl.BlockSpec((1, rows, n), lambda i, s: (i, 0, 0)) for n in sizes],
        ),
        out_shape=[pltpu.HBM((micro, rows, n), BF16) for n in sizes],
        cost_estimate=lasting(4),
        name="payloads",
    )(seat, *held_in_hbm(tokens, *([first_values] * (2 * spread))))


def middle_back(y, parts, pieces, grad, wout, wide):
    micro, rows, width = grad.shape
    seats = width // wide
    many = micro * rows

    def kernel(y_ref, g_ref, w_ref, *refs):
        zs = refs[: len(parts)]
        z = jnp.concatenate([r[...] for r in refs[len(parts) : len(parts) + len(pieces)]], axis=0)
        dy_out, dyb_out, do_out = refs[len(parts) + len(pieces) :]
        z = z.astype(F32)
        for ref in zs:
            z = z + ref[...].astype(F32)
        y = y_ref[...]
        r2 = lax.rsqrt(jnp.mean(y * y, axis=1, keepdims=True) + EPSILON)
        inner = jnp.mean(z * y, axis=1, keepdims=True)
        g = g_ref[...].reshape(many, width).astype(F32)
        dy = g + r2 * z - y * (r2 * r2 * r2 * inner)
        dy_out[...] = dy
        dyb = dy.astype(BF16)
        dyb_out[...] = dyb
        d_o = dot_nt(dyb, w_ref[...]).astype(BF16)
        for s in range(seats):
            do_out[s] = d_o[:, s * wide : (s + 1) * wide].reshape(micro, rows, wide)

    def fixed(shape):
        return pl.BlockSpec(shape, lambda i: (0,) * len(shape), pipeline_mode=pl.Buffered(1))

    given = held_in_hbm(y, grad, wout, parts[0]) + [*parts[1:], *pieces]
    return pl.pallas_call(
        kernel,
        grid=(1,),
        in_specs=[fixed(a.shape) for a in given],
        out_specs=[
            fixed((many, width)), fixed((many, width)), fixed((seats, micro, rows, wide)),
        ],
        out_shape=[
            pltpu.HBM((many, width), F32),
            pltpu.HBM((many, width), BF16),
            pltpu.HBM((seats, micro, rows, wide), BF16),
        ],
        compiler_params=vmem(24),
        cost_estimate=FREE,
        name="middle_back",
    )(*given)


def back_to_x(seat, mine, theirs, w_mine, w_theirs):
    count, micro, rows, lanes = mine.shape
    width = w_mine.shape[0]
    wide = lanes // 4
    many = micro * rows

    def kernel(seat_ref, a_ref, b_ref, wa, wb, *refs):
        outs = refs[:count]
        buf, sems = refs[-2:]
        core = seat_ref[0] % CORES
        copies = Copies(sems)
        for j in range(count):
            a = a_ref[j].reshape(many, lanes)
            b = b_ref[j].reshape(many, lanes)
            z = dot_nt(a[:, : 3 * wide], wa[...]) + dot_nt(b[:, : 3 * wide], wb[...])
            buf[j, :, :, :width] = z.astype(BF16).reshape(micro, rows, width)
            first = jnp.where(core == 0, a[:, 3 * wide :], b[:, 3 * wide :])
            second = jnp.where(core == 0, b[:, 3 * wide :], a[:, 3 * wide :])
            buf[j, :, :, width : width + wide] = first.reshape(micro, rows, wide)
            buf[j, :, :, width + wide :] = second.reshape(micro, rows, wide)
            copies.start("out", buf.at[j], outs[j])
        copies.wait()

    anywhere = pl.BlockSpec(memory_space=pl.ANY)
    out = pltpu.HBM((micro, rows, width + CORES * wide), BF16)
    fixed = lambda shape: pl.BlockSpec(
        shape, lambda i: (0,) * len(shape), pipeline_mode=pl.Buffered(1)
    )
    given = held_in_hbm(mine) + [theirs, w_mine, w_theirs]
    return pl.pallas_call(
        kernel,
        grid=(1,),
        in_specs=[pl.BlockSpec(memory_space=pltpu.SMEM)] + [fixed(a.shape) for a in given],
        out_specs=[anywhere] * count,
        out_shape=[out] * count,
        scratch_shapes=[
            pltpu.VMEM((count, micro, rows, width + CORES * wide), BF16),
            pltpu.SemaphoreType.DMA((count,)),
        ],
        compiler_params=vmem(32),
        cost_estimate=lasting(5),
        name="back_to_x",
    )(seat, *given)


def plane_sums(level, down, wout, parcels):
    depth, tall, width = down.shape
    held = wout.shape[0] // depth
    spread = (len(parcels) + 1) // 2

    def kernel(level_ref, down_ref, wout_ref, *refs):
        parts, outs = refs[: len(parcels)], refs[len(parcels) :]
        far = parts[spread - 1]
        for k, out in enumerate(outs):
            d = level_ref[0] ^ k
            at = pl.ds(pl.multiple_of(d * tall, tall), tall)
            out[:tall, :] = (down_ref[d].astype(F32) + far[at, :].astype(F32)).astype(BF16)
            at = pl.ds(pl.multiple_of(d * held, held), held)
            total = wout_ref[at, :].astype(F32)
            for part in parts:
                base = part.shape[0] - depth * held
                at = pl.ds(pl.multiple_of(base + d * held, held), held)
                total = total + part[at, :].astype(F32)
            out[tall:, :] = total.astype(BF16)

    fixed = lambda shape: pl.BlockSpec(
        shape, lambda i: (0,) * len(shape), pipeline_mode=pl.Buffered(1)
    )
    given = [down, wout, *parcels]
    shape = (tall + held, width)
    return pl.pallas_call(
        kernel,
        grid=(1,),
        in_specs=[pl.BlockSpec(memory_space=pltpu.SMEM)] + [fixed(a.shape) for a in given],
        out_specs=[fixed(shape)] * depth,
        out_shape=[pltpu.HBM(shape, BF16)] * depth,
        compiler_params=vmem(24),
        cost_estimate=FREE,
        name="plane_sums",
    )(level, *given)


def add_parts(mine, theirs):
    def kernel(a_ref, *refs):
        b = jnp.concatenate([r[...] for r in refs[:-1]], axis=0)
        refs[-1][...] = (a_ref[...].astype(F32) + b.astype(F32)).astype(BF16)

    fixed = lambda shape: pl.BlockSpec(
        shape, lambda i: (0,) * len(shape), pipeline_mode=pl.Buffered(1)
    )
    return pl.pallas_call(
        kernel,
        grid=(1,),
        in_specs=[fixed(a.shape) for a in (mine, *theirs)],
        out_specs=fixed(mine.shape),
        out_shape=pltpu.HBM(mine.shape, BF16),
        compiler_params=vmem(16),
        cost_estimate=FREE,
        name="add_parts",
    )(mine, *theirs)


def tail_grads(parts, tall, short):
    rows, width = parts[0].shape

    def kernel(*refs):
        *ins, down_out, wout_out = refs
        total = ins[0][...].astype(F32)
        for ref in ins[1:]:
            total = total + ref[...].astype(F32)
        down_out[...] = total[:short, :]
        wout_out[...] = total[tall:, :]

    return pl.pallas_call(
        kernel,
        out_shape=[pltpu.HBM((short, width), F32), pltpu.HBM((rows - tall, width), F32)],
        cost_estimate=FREE,
        name="tail_grads",
    )(*parts)


def onward(arrived, far_own, width, lanes, split):
    count = len(arrived)
    micro, rows, _ = far_own.shape

    def kernel(*refs):
        blocks, far, outs = refs[:count], refs[count], refs[count + 1 :]
        for j in range(count):
            outs[j][0] = blocks[j][0, :, :split]
            outs[count + j][0, :, : width - split] = far[0, :, split:width]
            at = width + (j + 1) * lanes
            outs[count + j][0, :, width - split :] = far[0, :, at : at + lanes]

    spec = lambda n: pl.BlockSpec((1, rows, n), lambda i: (i, 0, 0))
    sizes = [split] * count + [width + lanes - split] * count
    out = pl.pallas_call(
        kernel,
        grid=(micro,),
        in_specs=[spec(a.shape[2]) for a in (*arrived, far_own)],
        out_specs=[spec(n) for n in sizes],
        out_shape=[pltpu.HBM((micro, rows, n), BF16) for n in sizes],
        cost_estimate=FREE,
        name="onward",
    )(*arrived, far_own)
    return out[:count], out[count:]


def fence(value, ready):
    def kernel(*_):
        pass

    return pl.pallas_call(
        kernel,
        grid=(1,),
        in_specs=[pl.BlockSpec(memory_space=pl.ANY)] + [corner(a) for a in ready],
        out_specs=pl.BlockSpec(memory_space=pl.ANY),
        out_shape=pltpu.HBM(value.shape, value.dtype),
        input_output_aliases={0: 0},
        cost_estimate=FREE,
        name="fence",
    )(value, *ready)


def token_grads(seat, tokens, dy, got, wide, ready):
    micro, rows, width = tokens.shape
    lanes = CORES * wide

    def kernel(seat_ref, x_ref, dy_ref, *refs):
        parts = refs[: len(got)]
        dx_out, dv_out = refs[-2:]
        z = parts[0][0, :, :width].astype(F32)
        for ref in parts[1:]:
            z = z + ref[0, :, :width].astype(F32)
        x = x_ref[0].astype(F32)
        inv = lax.rsqrt(jnp.mean(x * x, axis=1, keepdims=True) + EPSILON)
        inner = jnp.mean(z * x, axis=1, keepdims=True)
        dx_out[0] = dy_ref[...] + z - x * (inv * inv * inner)
        firsts = pieces_at([ref[0, :, width:].astype(F32) for ref in parts], seat_ref[0] // CORES)
        for k, value in enumerate(firsts):
            dv_out[0, :, k * lanes : (k + 1) * lanes] = value

    spec = pl.BlockSpec((1, rows, width), lambda i: (i, 0, 0))
    return pl.pallas_call(
        kernel,
        grid=(micro,),
        in_specs=[
            pl.BlockSpec(memory_space=pltpu.SMEM), spec, pl.BlockSpec((rows, width), lambda i: (i, 0)),
        ]
        + [pl.BlockSpec((1, rows, width + lanes), lambda i: (i, 0, 0))] * len(got)
        + [corner(a) for a in ready],
        out_specs=[spec, spec],
        out_shape=[pltpu.HBM(tokens.shape, F32)] * 2,
        cost_estimate=FREE,
        name="token_grads",
    )(seat, tokens, dy, *got, *ready)


def projection_grads(parts, weight, gain, wide):
    seats, depth, held, _ = parts.shape
    width = seats * wide

    def kernel(p_ref, w_ref, gain_ref, dw_out, dg_out):
        gain = gain_ref[...]
        grown = jnp.zeros((held, 1), F32)
        for s in range(seats):
            total = p_ref[s, 0].astype(F32)
            for d in range(1, depth):
                total = total + p_ref[s, d].astype(F32)
            for t in range(3):
                at = slice(t * width + s * wide, t * width + (s + 1) * wide)
                piece = total[:, t * wide : (t + 1) * wide]
                dw_out[:, at] = piece * gain
                grown = grown + jnp.sum(piece * w_ref[:, at].astype(F32), axis=1, keepdims=True)
        dg_out[...] = grown

    return pl.pallas_call(
        kernel,
        out_shape=[
            pltpu.HBM(weight.shape, F32), pltpu.HBM((held, 1), F32),
        ],
        cost_estimate=FREE,
        name="projection_grads",
    )(parts, weight, gain)


def pair_grads(parts, gate, up, gain, depth, short):
    outer, group, held, slab2 = parts.shape
    slab = slab2 // 2
    tall = slab // (OUTER * depth)
    fan = gate.shape[1]

    def kernel(p_ref, gate_ref, up_ref, gain_ref, dgate_out, dup_out, dg_out):
        for q in range(group):
            total = p_ref[0, q].astype(F32)
            for y in range(1, outer):
                total = total + p_ref[y, q].astype(F32)
            for m, out in enumerate((dgate_out, dup_out)):
                for y in range(OUTER):
                    for d in range(depth):
                        at = m * slab + (y * depth + d) * tall
                        to = ((y * group + q) * depth + d) * short
                        out[:, to : to + short] = total[:, at : at + short]
        dgate = dgate_out[...]
        dup = dup_out[...]
        dg_out[...] = jnp.sum(
            dgate * gate_ref[...].astype(F32) + dup * up_ref[...].astype(F32),
            axis=1,
            keepdims=True,
        )
        dgate_out[...] = dgate * gain_ref[...]
        dup_out[...] = dup * gain_ref[...]

    return pl.pallas_call(
        kernel,
        out_shape=[
            pltpu.HBM((held, fan), F32), pltpu.HBM((held, fan), F32), pltpu.HBM((held, 1), F32),
        ],
        cost_estimate=FREE,
        name="pair_grads",
    )(parts, gate, up, gain)


def rope_tables(total, wide):
    positions = np.arange(total, dtype=np.float32)
    inverse = np.float32(10000.0) ** (-np.arange(0, HEAD_DIM, 2, dtype=np.float32) / HEAD_DIM)
    angles = (positions[:, None] * inverse[None, :].astype(np.float32)).astype(np.float64)
    cosine, sine = np.cos(angles), np.sin(angles)
    cosine = np.tile(cosine, (1, 2 * wide // HEAD_DIM))
    sine = np.tile(np.concatenate([-sine, sine], -1), (1, wide // HEAD_DIM))
    return jnp.asarray(cosine.astype(np.float32)), jnp.asarray(sine.astype(np.float32))


def local(
    tokens, first_values, out_grad, lengths, norm1_gain, qkv_weight, out_weight, norm2_gain,
    gate_weight, up_weight, down_weight,
):
    micro, rows, width = tokens.shape
    seats, depth = lax.axis_size("seq"), lax.axis_size("dp")
    devices = seats * depth
    seat = lax.axis_index("seq")
    group = seats // OUTER
    spread = group // CORES
    outer = seat // group
    total = seats * rows
    wide = width // seats
    held = qkv_weight.shape[0]
    fan_rows = down_weight.shape[0]
    fan = fan_rows * devices
    tall = -(-fan_rows // 16) * 16
    slab = OUTER * depth * tall
    many = micro * rows
    seat_arr = jnp.reshape(seat, (1,)).astype(jnp.int32)
    level_arr = jnp.reshape(lax.axis_index("dp"), (1,)).astype(jnp.int32)

    def swap(value, mask):
        return lax.ppermute(value, "seq", [(i, i ^ mask) for i in range(seats)])

    def token(value):
        return value[(0,) * value.ndim].astype(F32) * 0.0

    def swap_depth(value, mask):
        return lax.ppermute(value, "dp", [(i, i ^ mask) for i in range(depth)])

    same_core = [[i for i in range(seats) if i % CORES == c] for c in range(CORES)]
    every = ("seq", "dp")
    core = seat % CORES
    chip = seat // CORES
    inner = [2 * j for j in range(spread)]
    across = [group + 2 * j for j in range(spread)]

    gain1 = norm1_gain.astype(F32)[:, None]
    gain2 = norm2_gain.astype(F32)[:, None]

    lanes = width + CORES * wide

    def together(part, *operands):
        shapes = jax.eval_shape(part, *operands)
        return lax.cond(
            lengths[0] > 0,
            part,
            lambda *_: jax.tree.map(lambda s: jnp.zeros(s.shape, s.dtype), shapes),
            *operands,
        )

    def to_seats(value, groups=None):
        return lax.all_to_all(
            value, "seq", split_axis=0, concat_axis=0, tiled=True, axis_index_groups=groups
        )

    def to_all(value):
        return lax.all_to_all(value, every, split_axis=0, concat_axis=0, tiled=True)

    tail = jnp.concatenate(
        [jnp.pad(down_weight, ((0, tall - fan_rows), (0, 0))), out_weight], 0
    )
    tail = lax.all_gather(tail, "dp", axis=0)

    def columns(weight):
        scaled = (weight.astype(F32) * gain2).astype(BF16)
        scaled = scaled.reshape(held, OUTER, group, depth, fan_rows).transpose(2, 0, 1, 3, 4)
        scaled = jnp.pad(scaled, ((0, 0),) * 4 + ((0, tall - fan_rows),))
        return scaled.reshape(group, held, slab)

    def weights_first():
        pair = jnp.concatenate([columns(gate_weight), columns(up_weight)], -1)
        pair = jnp.concatenate([pair] * OUTER, 0)
        wqkv = (qkv_weight.astype(F32) * gain1).astype(BF16)
        wqkv = wqkv.reshape(held, 3, seats, wide).transpose(2, 0, 1, 3).reshape(seats, held, 3 * wide)
        both = to_seats(jnp.concatenate([pair, wqkv], -1))
        return (
            both[..., : 2 * slab], both[..., 2 * slab :],
            payloads(seat_arr, tokens, first_values, spread, wide),
        )

    pair, wqkv, (own, far_own, *arrived) = together(weights_first)
    pair = lax.all_gather(pair, "dp", axis=0).reshape(depth, OUTER, group, held, 2 * slab)

    def first_leg(arrived, far_own, own, wqkv):
        return (
            [swap(v, m) for v, m in zip(arrived, inner[1:])], swap(far_own, group),
            lax.all_gather(wqkv, "dp", axis=1).reshape(width, 3 * wide),
            swap(own, 1), swap(out_grad, 1),
        )

    arrived, far_own, wqkv, own_b, grad_b = together(first_leg, arrived, far_own, own, wqkv)
    split = 128 * (lanes // 256)

    def second_leg(lower, upper, arrived, far_own, tail):
        lower = [swap(v, group) for v in lower]
        upper = [swap(v, m) for v, m in zip(upper, inner[1:])]
        wout = tail[:, tall:]
        wout = jnp.stack([wout, swap(wout, group)])
        grads = [swap(out_grad[:1], m) for m in inner[1:]]
        return lower, upper, [swap(v, 1) for v in arrived], swap(far_own, 1), wout, grads

    lower, upper = onward(arrived, far_own, width, CORES * wide, split)
    lower, upper, arrived_b, far_own_b, wout, grads_lo = together(
        second_leg, lower, upper, arrived, far_own, tail
    )
    mine = [own, *arrived, far_own, *lower, *upper]
    theirs = [own_b, *arrived_b, far_own_b, *[swap(v, 1) for v in lower + upper]]
    places = [(m, 0) for m in inner + across] + [(m, split) for m in across[1:]]
    order = tuple(places) + tuple((m + 1, lane) for m, lane in places)
    xs = mine + theirs
    near = [(own, own_b)] + list(zip(arrived, arrived_b))
    cosine, sine = rope_tables(total, wide)

    def attend(xs, wqkv, tail, wout):
        down = tail[:, :tall]
        return (
            attn_fwd(seat_arr, lengths, xs, wqkv, cosine, sine, order, []),
            down,
            swap(down, group),
            jnp.stack([wout] + [swap(wout, m) for m in inner[1:]]),
            [swap(out_grad[1:], m) for m in inner[1:]],
        )

    (qkv, ot, *sends, lse, r1), down_mine, down_far, wout, grads_hi = together(
        attend, xs, wqkv, tail, wout
    )

    def spread_out(send, wout, wqkv, *grads):
        return to_seats(send, same_core), swap(wout, 1), swap(wqkv, 1), [[swap(v, 1) for v in g] for g in grads]

    turns = list(range(1, spread)) + [0]
    o, wout_theirs, wqkv_theirs, grads_b = together(
        spread_out, sends[turns[0]], wout, wqkv, grads_lo, grads_hi
    )
    cotangents = [((out_grad,), (grad_b,))]
    cotangents += list(zip(zip(grads_lo, grads_hi), zip(*grads_b)))
    weights = (pair, down_mine, down_far, wout, wout_theirs)
    near_z, sets, near_f, z_parts = [], [], [], []
    for turn, at in enumerate(turns):

        def rows_of(o, near_z, send, weights):
            z = [swap(v, m) for v, m in near_z]
            after = [to_seats(v, same_core) for v in send]
            return (
                feed_forward(seat_arr, *near[at], *cotangents[at], *o, weights, at == 0), z, after
            )

        masks_z = [inner[j] for j in turns[turn - 1 : turn]] if turn else []
        out, z, after = together(
            lambda o, near_z, send, weights: rows_of(
                o, list(zip(near_z, masks_z)), send, weights
            ),
            (o, swap(o, 1)), near_z[-1:], [sends[j] for j in turns[turn + 1 : turn + 2]], weights,
        )
        z_parts += z
        o = after[0] if after else None
        za, zb_lo, zb_hi, fa, fb, *kept = out
        sets.append((*kept[:4], *cotangents[at][0], *cotangents[at][1]))
        if at:
            near_z.append(add_parts(za, [swap(zb_lo, 1), swap(zb_hi, 1)]))
            near_f.append((fa, fb))
    y, o_both, wout = kept[4:]
    dy, dyb, d_o = middle_back(
        y, [za] + z_parts, [swap(zb_lo, 1), swap(zb_hi, 1)], out_grad, wout, wide
    )

    near_fa = jnp.stack([v[0] for v in near_f])
    near_fb = jnp.stack([v[1] for v in near_f])

    def weight_grads(d_o, dyb, kept, near_fa, near_fb):
        return to_seats(d_o), ff_grads(
            seat_arr, kept, o_both, dyb, swap(dyb, 1), near_fa, swap(near_fb, 1),
            (depth, OUTER * group, held, 2 * slab), tall, spread,
        )

    d_o, (pair, down_mine, wout_own, *parcels) = together(
        weight_grads, d_o, dyb, sets, near_fa, near_fb
    )
    pair = lax.psum_scatter(
        pair.reshape(-1, 2 * slab), "dp", scatter_dimension=0, tiled=True
    ).reshape(OUTER * group, held, 2 * slab)

    def attend_back(parcels, d_o, xs):
        out = attn_bwd(
            seat_arr, lengths, xs, wqkv.shape, d_o, cosine, sine, qkv, ot, lse, r1, order,
            across + inner, [],
        )
        return out, [swap(v, m) for v, m in zip(parcels, inner[1:] + across[:1])]

    (e_mine, e_theirs, dwq), landed = together(attend_back, parcels[:spread], d_o, xs)

    def to_x(e_theirs, parcels, fb):
        both = back_to_x(seat_arr, e_mine, swap(e_theirs, 1), wqkv, wqkv_theirs)
        return both, [swap(v, m) for v, m in zip(parcels, across[1:])], swap(fb, 1)

    both, more, fb = together(to_x, e_theirs, parcels[spread:], fb)
    landed = landed + more
    far, close = both[:spread], both[spread:]

    def first_return(close, far, dwq, down_mine, wout_own, landed):
        got = [swap(close[j], inner[j]) for j in range(1, spread)] + [swap(far[0], across[0])]
        dwq = to_all(dwq.reshape(devices, held, 3 * wide))
        tail = plane_sums(level_arr, down_mine, wout_own, landed)
        output = y + fa.astype(F32) + fb.astype(F32)
        output = output + sum(v[:many].astype(F32) for v in landed[: spread - 1])
        return got, dwq, tail, output.astype(BF16).reshape(tokens.shape)

    got, dwq, tail, output = together(first_return, close, far, dwq, down_mine, wout_own, landed)

    def second_return(far, pair, dwq, tail):
        tail = [tail[0]] + [swap_depth(tail[k], k) for k in range(1, depth)]
        pair = to_seats(pair)
        return (
            [swap(far[j], across[j]) for j in range(1, spread)],
            pair_grads(
                pair.reshape(OUTER, group, held, 2 * slab), gate_weight, up_weight, gain2, depth,
                fan_rows,
            ),
            projection_grads(dwq.reshape(seats, depth, held, 3 * wide), qkv_weight, gain1, wide),
            tail_grads(tail, tall, fan_rows),
        )

    rest, (gate_grad, up_grad, gain2_grad), (qkv_grad, gain1_grad), (down_grad, out_grad_w) = together(
        second_return, far, pair, dwq, tail
    )
    got = [close[0]] + got + rest
    d_tokens, d_first = token_grads(seat_arr, tokens, dy, got, wide, [])
    gain1_grad, gain2_grad = gain1_grad[:, 0], gain2_grad[:, 0]
    return (
        output, d_tokens, d_first, gain1_grad, qkv_grad, out_grad_w, gain2_grad, gate_grad, up_grad,
        down_grad,
    )


def solution(mesh):
    rows = P(("seq", "dp"), None)
    acts = P("dp", "seq", None)
    gains = P(("seq", "dp"))
    return jax.shard_map(
        local,
        mesh=mesh,
        in_specs=(acts, acts, acts, P("dp"), gains, rows, rows, gains, rows, rows, rows),
        out_specs=(acts, acts, acts, gains, rows, rows, gains, rows, rows, rows),
        check_vma=False,
    )
```

profile of v0, /device:TPU:0, one launch (start us, length us, event | category | flops | bytes accessed | tf_op | source)
XLA Modules:
  0.0 348.1 jit_solution(8108253338387837300)
XLA Ops:
  10.3 25.4 %conditional.12 = (bf16[8,32,1536]{2,1,0:T(8,128)(2,1)S(1)}, bf16[8,32,384]{2,1,0:T(8,128)(2,1)}, bf16[3,128,1280]{2,1,0:T(8,128)(2,1)S(1)}, bf16[3,128,1536]{2,1,0:T(8,128)(2,1)}, bf16[3,128,1280]{2,1,0:T(8,128)(2,1)}) conditional(s32[]{:T(128)} %bitcast.18, () %tuple.117, (bf16[32,2816]{1,0:T(8,128)(2,1)}, f32[32,1]{0,1:T(1,128)S(1)}, ...), branch_computations={%region_0.1_spmd, %region_1.2_spmd} | conditional | flops 5750784 | bytes 31898080 | solution.py:971
  15.1 5.2 %all-to-all-start.4 = ((bf16[8,32,1920]{2,1,0:T(8,128)(2,1)}), bf16[8,32,1920]{2,1,0:T(8,128)(2,1)S(1)}, u32[]{:S(2)}, u32[]{:S(2)}) async-start(bf16[8,32,1920]{2,1,0:T(8,128)(2,1)} %pad_maximum_fusion), calls=%async_computation.4 | async-start | bytes 1966080 | tf_op jit(solution)/shard_map/cond/branch_1_fun/all_to_all | solution.py:979
  20.2 3.7 %payloads.1 = (bf16[3,128,1280]{2,1,0:T(8,128)(2,1)}, bf16[3,128,1536]{2,1,0:T(8,128)(2,1)}, bf16[3,128,1280]{2,1,0:T(8,128)(2,1)}) custom-call(s32[1]{0:T(128)} %get-tuple-element.295.seat_ref, bf16[3,128,1024]{2,1,0:T(8,128)(2,1)} %get-tuple-element.296.x_ref, bf16[3,128,1024]{2,1,0:T(8,128)(2,1)} %get-tuple-element.687.refs_0_.refs_1_.refs_2_.refs_3_, ...), custom_call_target="tpu_custom_call" | custom-call | bytes 14760000 | tf_op jit(solution)/shard_map/cond/branch_1_fun/payloads/pallas_call | solution.py:593
  24.0 11.0 %all-to-all-done.4 = bf16[8,32,1920]{2,1,0:T(8,128)(2,1)S(1)} async-done(((bf16[8,32,1920]{2,1,0:T(8,128)(2,1)}), bf16[8,32,1920]{2,1,0:T(8,128)(2,1)S(1)}, u32[]{:S(2)}, u32[]{:S(2)}) %all-to-all-start.4) | async-done | bytes 983072 | tf_op jit(solution)/shard_map/cond/branch_1_fun/all_to_all | solution.py:979
  36.7 25.9 %conditional.13 = (bf16[3,128,1280]{2,1,0:T(8,128)(2,1)}, bf16[3,128,1536]{2,1,0:T(8,128)(2,1)}, bf16[1024,384]{1,0:T(8,128)(2,1)}, bf16[3,128,1280]{2,1,0:T(8,128)(2,1)}, bf16[3,128,1024]{2,1,0:T(8,128)(2,1)}) conditional(s32[]{:T(128)} %bitcast.18, () %tuple.119, (bf16[3,128,1280]{2,1,0:T(8,128)(2,1)}, bf16[3,128,1536]{2,1,0:T(8,128)(2,1)}, ...), branch_computations={%region_2.3_spmd, %region_3.4_spmd} | conditional | bytes 16711880 | solution.py:971
  38.5 24.1 %all-gather = bf16[8,128,384]{2,1,0:T(8,128)(2,1)} all-gather(bf16[8,32,384]{2,1,0:T(8,128)(2,1)} %get-tuple-element.303), channel_id=2, replica_groups=mesh['seq'=8,'dp'=4] {'dp'}, dimensions={1}, use_global_device_ids=true | all-gather | bytes 983040 | tf_op jit(solution)/shard_map/cond/branch_1_fun/all_gather | solution.py:1014
  62.6 3.3 onward.1
  65.9 23.6 %conditional.14 = (bf16[3,128,640]{2,1,0:T(8,128)(2,1)}, bf16[3,128,640]{2,1,0:T(8,128)(2,1)}, bf16[3,128,1280]{2,1,0:T(8,128)(2,1)}, bf16[3,128,1536]{2,1,0:T(8...) conditional(s32[]{:T(128)} %bitcast.18, () %tuple.122, ...), branch_computations={%region_4.5_spmd, %region_5.6_spmd} | conditional | flops 262144 | bytes 17039648 | solution.py:971
  69.5 3.1 collective-permute-start.21
  72.6 4.1 %collective-permute-done.24 = bf16[4,32,1024]{2,1,0:T(8,128)(2,1)S(1)} collective-permute-done((bf16[4,32,1024]{2,1,0:T(8,128)(2,1)S(1)}, bf16[4,32,1024]{2,1,0:T(8,128)(2,1)S(1)}, u32[]{:S(2)}, u32[]{:S(2)}) %collective-permute-start.24) | collective-permute-done | bytes 262176 | tf_op jit(solution)/shard_map/cond/branch_1_fun/ppermute | solution.py:949
  76.7 3.1 collective-permute-start.25
  79.8 9.6 %collective-permute-done.25 = bf16[1,128,1024]{2,1,0:T(8,128)(2,1)} collective-permute-done((bf16[1,128,1024]{2,1,0:T(8,128)(2,1)S(1)}, bf16[1,128,1024]{2,1,0:T(8,128)(2,1)}, u32[]{:S(2)}, u32[]{:S(2)}) %collective-permute-start.25) | collective-permute-done | bytes 262176 | tf_op jit(solution)/shard_map/cond/branch_1_fun/ppermute | solution.py:949
  93.1 28.0 %conditional.15 = (bf16[3,1024,384]{2,1,0:T(8,128)(2,1)}, f32[3,128,1024]{2,1,0:T(8,128)}, bf16[4,3,256,128]{3,2,1,0:T(8,128)(2,1)}, bf16[4,3,256,128]{3,2,1,0:T...) conditional(s32[]{:T(128)} %bitcast.18, () %tuple.125, ...), branch_computations={%region_6.7_spmd, %region_7.8_spmd} | conditional | flops 524288 | bytes 89791040 | solution.py:971
  93.3 2.4 slice.18
  98.3 21.5 %attn_fwd.1 = (bf16[3,1024,384]{2,1,0:T(8,128)(2,1)}, f32[3,128,1024]{2,1,0:T(8,128)}, bf16[4,3,256,128]{3,2,1,0:T(8,128)(2,1)}, bf16[4,3,256,128]{3,2,1,0:T(8,1...) custom-call(s32[1]{0:T(128)} %get-tuple-element.312.seat_ref, s32[3]{0:T(128)S(1)} %get-tuple-element.313.len_ref, ...), custom_call_target="tpu_custom_call" | custom-call | bytes 73800000 | tf_op jit(solution)/shard_map/cond/branch_1_fun/attn_fwd/pallas_call | solution.py:188
  121.1 16.1 %conditional.16 = (bf16[4,3,256,128]{3,2,1,0:T(8,128)(2,1)}, bf16[2,2,4,32,1024]{4,3,2,1,0:T(8,128)(2,1)}, bf16[1024,384]{1,0:T(8,128)(2,1)}, bf16[1,128,1024]{2,1,0:T(8,128)(2,1)}, bf16[2,128,1024]{2,1,0:T(8,128)(2,1)}) conditional(s32[]{:T(128)} %bitcast.18, () %tuple.124, (bf16[4,3,256,128]{3,2,1,0:T(8,128)(2,1)}, ...), branch_computations={%region_8.9_spmd, %region_9.10_spmd} | conditional | bytes 12845288 | solution.py:971
  121.7 4.2 %all-to-all-start = ((bf16[4,3,256,128]{3,2,1,0:T(8,128)(2,1)}), bf16[4,3,256,128]{3,2,1,0:T(8,128)(2,1)}, u32[]{:S(2)}, u32[]{:S(2)}) async-start(bf16[4,3,256,128]{3,2,1,0:T(8,128)(2,1)} %get-tuple-element.336), calls=%async_computation | async-start | bytes 1572864 | tf_op jit(solution)/shard_map/cond/branch_1_fun/all_to_all | solution.py:979
  126.4 2.1 collective-permute-done.6
  128.5 8.7 %all-to-all-done = bf16[4,3,256,128]{3,2,1,0:T(8,128)(2,1)} async-done(((bf16[4,3,256,128]{3,2,1,0:T(8,128)(2,1)}), bf16[4,3,256,128]{3,2,1,0:T(8,128)(2,1)}, u32[]{:S(2)}, u32[]{:S(2)}) %all-to-all-start) | async-done | bytes 786464 | tf_op jit(solution)/shard_map/cond/branch_1_fun/all_to_all | solution.py:979
  137.3 2.6 collective-permute-done.33
  139.9 22.5 %conditional.17 = (bf16[384,1024]{1,0:T(8,128)(2,1)}, bf16[192,1024]{1,0:T(8,128)(2,1)}, bf16[192,1024]{1,0:T(8,128)(2,1)}, bf16[768,1024]{1,0:T(8,128)(2,1)}, b...) conditional(s32[]{:T(128)} %bitcast.18, () %tuple.121, ...), branch_computations={%region_10.11_spmd, %region_11.12_spmd} | conditional | bytes 61399408 | solution.py:971
  139.9 4.2 %all-to-all-start.1 = ((bf16[4,3,256,128]{3,2,1,0:T(8,128)(2,1)}), bf16[4,3,256,128]{3,2,1,0:T(8,128)(2,1)}, u32[]{:S(2)}, u32[]{:S(2)}) async-start(bf16[4,3,256,128]{3,2,1,0:T(8,128)(2,1)} %get-tuple-element.362), calls=%async_computation.1 | async-start | bytes 1572864 | tf_op jit(solution)/shard_map/cond/branch_1_fun/all_to_all | solution.py:979
  144.1 17.9 %ff_near.1 = (bf16[384,1024]{1,0:T(8,128)(2,1)}, bf16[192,1024]{1,0:T(8,128)(2,1)}, bf16[192,1024]{1,0:T(8,128)(2,1)}, bf16[384,1024]{1,0:T(8,128)(2,1)}, bf16[3...) custom-call(s32[1]{0:T(128)} %get-tuple-element.341.seat_ref, ...), custom_call_target="tpu_custom_call" | custom-call | bytes 59040000 | tf_op jit(solution)/shard_map/cond/branch_1_fun/ff_near/pallas_call | solution.py:465
  163.1 2.4 collective-permute-done.35.refs_0_
  166.1 2.2 add_parts.1
  168.3 20.3 %conditional.18 = (bf16[384,1024]{1,0:T(8,128)(2,1)}, bf16[192,1024]{1,0:T(8,128)(2,1)}, bf16[192,1024]{1,0:T(8,128)(2,1)}, bf16[384,1024]{1,0:T(8,128)(2,1)}, b...) conditional(s32[]{:T(128)} %bitcast.18, () %tuple.116, ...), branch_computations={%region_12.13_spmd, %region_13.14_spmd} | conditional | bytes 72671712 | solution.py:971
  170.3 16.7 %ff_own.1 = (bf16[384,1024]{1,0:T(8,128)(2,1)}, bf16[192,1024]{1,0:T(8,128)(2,1)}, bf16[192,1024]{1,0:T(8,128)(2,1)}, bf16[384,1024]{1,0:T(8,128)(2,1)}, bf16[38...) custom-call(s32[1]{0:T(128)} %get-tuple-element.365.seat_ref, ...), custom_call_target="tpu_custom_call" | custom-call | bytes 59040000 | tf_op jit(solution)/shard_map/cond/branch_1_fun/ff_own/pallas_call | solution.py:465
  191.2 5.4 %middle_back.1 = (f32[384,1024]{1,0:T(8,128)}, bf16[384,1024]{1,0:T(8,128)(2,1)}, bf16[8,3,128,128]{3,2,1,0:T(8,128)(2,1)}) custom-call(f32[384,1024]{1,0:T(8,128)} %get-tuple-element.623.y_ref, bf16[3,128,1024]{2,1,0:T(8,128)(2,1)} %g_ref.1, bf16[1024,1024]{1,0:T(8,128)(2,1)} %get-tuple-element.624.w_ref, bf16[384,1024]{1,0:T(8,128)(2,1)} %get-tuple-element.625.refs_0_, ...), custom_call_target="tpu_custom_call" | custom-call | tf_op jit(solution)/shard_map/middle_back/pallas_call | solution.py:636
  196.6 21.6 %conditional.19 = (bf16[8,3,128,128]{3,2,1,0:T(8,128)(2,1)}, bf16[4,8,32,1536]{3,2,1,0:T(8,128)(2,1)}, bf16[4,96,1024]{2,1,0:T(8,128)(2,1)}, bf16[128,1024]{1,0:...) conditional(s32[]{:T(128)} %bitcast.18, () %tuple.115, ...), branch_computations={%region_14.15_spmd, %region_15.16_spmd} | conditional | bytes 66602432 | solution.py:971
  197.1 4.2 %all-to-all-start.2 = ((bf16[8,3,128,128]{3,2,1,0:T(8,128)(2,1)}), bf16[8,3,128,128]{3,2,1,0:T(8,128)(2,1)}, u32[]{:S(2)}, u32[]{:S(2)}) async-start(bf16[8,3,128,128]{3,2,1,0:T(8,128)(2,1)} %get-tuple-element.390), calls=%async_computation.2 | async-start | bytes 1572864 | tf_op jit(solution)/shard_map/cond/branch_1_fun/all_to_all | solution.py:979
  202.2 16.0 %ff_grads.1 = (bf16[4,8,32,1536]{3,2,1,0:T(8,128)(2,1)}, bf16[4,96,1024]{2,1,0:T(8,128)(2,1)}, bf16[128,1024]{1,0:T(8,128)(2,1)}, bf16[512,1024]{1,0:T(8,128)(2,...) custom-call(s32[1]{0:T(128)} %get-tuple-element.391.seat_ref, bf16[768,1024]{1,0:T(8,128)(2,1)} %get-tuple-element.392.refs_0_, ...), custom_call_target="tpu_custom_call" | custom-call | bytes 51660000 | tf_op jit(solution)/shard_map/cond/branch_1_fun/ff_grads/pallas_call | solution.py:552
  218.2 27.5 %conditional.20 = (bf16[4,3,128,512]{3,2,1,0:T(8,128)(2,1)}, bf16[4,3,128,512]{3,2,1,0:T(8,128)(2,1)}, bf16[1024,384]{1,0:T(8,128)(2,1)}, bf16[512,1024]{1,0:T(8,128)(2,1)}, bf16[512,1024]{1,0:T(8,128)(2,1)}) conditional(s32[]{:T(128)} %bitcast.18, () %tuple.114, (s32[1]{0:T(128)}, s32[3]{0:T(128)S(1)}, bf16[8,3,128,128]{3,2,1,0:T(8,128)(2,1)}, ...), branch_computations={%region_16.17_spmd, %region_17.18_spmd} | conditional | bytes 86120920 | solution.py:971
  221.9 20.6 %attn_bwd.1 = (bf16[4,3,128,512]{3,2,1,0:T(8,128)(2,1)}, bf16[4,3,128,512]{3,2,1,0:T(8,128)(2,1)}, bf16[1024,384]{1,0:T(8,128)(2,1)}) custom-call(s32[1]{0:T(128)} %get-tuple-element.416.seat_ref, s32[3]{0:T(128)S(1)} %get-tuple-element.417.len_ref, bf16[8,3,128,128]{3,2,1,0:T(8,128)(2,1)} %get-tuple-element.418.do_ref, ...), custom_call_target="tpu_custom_call" | custom-call | bytes 73800000 | tf_op jit(solution)/shard_map/cond/branch_1_fun/attn_bwd/pallas_call | solution.py:310
  245.7 11.1 %conditional.21 = (bf16[3,128,1280]{2,1,0:T(8,128)(2,1)}, bf16[3,128,1280]{2,1,0:T(8,128)(2,1)}, bf16[3,128,1280]{2,1,0:T(8,128)(2,1)}, bf16[3,128,1280]{2,1,0:T...) conditional(s32[]{:T(128)} %bitcast.18, () %tuple.113, ...), branch_computations={%region_18.19_spmd, %region_19.20_spmd} | conditional | bytes 28935928 | solution.py:971
  247.7 2.8 collective-permute-done.13.b_ref
  250.4 6.4 %back_to_x.1 = (bf16[3,128,1280]{2,1,0:T(8,128)(2,1)}, bf16[3,128,1280]{2,1,0:T(8,128)(2,1)}, bf16[3,128,1280]{2,1,0:T(8,128)(2,1)}, bf16[3,128,1280]{2,1,0:T(8,128)(2,1)}) custom-call(s32[1]{0:T(128)} %get-tuple-element.440.seat_ref, bf16[4,3,128,512]{3,2,1,0:T(8,128)(2,1)} %get-tuple-element.441.a_ref, ...), custom_call_target="tpu_custom_call" | custom-call | bytes 18450000 | tf_op jit(solution)/shard_map/cond/branch_1_fun/back_to_x/pallas_call | solution.py:683
  256.9 39.0 %conditional.22 = (bf16[3,128,1280]{2,1,0:T(8,128)(2,1)}, bf16[3,128,1280]{2,1,0:T(8,128)(2,1)}, bf16[32,32,384]{2,1,0:T(8,128)(2,1)}, bf16[128,1024]{1,0:T(8,12...) conditional(s32[]{:T(128)} %bitcast.18, () %tuple.112, ...), branch_computations={%region_20.21_spmd, %region_21.22_spmd} | conditional | flops 2752512 | bytes 17039592 | solution.py:971
  256.9 5.0 %all-to-all-start.5 = ((bf16[32,32,384]{2,1,0:T(8,128)(2,1)}), bf16[32,32,384]{2,1,0:T(8,128)(2,1)}, u32[]{:S(2)}, u32[]{:S(2)}) async-start(bf16[32,32,384]{2,1,0:T(8,128)(2,1)} %bitcast.12), calls=%async_computation.5 | async-start | bytes 1572864 | tf_op jit(solution)/shard_map/cond/branch_1_fun/all_to_all | solution.py:984
  265.1 3.0 plane_sums.1
  268.1 2.6 add_convert_fusion
  270.8 22.9 %collective-permute-done.29 = bf16[3,128,1280]{2,1,0:T(8,128)(2,1)} collective-permute-done((bf16[3,128,1280]{2,1,0:T(8,128)(2,1)}, bf16[3,128,1280]{2,1,0:T(8,128)(2,1)}, u32[]{:S(2)}, u32[]{:S(2)}) %collective-permute-start.29) | collective-permute-done | bytes 983072 | tf_op jit(solution)/shard_map/cond/branch_1_fun/ppermute | solution.py:949
  296.8 39.2 %conditional.23 = (bf16[3,128,1280]{2,1,0:T(8,128)(2,1)}, f32[32,2816]{1,0:T(8,128)}, f32[32,2816]{1,0:T(8,128)}, f32[32,3072]{1,0:T(8,128)}, f32[88,1024]{1,0:T...) conditional(s32[]{:T(128)} %bitcast.18, () %tuple.134, (bf16[3,128,1280]{2,1,0:T(8,128)(2,1)}, ...), branch_computations={%region_23.24_spmd, %region_24.25_spmd} | conditional | bytes 15730040 | solution.py:971
  296.8 2.4 collective-permute-start.16
  299.2 3.5 %all-to-all-start.3 = ((bf16[8,32,1536]{2,1,0:T(8,128)(2,1)}), bf16[8,32,1536]{2,1,0:T(8,128)(2,1)S(1)}, u32[]{:S(2)}, u32[]{:S(2)}) async-start(bf16[8,32,1536]{2,1,0:T(8,128)(2,1)} %bitcast.51), calls=%async_computation.3 | async-start | bytes 1572864 | tf_op jit(solution)/shard_map/cond/branch_1_fun/all_to_all | solution.py:979
  311.4 2.5 collective-permute-done.19.refs_3_
  313.8 15.0 %collective-permute-done.18.refs_2_ = bf16[128,1024]{1,0:T(8,128)(2,1)S(1)} collective-permute-done((bf16[128,1024]{1,0:T(8,128)(2,1)}, bf16[128,1024]{1,0:T(8,128)(2,1)S(1)}, u32[]{:S(2)}, u32[]{:S(2)}) %collective-permute-start.18) | collective-permute-done | bytes 262176 | tf_op jit(solution)/shard_map/cond/branch_1_fun/ppermute | solution.py:955
  332.5 2.6 pair_grads.1
  336.0 5.3 %token_grads.1 = (f32[3,128,1024]{2,1,0:T(8,128)}, f32[3,128,1024]{2,1,0:T(8,128)}) custom-call(s32[1]{0:T(128)} %bitcast.19.seat_ref, bf16[3,128,1024]{2,1,0:T(8,128)(2,1)S(1)} %copy-done.6, f32[384,1024]{1,0:T(8,128)} %get-tuple-element.665.dy_ref, bf16[3,128,1280]{2,1,0:T(8,128)(2,1)} %get-tuple-element.666.refs_0_, ...), custom_call_target="tpu_custom_call" | custom-call | tf_op jit(solution)/shard_map/token_grads/pallas_call | solution.py:836
  (168 shorter events, 59.6 us)
Async XLA Ops:
  7.2 58.7 %all-gather.6.cloned.1.call-start = ((), (), s32[]{:S(2)}) async-start(), calls=%async_computation.8 | async-start | bytes 1310720 | tf_op jit(solution)/shard_map/all_gather | solution.py:989
  8.9 131.0 %all-gather.8.cloned.1.call-start = ((), (), s32[]{:S(2)}) async-start(), calls=%async_computation.9 | async-start | bytes 3932160 | tf_op jit(solution)/shard_map/all_gather | solution.py:1009
  15.1 19.9 %all-to-all-start.4 = ((bf16[8,32,1920]{2,1,0:T(8,128)(2,1)}), bf16[8,32,1920]{2,1,0:T(8,128)(2,1)S(1)}, u32[]{:S(2)}, u32[]{:S(2)}) async-start(bf16[8,32,1920]{2,1,0:T(8,128)(2,1)} %pad_maximum_fusion), calls=%async_computation.4 | async-start | bytes 1966080 | tf_op jit(solution)/shard_map/cond/branch_1_fun/all_to_all | solution.py:979
  36.6 259.3 %reduce-scatter.2.cloned.1.call-start = ((), (), s32[]{:S(2)}) async-start(), calls=%async_computation.7 | async-start | bytes 3932160 | tf_op jit(solution)/shard_map/reduce_scatter | solution.py:1106
  36.7 25.9 %collective-permute-start.1 = (bf16[3,128,1536]{2,1,0:T(8,128)(2,1)}, bf16[3,128,1536]{2,1,0:T(8,128)(2,1)}, u32[]{:S(2)}, u32[]{:S(2)}) collective-permute-start(bf16[3,128,1536]{2,1,0:T(8,128)(2,1)} %get-tuple-element.302), channel_id=1, source_target_pairs={{0,16},{4,20},{8,24},{12,28},{16,0},{20,4},{24,8},{28,12},{1,17},{... | collective-permute-start | bytes 3538952 | tf_op jit(solution)/shard_map/cond/branch_1_fun/ppermute | solution.py:949
  37.3 25.2 %collective-permute-start = (bf16[3,128,1280]{2,1,0:T(8,128)(2,1)}, bf16[3,128,1280]{2,1,0:T(8,128)(2,1)}, u32[]{:S(2)}, u32[]{:S(2)}) collective-permute-start(bf16[3,128,1280]{2,1,0:T(8,128)(2,1)} %get-tuple-element.301), channel_id=1, source_target_pairs={{0,8},{4,12},{8,0},{12,4},{16,24},{20,28},{24,16},{28,20},{1,9},{5... | collective-permute-start | bytes 2949128 | tf_op jit(solution)/shard_map/cond/branch_1_fun/ppermute | solution.py:949
  37.9 24.6 %collective-permute-start.2 = (bf16[3,128,1280]{2,1,0:T(8,128)(2,1)S(1)}, bf16[3,128,1280]{2,1,0:T(8,128)(2,1)}, u32[]{:S(2)}, u32[]{:S(2)}) collective-permute-start(bf16[3,128,1280]{2,1,0:T(8,128)(2,1)S(1)} %get-tuple-element.304), channel_id=1, source_target_pairs={{0,4},{4,0},{8,12},{12,8},{16,20},{20,16},{24,28},{28,24},{1,5},{5... | collective-permute-start | bytes 2949128 | tf_op jit(solution)/shard_map/cond/branch_1_fun/ppermute | solution.py:949
  38.0 24.6 %collective-permute-start.3 = (bf16[3,128,1024]{2,1,0:T(8,128)(2,1)S(1)}, bf16[3,128,1024]{2,1,0:T(8,128)(2,1)}, u32[]{:S(2)}, u32[]{:S(2)}) collective-permute-start(bf16[3,128,1024]{2,1,0:T(8,128)(2,1)S(1)} %get-tuple-element.305), channel_id=1, source_target_pairs={{0,4},{4,0},{8,12},{12,8},{16,20},{20,16},{24,28},{28,24},{1,5},{5... | collective-permute-start | bytes 2359304 | tf_op jit(solution)/shard_map/cond/branch_1_fun/ppermute | solution.py:949
  65.9 23.6 %collective-permute-start.23 = (bf16[3,128,1536]{2,1,0:T(8,128)(2,1)}, bf16[3,128,1536]{2,1,0:T(8,128)(2,1)}, u32[]{:S(2)}, u32[]{:S(2)}) collective-permute-start(bf16[3,128,1536]{2,1,0:T(8,128)(2,1)} %get-tuple-element.309), channel_id=1, source_target_pairs={{0,4},{4,0},{8,12},{12,8},{16,20},{20,16},{24,28},{28,24},{1,5},{5... | collective-permute-start | bytes 3538952 | tf_op jit(solution)/shard_map/cond/branch_1_fun/ppermute | solution.py:949
  66.0 23.5 %collective-permute-start.22 = (bf16[3,128,1280]{2,1,0:T(8,128)(2,1)}, bf16[3,128,1280]{2,1,0:T(8,128)(2,1)}, u32[]{:S(2)}, u32[]{:S(2)}) collective-permute-start(bf16[3,128,1280]{2,1,0:T(8,128)(2,1)} %get-tuple-element.308), channel_id=1, source_target_pairs={{0,4},{4,0},{8,12},{12,8},{16,20},{20,16},{24,28},{28,24},{1,5},{5... | collective-permute-start | bytes 2949128 | tf_op jit(solution)/shard_map/cond/branch_1_fun/ppermute | solution.py:949
  67.4 9.2 %collective-permute-start.24 = (bf16[4,32,1024]{2,1,0:T(8,128)(2,1)S(1)}, bf16[4,32,1024]{2,1,0:T(8,128)(2,1)S(1)}, u32[]{:S(2)}, u32[]{:S(2)}) collective-permute-start(bf16[4,32,1024]{2,1,0:T(8,128)(2,1)S(1)} %get-tuple-element.727), channel_id=1, source_target_pairs={{0,16},{4,20},{8,24},{12,28},{16,0},{20,4},{24,8},{28,12},{1,17},{... | collective-permute-start | bytes 786440 | tf_op jit(solution)/shard_map/cond/branch_1_fun/ppermute | solution.py:949
  68.7 20.8 %collective-permute-start.20 = (bf16[3,128,640]{2,1,0:T(8,128)(2,1)}, bf16[3,128,640]{2,1,0:T(8,128)(2,1)}, u32[]{:S(2)}, u32[]{:S(2)}) collective-permute-start(bf16[3,128,640]{2,1,0:T(8,128)(2,1)} %get-tuple-element.306), channel_id=1, source_target_pairs={{0,16},{4,20},{8,24},{12,28},{16,0},{20,4},{24,8},{28,12},{1,17},{... | collective-permute-start | bytes 1474568 | tf_op jit(solution)/shard_map/cond/branch_1_fun/ppermute | solution.py:949
  69.5 19.9 %collective-permute-start.21 = (bf16[3,128,640]{2,1,0:T(8,128)(2,1)}, bf16[3,128,640]{2,1,0:T(8,128)(2,1)}, u32[]{:S(2)}, u32[]{:S(2)}) collective-permute-start(bf16[3,128,640]{2,1,0:T(8,128)(2,1)} %get-tuple-element.307), channel_id=1, source_target_pairs={{0,8},{4,12},{8,0},{12,4},{16,24},{20,28},{24,16},{28,20},{1,9},{5... | collective-permute-start | bytes 1474568 | tf_op jit(solution)/shard_map/cond/branch_1_fun/ppermute | solution.py:949
  76.7 12.8 %collective-permute-start.25 = (bf16[1,128,1024]{2,1,0:T(8,128)(2,1)S(1)}, bf16[1,128,1024]{2,1,0:T(8,128)(2,1)}, u32[]{:S(2)}, u32[]{:S(2)}) collective-permute-start(bf16[1,128,1024]{2,1,0:T(8,128)(2,1)S(1)} %slice.17), channel_id=1, source_target_pairs={{0,8},{4,12},{8,0},{12,4},{16,24},{20,28},{24,16},{28,20},{1,9},{5... | collective-permute-start | bytes 786440 | tf_op jit(solution)/shard_map/cond/branch_1_fun/ppermute | solution.py:949
  89.5 2.1 collective-permute-start.31
  89.5 2.8 collective-permute-start.32
  95.7 25.4 %collective-permute-start.26 = (bf16[4,96,1024]{2,1,0:T(8,128)(2,1)}, bf16[4,96,1024]{2,1,0:T(8,128)(2,1)}, u32[]{:S(2)}, u32[]{:S(2)}) collective-permute-start(bf16[4,96,1024]{2,1,0:T(8,128)(2,1)} %slice.18), channel_id=1, source_target_pairs={{0,16},{4,20},{8,24},{12,28},{16,0},{20,4},{24,8},{28,12},{1,17},{... | collective-permute-start | bytes 2359304 | tf_op jit(solution)/shard_map/cond/branch_1_fun/ppermute | solution.py:949
  96.1 23.6 %collective-permute-start.27 = (bf16[2,4,32,1024]{3,2,1,0:T(8,128)(2,1)S(1)}, bf16[2,4,32,1024]{3,2,1,0:T(8,128)(2,1)S(1)}, u32[]{:S(2)}, u32[]{:S(2)}) collective-permute-start(bf16[2,4,32,1024]{3,2,1,0:T(8,128)(2,1)S(1)} %get-tuple-element.334), channel_id=1, source_target_pairs={{0,8},{4,12},{8,0},{12,4},{16,24},{20,28},{24,16},{28,20},{1,9},{5... | collective-permute-start | bytes 1572872 | tf_op jit(solution)/shard_map/cond/branch_1_fun/ppermute | solution.py:949
  97.9 23.2 %collective-permute-start.28 = (bf16[2,128,1024]{2,1,0:T(8,128)(2,1)S(1)}, bf16[2,128,1024]{2,1,0:T(8,128)(2,1)}, u32[]{:S(2)}, u32[]{:S(2)}) collective-permute-start(bf16[2,128,1024]{2,1,0:T(8,128)(2,1)S(1)} %slice.19), channel_id=1, source_target_pairs={{0,8},{4,12},{8,0},{12,4},{16,24},{20,28},{24,16},{28,20},{1,9},{5... | collective-permute-start | bytes 1572872 | tf_op jit(solution)/shard_map/cond/branch_1_fun/ppermute | solution.py:949
  121.1 16.1 %collective-permute-start.4 = (bf16[2,2,4,32,1024]{4,3,2,1,0:T(8,128)(2,1)S(1)}, bf16[2,2,4,32,1024]{4,3,2,1,0:T(8,128)(2,1)}, u32[]{:S(2)}, u32[]{:S(2)}) collective-permute-start(bf16[2,2,4,32,1024]{4,3,2,1,0:T(8,128)(2,1)S(1)} %get-tuple-element.337), channel_id=1, source_target_pairs={{0,4},{4,0},{8,12},{12,8},{16,20},{20,16},{24,28},{28,24},{1,5},{5... | collective-permute-start | bytes 3145736 | tf_op jit(solution)/shard_map/cond/branch_1_fun/ppermute | solution.py:949
  121.1 16.1 %collective-permute-start.5 = (bf16[1024,384]{1,0:T(8,128)(2,1)}, bf16[1024,384]{1,0:T(8,128)(2,1)}, u32[]{:S(2)}, u32[]{:S(2)}) collective-permute-start(bf16[1024,384]{1,0:T(8,128)(2,1)} %get-tuple-element.338), channel_id=1, source_target_pairs={{0,4},{4,0},{8,12},{12,8},{16,20},{20,16},{24,28},{28,24},{1,5},{5... | collective-permute-start | bytes 2359304 | tf_op jit(solution)/shard_map/cond/branch_1_fun/ppermute | solution.py:949
  121.7 15.6 %all-to-all-start = ((bf16[4,3,256,128]{3,2,1,0:T(8,128)(2,1)}), bf16[4,3,256,128]{3,2,1,0:T(8,128)(2,1)}, u32[]{:S(2)}, u32[]{:S(2)}) async-start(bf16[4,3,256,128]{3,2,1,0:T(8,128)(2,1)} %get-tuple-element.336), calls=%async_computation | async-start | bytes 1572864 | tf_op jit(solution)/shard_map/cond/branch_1_fun/all_to_all | solution.py:979
  125.9 2.7 collective-permute-start.7
  126.0 2.6 collective-permute-start.6
  137.3 2.6 collective-permute-start.33
  139.9 22.1 %all-to-all-start.1 = ((bf16[4,3,256,128]{3,2,1,0:T(8,128)(2,1)}), bf16[4,3,256,128]{3,2,1,0:T(8,128)(2,1)}, u32[]{:S(2)}, u32[]{:S(2)}) async-start(bf16[4,3,256,128]{3,2,1,0:T(8,128)(2,1)} %get-tuple-element.362), calls=%async_computation.1 | async-start | bytes 1572864 | tf_op jit(solution)/shard_map/cond/branch_1_fun/all_to_all | solution.py:979
  162.4 5.9 %collective-permute-start.34 = (bf16[4,3,256,128]{3,2,1,0:T(8,128)(2,1)}, bf16[4,3,256,128]{3,2,1,0:T(8,128)(2,1)S(1)}, u32[]{:S(2)}, u32[]{:S(2)}) collective-permute-start(bf16[4,3,256,128]{3,2,1,0:T(8,128)(2,1)} %get-tuple-element.618), channel_id=1, source_target_pairs={{0,4},{4,0},{8,12},{12,8},{16,20},{20,16},{24,28},{28,24},{1,5},{5... | collective-permute-start | bytes 2359304 | tf_op jit(solution)/shard_map/ppermute | solution.py:949
  162.6 2.9 collective-permute-start.35
  163.0 3.1 collective-permute-start.36
  168.3 20.1 %collective-permute-start.8 = (bf16[384,1024]{1,0:T(8,128)(2,1)}, bf16[384,1024]{1,0:T(8,128)(2,1)}, u32[]{:S(2)}, u32[]{:S(2)}) collective-permute-start(bf16[384,1024]{1,0:T(8,128)(2,1)} %get-tuple-element.389), channel_id=1, source_target_pairs={{0,8},{4,12},{8,0},{12,4},{16,24},{20,28},{24,16},{28,20},{1,9},{5... | collective-permute-start | bytes 2359304 | tf_op jit(solution)/shard_map/cond/branch_1_fun/ppermute | solution.py:949
  188.6 2.0 collective-permute-start.37
  188.7 2.5 collective-permute-start.38
  196.6 4.7 %collective-permute-start.10 = (bf16[1,384,1024]{2,1,0:T(8,128)(2,1)}, bf16[1,384,1024]{2,1,0:T(8,128)(2,1)S(1)}, u32[]{:S(2)}, u32[]{:S(2)}) collective-permute-start(bf16[1,384,1024]{2,1,0:T(8,128)(2,1)} %get-tuple-element.409), channel_id=1, source_target_pairs={{0,4},{4,0},{8,12},{12,8},{16,20},{20,16},{24,28},{28,24},{1,5},{5... | collective-permute-start | bytes 2359304 | tf_op jit(solution)/shard_map/cond/branch_1_fun/ppermute | solution.py:949
  196.7 4.6 %collective-permute-start.9 = (bf16[384,1024]{1,0:T(8,128)(2,1)}, bf16[384,1024]{1,0:T(8,128)(2,1)}, u32[]{:S(2)}, u32[]{:S(2)}) collective-permute-start(bf16[384,1024]{1,0:T(8,128)(2,1)} %get-tuple-element.407.refs_15_), channel_id=1, source_target_pairs={{0,4},{4,0},{8,12},{12,8},{16,20},{20,16},{24,28},{28,24},{1,5},{5... | collective-permute-start | bytes 2359304 | tf_op jit(solution)/shard_map/cond/branch_1_fun/ppermute | solution.py:949
  197.1 21.1 %all-to-all-start.2 = ((bf16[8,3,128,128]{3,2,1,0:T(8,128)(2,1)}), bf16[8,3,128,128]{3,2,1,0:T(8,128)(2,1)}, u32[]{:S(2)}, u32[]{:S(2)}) async-start(bf16[8,3,128,128]{3,2,1,0:T(8,128)(2,1)} %get-tuple-element.390), calls=%async_computation.2 | async-start | bytes 1572864 | tf_op jit(solution)/shard_map/cond/branch_1_fun/all_to_all | solution.py:979
  218.5 25.8 %collective-permute-start.11 = (bf16[512,1024]{1,0:T(8,128)(2,1)}, bf16[512,1024]{1,0:T(8,128)(2,1)}, u32[]{:S(2)}, u32[]{:S(2)}) collective-permute-start(bf16[512,1024]{1,0:T(8,128)(2,1)} %get-tuple-element.438), channel_id=1, source_target_pairs={{0,8},{4,12},{8,0},{12,4},{16,24},{20,28},{24,16},{28,20},{1,9},{5... | collective-permute-start | bytes 3145736 | tf_op jit(solution)/shard_map/cond/branch_1_fun/ppermute | solution.py:949
  220.4 25.2 %collective-permute-start.12 = (bf16[512,1024]{1,0:T(8,128)(2,1)}, bf16[512,1024]{1,0:T(8,128)(2,1)}, u32[]{:S(2)}, u32[]{:S(2)}) collective-permute-start(bf16[512,1024]{1,0:T(8,128)(2,1)} %get-tuple-element.439), channel_id=1, source_target_pairs={{0,16},{4,20},{8,24},{12,28},{16,0},{20,4},{24,8},{28,12},{1,17},{... | collective-permute-start | bytes 3145736 | tf_op jit(solution)/shard_map/cond/branch_1_fun/ppermute | solution.py:949
  245.7 4.7 %collective-permute-start.13 = (bf16[4,3,128,512]{3,2,1,0:T(8,128)(2,1)}, bf16[4,3,128,512]{3,2,1,0:T(8,128)(2,1)S(1)}, u32[]{:S(2)}, u32[]{:S(2)}) collective-permute-start(bf16[4,3,128,512]{3,2,1,0:T(8,128)(2,1)} %get-tuple-element.442), channel_id=1, source_target_pairs={{0,4},{4,0},{8,12},{12,8},{16,20},{20,16},{24,28},{28,24},{1,5},{5... | collective-permute-start | bytes 4718600 | tf_op jit(solution)/shard_map/cond/branch_1_fun/ppermute | solution.py:949
  245.7 11.1 %collective-permute-start.15 = (bf16[384,1024]{1,0:T(8,128)(2,1)}, bf16[384,1024]{1,0:T(8,128)(2,1)}, u32[]{:S(2)}, u32[]{:S(2)}) collective-permute-start(bf16[384,1024]{1,0:T(8,128)(2,1)} %get-tuple-element.450), channel_id=1, source_target_pairs={{0,4},{4,0},{8,12},{12,8},{16,20},{20,16},{24,28},{28,24},{1,5},{5... | collective-permute-start | bytes 2359304 | tf_op jit(solution)/shard_map/cond/branch_1_fun/ppermute | solution.py:949
  246.2 10.6 %collective-permute-start.14 = (bf16[128,1024]{1,0:T(8,128)(2,1)}, bf16[128,1024]{1,0:T(8,128)(2,1)}, u32[]{:S(2)}, u32[]{:S(2)}) collective-permute-start(bf16[128,1024]{1,0:T(8,128)(2,1)} %get-tuple-element.449), channel_id=1, source_target_pairs={{0,24},{4,28},{8,16},{12,20},{16,8},{20,12},{24,0},{28,4},{1,25},{... | collective-permute-start | bytes 786440 | tf_op jit(solution)/shard_map/cond/branch_1_fun/ppermute | solution.py:949
  256.9 39.0 %all-to-all-start.5 = ((bf16[32,32,384]{2,1,0:T(8,128)(2,1)}), bf16[32,32,384]{2,1,0:T(8,128)(2,1)}, u32[]{:S(2)}, u32[]{:S(2)}) async-start(bf16[32,32,384]{2,1,0:T(8,128)(2,1)} %bitcast.12), calls=%async_computation.5 | async-start | bytes 1572864 | tf_op jit(solution)/shard_map/cond/branch_1_fun/all_to_all | solution.py:984
  261.9 31.8 %collective-permute-start.29 = (bf16[3,128,1280]{2,1,0:T(8,128)(2,1)}, bf16[3,128,1280]{2,1,0:T(8,128)(2,1)}, u32[]{:S(2)}, u32[]{:S(2)}) collective-permute-start(bf16[3,128,1280]{2,1,0:T(8,128)(2,1)} %get-tuple-element.451), channel_id=1, source_target_pairs={{0,8},{4,12},{8,0},{12,4},{16,24},{20,28},{24,16},{28,20},{1,9},{5... | collective-permute-start | bytes 2949128 | tf_op jit(solution)/shard_map/cond/branch_1_fun/ppermute | solution.py:949
  263.7 30.6 %collective-permute-start.30 = (bf16[3,128,1280]{2,1,0:T(8,128)(2,1)}, bf16[3,128,1280]{2,1,0:T(8,128)(2,1)}, u32[]{:S(2)}, u32[]{:S(2)}) collective-permute-start(bf16[3,128,1280]{2,1,0:T(8,128)(2,1)} %get-tuple-element.452), channel_id=1, source_target_pairs={{0,16},{4,20},{8,24},{12,28},{16,0},{20,4},{24,8},{28,12},{1,17},{... | collective-permute-start | bytes 2949128 | tf_op jit(solution)/shard_map/cond/branch_1_fun/ppermute | solution.py:949
  296.8 39.2 %collective-permute-start.16 = (bf16[3,128,1280]{2,1,0:T(8,128)(2,1)}, bf16[3,128,1280]{2,1,0:T(8,128)(2,1)}, u32[]{:S(2)}, u32[]{:S(2)}) collective-permute-start(bf16[3,128,1280]{2,1,0:T(8,128)(2,1)} %get-tuple-element.467), channel_id=1, source_target_pairs={{0,24},{4,28},{8,16},{12,20},{16,8},{20,12},{24,0},{28,4},{1,25},{... | collective-permute-start | bytes 2949128 | tf_op jit(solution)/shard_map/cond/branch_1_fun/ppermute | solution.py:949
  299.2 32.5 %all-to-all-start.3 = ((bf16[8,32,1536]{2,1,0:T(8,128)(2,1)}), bf16[8,32,1536]{2,1,0:T(8,128)(2,1)S(1)}, u32[]{:S(2)}, u32[]{:S(2)}) async-start(bf16[8,32,1536]{2,1,0:T(8,128)(2,1)} %bitcast.51), calls=%async_computation.3 | async-start | bytes 1572864 | tf_op jit(solution)/shard_map/cond/branch_1_fun/all_to_all | solution.py:979
  302.7 11.1 %collective-permute-start.19 = (bf16[128,1024]{1,0:T(8,128)(2,1)S(1)}, bf16[128,1024]{1,0:T(8,128)(2,1)S(1)}, u32[]{:S(2)}, u32[]{:S(2)}) collective-permute-start(bf16[128,1024]{1,0:T(8,128)(2,1)S(1)} %get-tuple-element.481), channel_id=1, source_target_pairs={{0,3},{1,2},{2,1},{3,0},{4,7},{5,6},{6,5},{7,4},{8,11},{9,10},{10,... | collective-permute-start | bytes 786440 | tf_op jit(solution)/shard_map/cond/branch_1_fun/ppermute | solution.py:955
  304.2 24.7 %collective-permute-start.18 = (bf16[128,1024]{1,0:T(8,128)(2,1)}, bf16[128,1024]{1,0:T(8,128)(2,1)S(1)}, u32[]{:S(2)}, u32[]{:S(2)}) collective-permute-start(bf16[128,1024]{1,0:T(8,128)(2,1)} %get-tuple-element.480), channel_id=1, source_target_pairs={{0,2},{1,3},{2,0},{3,1},{4,6},{5,7},{6,4},{7,5},{8,10},{9,11},{10,... | collective-permute-start | bytes 786440 | tf_op jit(solution)/shard_map/cond/branch_1_fun/ppermute | solution.py:955
  305.4 23.5 %collective-permute-start.17 = (bf16[128,1024]{1,0:T(8,128)(2,1)}, bf16[128,1024]{1,0:T(8,128)(2,1)S(1)}, u32[]{:S(2)}, u32[]{:S(2)}) collective-permute-start(bf16[128,1024]{1,0:T(8,128)(2,1)} %get-tuple-element.479), channel_id=1, source_target_pairs={{0,1},{1,0},{2,3},{3,2},{4,5},{5,4},{6,7},{7,6},{8,9},{9,8},{10,11... | collective-permute-start | bytes 786440 | tf_op jit(solution)/shard_map/cond/branch_1_fun/ppermute | solution.py:955
  (30 other events, 343.2 us)
Sparse Core Ops, SparseCore 0:
  10.2 30.6 all-gather.5
  42.4 66.3 all-gather.7
  218.3 73.8 reduce-scatter.1
where the time goes:
time: 354 us; the launch traced here: 348 us
  Pallas kernels  128 us (36%)
  waiting for transfers between devices  96.7 us (27%)
  starting transfers between devices  60.3 us (17%)
  blocking collectives  24.1 us (7%)
  between operations  14.9 us (4%)
  local copies, waits for them, and re-layouts  13.1 us (4%)
  other arithmetic  9.07 us (3%)
    ppermute x36, waiting for transfers between devices, swap(): return lax.ppermute(value, 'seq', [(i, i ^ mask) for i in range(seats)])  57.9 us
    pallas_call x2, Pallas kernels, feed_forward(): pl.pallas_call(functools.partial(ff_kernel, own, len(ga)), grid=(1,), in_...  34.5 us
    ppermute x36, starting transfers between devices, swap(): return lax.ppermute(value, 'seq', [(i, i ^ mask) for i in range(seats)])  29.4 us
    all_gather x1, blocking collectives, first_leg(): lax.all_gather(wqkv, 'dp', axis=1).reshape(width, 3 * wide)  24.1 us
    pallas_call x1, Pallas kernels, attn_fwd(): pl.pallas_call(functools.partial(attn_fwd_kernel, order), grid=(micro,),...  21.5 us
    all_to_all x5, starting transfers between devices, to_seats(): lax.all_to_all(value, 'seq', split_axis=0, concat_axis=0, tiled=True, axi...  21.3 us
    pallas_call x1, Pallas kernels, attn_bwd(): pl.pallas_call(functools.partial(attn_bwd_kernel, order, sent), grid=(mic...  20.6 us
    all_to_all x5, waiting for transfers between devices, to_seats(): lax.all_to_all(value, 'seq', split_axis=0, concat_axis=0, tiled=True, axi...  19.7 us
  transfers between devices with their start and end apart: 48, of which 22 were waited for; matrix products, arithmetic and copies ran while one was open for 4% of the time, Pallas kernels for 34%

commit v1 on v0

--- a/solution.py
+++ b/solution.py
@@ -750,7 +750,7 @@
         compiler_params=vmem(16),
         cost_estimate=FREE,
         name="add_parts",
-    )(mine, *theirs)
+    )(*held_in_hbm(mine), *theirs)
 
 
 def tail_grads(parts, tall, short):
@@ -770,32 +770,6 @@
         cost_estimate=FREE,
         name="tail_grads",
     )(*parts)
-
-
-def onward(arrived, far_own, width, lanes, split):
-    count = len(arrived)
-    micro, rows, _ = far_own.shape
-
-    def kernel(*refs):
-        blocks, far, outs = refs[:count], refs[count], refs[count + 1 :]
-        for j in range(count):
-            outs[j][0] = blocks[j][0, :, :split]
-            outs[count + j][0, :, : width - split] = far[0, :, split:width]
-            at = width + (j + 1) * lanes
-            outs[count + j][0, :, width - split :] = far[0, :, at : at + lanes]
-
-    spec = lambda n: pl.BlockSpec((1, rows, n), lambda i: (i, 0, 0))
-    sizes = [split] * count + [width + lanes - split] * count
-    out = pl.pallas_call(
-        kernel,
-        grid=(micro,),
-        in_specs=[spec(a.shape[2]) for a in (*arrived, far_own)],
-        out_specs=[spec(n) for n in sizes],
-        out_shape=[pltpu.HBM((micro, rows, n), BF16) for n in sizes],
-        cost_estimate=FREE,
-        name="onward",
-    )(*arrived, far_own)
-    return out[:count], out[count:]
 
 
 def fence(value, ready):
@@ -814,38 +788,79 @@
     )(value, *ready)
 
 
-def token_grads(seat, tokens, dy, got, wide, ready):
-    micro, rows, width = tokens.shape
-    lanes = CORES * wide
-
-    def kernel(seat_ref, x_ref, dy_ref, *refs):
-        parts = refs[: len(got)]
-        dx_out, dv_out = refs[-2:]
+def token_sums(seat, dy, got, chips, wide):
+    micro, rows, lanes = got[0].shape
+    pair = CORES * wide
+    width = lanes - pair
+    many = len(got)
+
+    def kernel(seat_ref, *refs):
+        parts, (dx_out, dv_out) = refs[:many], refs[many:]
         z = parts[0][0, :, :width].astype(F32)
         for ref in parts[1:]:
             z = z + ref[0, :, :width].astype(F32)
-        x = x_ref[0].astype(F32)
-        inv = lax.rsqrt(jnp.mean(x * x, axis=1, keepdims=True) + EPSILON)
-        inner = jnp.mean(z * x, axis=1, keepdims=True)
-        dx_out[0] = dy_ref[...] + z - x * (inv * inv * inner)
-        firsts = pieces_at([ref[0, :, width:].astype(F32) for ref in parts], seat_ref[0] // CORES)
-        for k, value in enumerate(firsts):
-            dv_out[0, :, k * lanes : (k + 1) * lanes] = value
-
-    spec = pl.BlockSpec((1, rows, width), lambda i: (i, 0, 0))
+        dx_out[0] = z
+        chip = seat_ref[0] // CORES
+        for ref, j in zip(parts, chips):
+            at = pl.multiple_of((chip ^ j) * pair, pair)
+            dv_out[0, :, pl.ds(at, pair)] = ref[0, :, width:].astype(F32)
+
+    spec = lambda n: pl.BlockSpec((1, rows, n), lambda i: (i, 0, 0))
     return pl.pallas_call(
         kernel,
         grid=(micro,),
-        in_specs=[
-            pl.BlockSpec(memory_space=pltpu.SMEM), spec, pl.BlockSpec((rows, width), lambda i: (i, 0)),
-        ]
-        + [pl.BlockSpec((1, rows, width + lanes), lambda i: (i, 0, 0))] * len(got)
-        + [corner(a) for a in ready],
-        out_specs=[spec, spec],
+        in_specs=[pl.BlockSpec(memory_space=pltpu.SMEM)] + [spec(lanes)] * many,
+        out_specs=[spec(width)] * 2,
+        out_shape=[pltpu.HBM((micro, rows, width), F32)] * 2,
+        cost_estimate=FREE,
+        name="token_sums",
+    )(seat, *got)
+
+
+def token_grads(seat, tokens, dy, dx, dv, rest, chips, wide):
+    micro, rows, width = tokens.shape
+    pair = CORES * wide
+    many = len(rest)
+
+    def kernel(seat_ref, x_ref, dy_ref, dx_ref, *refs):
+        parts = refs[:many]
+        dx_out, dv_out, buf, sems = refs[many + 1 :]
+        chip = seat_ref[0] // CORES
+        copies = Copies(sems)
+        for k, j in enumerate(chips):
+            buf[k] = parts[k][:, :, width:].astype(F32)
+            at = pl.multiple_of((chip ^ j) * pair, pair)
+            copies.start("dv", buf.at[k], dv_out.at[:, :, pl.ds(at, pair)])
+        z = dx_ref[...]
+        for ref in parts:
+            z = z + ref[:, :, :width].astype(F32)
+        x = x_ref[...].astype(F32)
+        inv = lax.rsqrt(jnp.mean(x * x, axis=2, keepdims=True) + EPSILON)
+        inner = jnp.mean(z * x, axis=2, keepdims=True)
+        dx_out[...] = dy_ref[...].reshape(micro, rows, width) + z - x * (inv * inv * inner)
+        copies.wait()
+
+    def fixed(shape):
+        return pl.BlockSpec(shape, lambda i: (0,) * len(shape), pipeline_mode=pl.Buffered(1))
+
+    anywhere = pl.BlockSpec(memory_space=pl.ANY)
+    given = [tokens, dy, dx, *rest]
+    return pl.pallas_call(
+        kernel,
+        grid=(1,),
+        in_specs=[pl.BlockSpec(memory_space=pltpu.SMEM)]
+        + [fixed(a.shape) for a in given]
+        + [anywhere],
+        out_specs=[fixed(tokens.shape), anywhere],
         out_shape=[pltpu.HBM(tokens.shape, F32)] * 2,
+        scratch_shapes=[
+            pltpu.VMEM((many, micro, rows, pair), F32), pltpu.SemaphoreType.DMA((many,)),
+        ],
+        input_output_aliases={1 + len(given): 1},
+        compiler_params=vmem(24),
         cost_estimate=FREE,
         name="token_grads",
-    )(seat, tokens, dy, *got, *ready)
+    )(seat, *given, dv)
 
 
 def projection_grads(parts, weight, gain, wide):
@@ -864,12 +879,12 @@
                 piece = total[:, t * wide : (t + 1) * wide]
                 dw_out[:, at] = piece * gain
                 grown = grown + jnp.sum(piece * w_ref[:, at].astype(F32), axis=1, keepdims=True)
-        dg_out[...] = grown
+        dg_out[...] = jnp.broadcast_to(grown, (held, 128)).T[:1, :]
 
     return pl.pallas_call(
         kernel,
         out_shape=[
-            pltpu.HBM(weight.shape, F32), pltpu.HBM((held, 1), F32),
+            pltpu.HBM(weight.shape, F32), pltpu.HBM((1, held), F32),
         ],
         cost_estimate=FREE,
         name="projection_grads",
@@ -895,18 +910,19 @@
                         out[:, to : to + short] = total[:, at : at + short]
         dgate = dgate_out[...]
         dup = dup_out[...]
-        dg_out[...] = jnp.sum(
+        grown = jnp.sum(
             dgate * gate_ref[...].astype(F32) + dup * up_ref[...].astype(F32),
             axis=1,
             keepdims=True,
         )
+        dg_out[...] = jnp.broadcast_to(grown, (held, 128)).T[:1, :]
         dgate_out[...] = dgate * gain_ref[...]
         dup_out[...] = dup * gain_ref[...]
 
     return pl.pallas_call(
         kernel,
         out_shape=[
-            pltpu.HBM((held, fan), F32), pltpu.HBM((held, fan), F32), pltpu.HBM((held, 1), F32),
+            pltpu.HBM((held, fan), F32), pltpu.HBM((held, fan), F32), pltpu.HBM((1, held), F32),
         ],
         cost_estimate=FREE,
         name="pair_grads",
@@ -1018,17 +1034,23 @@
     arrived, far_own, wqkv, own_b, grad_b = together(first_leg, arrived, far_own, own, wqkv)
     split = 128 * (lanes // 256)
 
-    def second_leg(lower, upper, arrived, far_own, tail):
-        lower = [swap(v, group) for v in lower]
-        upper = [swap(v, m) for v, m in zip(upper, inner[1:])]
-        wout = tail[:, tall:]
-        wout = jnp.stack([wout, swap(wout, group)])
+    def second_leg(arrived, far_own, tail):
+        pair = CORES * wide
+        lower, upper = [], []
+        for j in range(1, spread):
+            lower.append(swap(arrived[j - 1][..., :split], group))
+            at = width + j * pair
+            rest = jnp.concatenate([far_own[..., split:width], far_own[..., at : at + pair]], -1)
+            upper.append(swap(rest, inner[j]))
+        down, wout = tail[:, :tall], tail[:, tall:]
         grads = [swap(out_grad[:1], m) for m in inner[1:]]
-        return lower, upper, [swap(v, 1) for v in arrived], swap(far_own, 1), wout, grads
-
-    lower, upper = onward(arrived, far_own, width, CORES * wide, split)
-    lower, upper, arrived_b, far_own_b, wout, grads_lo = together(
-        second_leg, lower, upper, arrived, far_own, tail
+        return (
+            lower, upper, [swap(v, 1) for v in arrived], swap(far_own, 1), down,
+            [wout, swap(wout, group)], grads,
+        )
+
+    lower, upper, arrived_b, far_own_b, down_mine, wout, grads_lo = together(
+        second_leg, arrived, far_own, tail
     )
     mine = [own, *arrived, far_own, *lower, *upper]
     theirs = [own_b, *arrived_b, far_own_b, *[swap(v, 1) for v in lower + upper]]
@@ -1038,18 +1060,17 @@
     near = [(own, own_b)] + list(zip(arrived, arrived_b))
     cosine, sine = rope_tables(total, wide)
 
-    def attend(xs, wqkv, tail, wout):
-        down = tail[:, :tall]
+    def attend(xs, wqkv, down, wout):
+        wout = jnp.stack(wout)
         return (
             attn_fwd(seat_arr, lengths, xs, wqkv, cosine, sine, order, []),
-            down,
             swap(down, group),
             jnp.stack([wout] + [swap(wout, m) for m in inner[1:]]),
             [swap(out_grad[1:], m) for m in inner[1:]],
         )
 
-    (qkv, ot, *sends, lse, r1), down_mine, down_far, wout, grads_hi = together(
-        attend, xs, wqkv, tail, wout
+    (qkv, ot, *sends, lse, r1), down_far, wout, grads_hi = together(
+        attend, xs, wqkv, down_mine, wout
     )
 
     def spread_out(send, wout, wqkv, *grads):
@@ -1134,11 +1155,12 @@
 
     got, dwq, tail, output = together(first_return, close, far, dwq, down_mine, wout_own, landed)
 
-    def second_return(far, pair, dwq, tail):
+    def second_return(got, far, pair, dwq, tail):
         tail = [tail[0]] + [swap_depth(tail[k], k) for k in range(1, depth)]
         pair = to_seats(pair)
         return (
             [swap(far[j], across[j]) for j in range(1, spread)],
+            token_sums(seat_arr, dy, got, list(range(spread + 1)), wide),
             pair_grads(
                 pair.reshape(OUTER, group, held, 2 * slab), gate_weight, up_weight, gain2, depth,
                 fan_rows,
@@ -1147,12 +1169,15 @@
             tail_grads(tail, tall, fan_rows),
         )
 
-    rest, (gate_grad, up_grad, gain2_grad), (qkv_grad, gain1_grad), (down_grad, out_grad_w) = together(
-        second_return, far, pair, dwq, tail
-    )
-    got = [close[0]] + got + rest
-    d_tokens, d_first = token_grads(seat_arr, tokens, dy, got, wide, [])
-    gain1_grad, gain2_grad = gain1_grad[:, 0], gain2_grad[:, 0]
+    rest, (dx, dv), pair_out, projection_out, (down_grad, out_grad_w) = together(
+        second_return, [close[0]] + got, far, pair, dwq, tail
+    )
+    gate_grad, up_grad, gain2_grad = pair_out
+    qkv_grad, gain1_grad = projection_out
+    d_tokens, d_first = token_grads(
+        seat_arr, tokens, dy, dx, dv, rest, list(range(spread + 1, 2 * spread)), wide
+    )
+    gain1_grad, gain2_grad = gain1_grad.reshape(held), gain2_grad.reshape(held)
     return (
         output, d_tokens, d_first, gain1_grad, qkv_grad, out_grad_w, gain2_grad, gate_grad, up_grad,
         down_grad,

time: 354 us -> 347 us (0.980)
  starting transfers between devices: 60.3 us -> 56 us
    ppermute x36, starting transfers between devices: 29.4 us -> 25.1 us  [swap(): return lax.ppermute(value, 'seq', [(i, i ^ mask) for i in range(seats)])]
  transfers between devices with their start and end apart: 48 -> 48, of which waited for: 22 -> 21; matrix products, arithmetic and copies ran while one was open for 4% -> 5% of each run, Pallas kernels for 34% -> 35%
where the time goes in v1:
time: 347 us; the launch traced here: 341 us
  Pallas kernels  129 us (37%)
  waiting for transfers between devices  94.6 us (27%)
  starting transfers between devices  56 us (16%)
  blocking collectives  24.1 us (7%)
  between operations  14.8 us (4%)
  local copies, waits for them, and re-layouts  12.8 us (4%)
  other arithmetic  8.46 us (2%)
    ppermute x36, waiting for transfers between devices, swap(): return lax.ppermute(value, 'seq', [(i, i ^ mask) for i in range(seats)])  59 us
    pallas_call x2, Pallas kernels, feed_forward(): pl.pallas_call(functools.partial(ff_kernel, own, len(ga)), grid=(1,), in_...  34.5 us
    ppermute x36, starting transfers between devices, swap(): return lax.ppermute(value, 'seq', [(i, i ^ mask) for i in range(seats)])  25.1 us
    all_gather x1, blocking collectives, first_leg(): lax.all_gather(wqkv, 'dp', axis=1).reshape(width, 3 * wide)  24.1 us
    pallas_call x1, Pallas kernels, attn_fwd(): pl.pallas_call(functools.partial(attn_fwd_kernel, order), grid=(micro,),...  21.4 us
    all_to_all x5, starting transfers between devices, to_seats(): lax.all_to_all(value, 'seq', split_axis=0, concat_axis=0, tiled=True, axi...  21.3 us
    pallas_call x1, Pallas kernels, attn_bwd(): pl.pallas_call(functools.partial(attn_bwd_kernel, order, sent), grid=(mic...  20.6 us
    all_to_all x5, waiting for transfers between devices, to_seats(): lax.all_to_all(value, 'seq', split_axis=0, concat_axis=0, tiled=True, axi...  19.7 us
  transfers between devices with their start and end apart: 48, of which 21 were waited for; matrix products, arithmetic and copies ran while one was open for 5% of the time, Pallas kernels for 35%

profile of v1, /device:TPU:0, one launch (start us, length us, event | category | flops | bytes accessed | tf_op | source)
XLA Modules:
  0.0 340.9 jit_solution(8530617124614916547)
XLA Ops:
  10.3 25.4 %conditional.12 = (bf16[8,32,1536]{2,1,0:T(8,128)(2,1)S(1)}, bf16[8,32,384]{2,1,0:T(8,128)(2,1)}, bf16[3,128,1280]{2,1,0:T(8,128)(2,1)S(1)}, bf16[3,128,1536]{2,1,0:T(8,128)(2,1)}, bf16[3,128,1280]{2,1,0:T(8,128)(2,1)}) conditional(s32[]{:T(128)} %bitcast.21, () %tuple.117, (bf16[32,2816]{1,0:T(8,128)(2,1)}, f32[32,1]{0,1:T(1,128)S(1)}, ...), branch_computations={%region_0.1_spmd, %region_1.2_spmd} | conditional | flops 5750784 | bytes 31898080 | solution.py:987
  15.1 5.2 %all-to-all-start.4 = ((bf16[8,32,1920]{2,1,0:T(8,128)(2,1)}), bf16[8,32,1920]{2,1,0:T(8,128)(2,1)S(1)}, u32[]{:S(2)}, u32[]{:S(2)}) async-start(bf16[8,32,1920]{2,1,0:T(8,128)(2,1)} %pad_maximum_fusion), calls=%async_computation.4 | async-start | bytes 1966080 | tf_op jit(solution)/shard_map/cond/branch_1_fun/all_to_all | solution.py:995
  20.2 3.7 %payloads.1 = (bf16[3,128,1280]{2,1,0:T(8,128)(2,1)}, bf16[3,128,1536]{2,1,0:T(8,128)(2,1)}, bf16[3,128,1280]{2,1,0:T(8,128)(2,1)}) custom-call(s32[1]{0:T(128)} %get-tuple-element.301.seat_ref, bf16[3,128,1024]{2,1,0:T(8,128)(2,1)} %get-tuple-element.302.x_ref, bf16[3,128,1024]{2,1,0:T(8,128)(2,1)} %get-tuple-element.700.refs_0_.refs_1_.refs_2_.refs_3_, ...), custom_call_target="tpu_custom_call" | custom-call | bytes 14760000 | tf_op jit(solution)/shard_map/cond/branch_1_fun/payloads/pallas_call | solution.py:593
  24.0 11.0 %all-to-all-done.4 = bf16[8,32,1920]{2,1,0:T(8,128)(2,1)S(1)} async-done(((bf16[8,32,1920]{2,1,0:T(8,128)(2,1)}), bf16[8,32,1920]{2,1,0:T(8,128)(2,1)S(1)}, u32[]{:S(2)}, u32[]{:S(2)}) %all-to-all-start.4) | async-done | bytes 983072 | tf_op jit(solution)/shard_map/cond/branch_1_fun/all_to_all | solution.py:995
  36.7 25.8 %conditional.13 = (bf16[3,128,1280]{2,1,0:T(8,128)(2,1)}, bf16[3,128,1536]{2,1,0:T(8,128)(2,1)}, bf16[1024,384]{1,0:T(8,128)(2,1)}, bf16[3,128,1280]{2,1,0:T(8,128)(2,1)}, bf16[3,128,1024]{2,1,0:T(8,128)(2,1)}) conditional(s32[]{:T(128)} %bitcast.21, () %tuple.119, (bf16[3,128,1280]{2,1,0:T(8,128)(2,1)}, bf16[3,128,1536]{2,1,0:T(8,128)(2,1)}, ...), branch_computations={%region_2.3_spmd, %region_3.4_spmd} | conditional | bytes 16711880 | solution.py:987
  38.4 24.1 %all-gather = bf16[8,128,384]{2,1,0:T(8,128)(2,1)} all-gather(bf16[8,32,384]{2,1,0:T(8,128)(2,1)} %get-tuple-element.309), channel_id=2, replica_groups=mesh['seq'=8,'dp'=4] {'dp'}, dimensions={1}, use_global_device_ids=true | all-gather | bytes 983040 | tf_op jit(solution)/shard_map/cond/branch_1_fun/all_gather | solution.py:1030
  62.6 23.5 %conditional.14 = (bf16[3,128,640]{2,1,0:T(8,128)(2,1)}, bf16[3,128,640]{2,1,0:T(8,128)(2,1)}, bf16[3,128,1280]{2,1,0:T(8,128)(2,1)}, bf16[3,128,1536]{2,1,0:T(8...) conditional(s32[]{:T(128)} %bitcast.21, () %tuple.122, ...), branch_computations={%region_4.5_spmd, %region_5.6_spmd} | conditional | flops 983040 | bytes 24445260 | solution.py:987
  63.2 3.1 collective-permute-start.25
  70.7 2.8 collective-permute-done.25
  74.5 11.6 %collective-permute-done.24 = bf16[4,32,1024]{2,1,0:T(8,128)(2,1)} collective-permute-done((bf16[4,32,1024]{2,1,0:T(8,128)(2,1)}, bf16[4,32,1024]{2,1,0:T(8,128)(2,1)}, u32[]{:S(2)}, u32[]{:S(2)}) %collective-permute-start.24) | collective-permute-done | bytes 262176 | tf_op jit(solution)/shard_map/cond/branch_1_fun/ppermute | solution.py:965
  89.8 27.0 %conditional.15 = (bf16[3,1024,384]{2,1,0:T(8,128)(2,1)}, f32[3,128,1024]{2,1,0:T(8,128)}, bf16[4,3,256,128]{3,2,1,0:T(8,128)(2,1)}, bf16[4,3,256,128]{3,2,1,0:T...) conditional(s32[]{:T(128)} %bitcast.21, () %tuple.125, ...), branch_computations={%region_6.7_spmd, %region_7.8_spmd} | conditional | flops 786432 | bytes 89791032 | solution.py:987
  93.7 21.4 %attn_fwd.1 = (bf16[3,1024,384]{2,1,0:T(8,128)(2,1)}, f32[3,128,1024]{2,1,0:T(8,128)}, bf16[4,3,256,128]{3,2,1,0:T(8,128)(2,1)}, bf16[4,3,256,128]{3,2,1,0:T(8,1...) custom-call(s32[1]{0:T(128)} %get-tuple-element.316.seat_ref, s32[3]{0:T(128)S(1)} %get-tuple-element.317.len_ref, ...), custom_call_target="tpu_custom_call" | custom-call | bytes 73800000 | tf_op jit(solution)/shard_map/cond/branch_1_fun/attn_fwd/pallas_call | solution.py:188
  116.8 16.1 %conditional.16 = (bf16[4,3,256,128]{3,2,1,0:T(8,128)(2,1)}, bf16[2,2,4,32,1024]{4,3,2,1,0:T(8,128)(2,1)}, bf16[1024,384]{1,0:T(8,128)(2,1)}, bf16[1,128,1024]{2,1,0:T(8,128)(2,1)}, bf16[2,128,1024]{2,1,0:T(8,128)(2,1)}) conditional(s32[]{:T(128)} %bitcast.21, () %tuple.124, (bf16[4,3,256,128]{3,2,1,0:T(8,128)(2,1)}, ...), branch_computations={%region_8.9_spmd, %region_9.10_spmd} | conditional | bytes 12845288 | solution.py:987
  117.3 4.2 %all-to-all-start = ((bf16[4,3,256,128]{3,2,1,0:T(8,128)(2,1)}), bf16[4,3,256,128]{3,2,1,0:T(8,128)(2,1)}, u32[]{:S(2)}, u32[]{:S(2)}) async-start(bf16[4,3,256,128]{3,2,1,0:T(8,128)(2,1)} %get-tuple-element.341), calls=%async_computation | async-start | bytes 1572864 | tf_op jit(solution)/shard_map/cond/branch_1_fun/all_to_all | solution.py:995
  122.1 2.1 collective-permute-done.6
  124.2 8.7 %all-to-all-done = bf16[4,3,256,128]{3,2,1,0:T(8,128)(2,1)} async-done(((bf16[4,3,256,128]{3,2,1,0:T(8,128)(2,1)}), bf16[4,3,256,128]{3,2,1,0:T(8,128)(2,1)}, u32[]{:S(2)}, u32[]{:S(2)}) %all-to-all-start) | async-done | bytes 786464 | tf_op jit(solution)/shard_map/cond/branch_1_fun/all_to_all | solution.py:995
  132.9 2.6 collective-permute-done.33
  135.5 22.5 %conditional.17 = (bf16[384,1024]{1,0:T(8,128)(2,1)}, bf16[192,1024]{1,0:T(8,128)(2,1)}, bf16[192,1024]{1,0:T(8,128)(2,1)}, bf16[768,1024]{1,0:T(8,128)(2,1)}, b...) conditional(s32[]{:T(128)} %bitcast.21, () %tuple.121, ...), branch_computations={%region_10.11_spmd, %region_11.12_spmd} | conditional | bytes 61399408 | solution.py:987
  135.5 4.2 %all-to-all-start.1 = ((bf16[4,3,256,128]{3,2,1,0:T(8,128)(2,1)}), bf16[4,3,256,128]{3,2,1,0:T(8,128)(2,1)}, u32[]{:S(2)}, u32[]{:S(2)}) async-start(bf16[4,3,256,128]{3,2,1,0:T(8,128)(2,1)} %get-tuple-element.367), calls=%async_computation.1 | async-start | bytes 1572864 | tf_op jit(solution)/shard_map/cond/branch_1_fun/all_to_all | solution.py:995
  139.7 17.9 %ff_near.1 = (bf16[384,1024]{1,0:T(8,128)(2,1)}, bf16[192,1024]{1,0:T(8,128)(2,1)}, bf16[192,1024]{1,0:T(8,128)(2,1)}, bf16[384,1024]{1,0:T(8,128)(2,1)}, bf16[3...) custom-call(s32[1]{0:T(128)} %get-tuple-element.346.seat_ref, ...), custom_call_target="tpu_custom_call" | custom-call | bytes 59040000 | tf_op jit(solution)/shard_map/cond/branch_1_fun/ff_near/pallas_call | solution.py:465
  158.8 2.4 collective-permute-done.35.refs_0_
  161.8 2.2 add_parts.1
  164.0 20.3 %conditional.18 = (bf16[384,1024]{1,0:T(8,128)(2,1)}, bf16[192,1024]{1,0:T(8,128)(2,1)}, bf16[192,1024]{1,0:T(8,128)(2,1)}, bf16[384,1024]{1,0:T(8,128)(2,1)}, b...) conditional(s32[]{:T(128)} %bitcast.21, () %tuple.116, ...), branch_computations={%region_12.13_spmd, %region_13.14_spmd} | conditional | bytes 72671712 | solution.py:987
  164.0 2.0 collective-permute-start.8
  166.0 16.6 %ff_own.1 = (bf16[384,1024]{1,0:T(8,128)(2,1)}, bf16[192,1024]{1,0:T(8,128)(2,1)}, bf16[192,1024]{1,0:T(8,128)(2,1)}, bf16[384,1024]{1,0:T(8,128)(2,1)}, bf16[38...) custom-call(s32[1]{0:T(128)} %get-tuple-element.370.seat_ref, ...), custom_call_target="tpu_custom_call" | custom-call | bytes 59040000 | tf_op jit(solution)/shard_map/cond/branch_1_fun/ff_own/pallas_call | solution.py:465
  186.9 5.4 %middle_back.1 = (f32[384,1024]{1,0:T(8,128)}, bf16[384,1024]{1,0:T(8,128)(2,1)}, bf16[8,3,128,128]{3,2,1,0:T(8,128)(2,1)}) custom-call(f32[384,1024]{1,0:T(8,128)} %get-tuple-element.634.y_ref, bf16[3,128,1024]{2,1,0:T(8,128)(2,1)} %g_ref.1, bf16[1024,1024]{1,0:T(8,128)(2,1)} %get-tuple-element.635.w_ref, bf16[384,1024]{1,0:T(8,128)(2,1)} %get-tuple-element.636.refs_0_, ...), custom_call_target="tpu_custom_call" | custom-call | tf_op jit(solution)/shard_map/middle_back/pallas_call | solution.py:636
  192.3 21.0 %conditional.19 = (bf16[8,3,128,128]{3,2,1,0:T(8,128)(2,1)}, bf16[4,8,32,1536]{3,2,1,0:T(8,128)(2,1)}, bf16[4,96,1024]{2,1,0:T(8,128)(2,1)}, bf16[128,1024]{1,0:...) conditional(s32[]{:T(128)} %bitcast.21, () %tuple.115, ...), branch_computations={%region_14.15_spmd, %region_15.16_spmd} | conditional | bytes 63456676 | solution.py:987
  192.8 4.2 %all-to-all-start.2 = ((bf16[8,3,128,128]{3,2,1,0:T(8,128)(2,1)}), bf16[8,3,128,128]{3,2,1,0:T(8,128)(2,1)}, u32[]{:S(2)}, u32[]{:S(2)}) async-start(bf16[8,3,128,128]{3,2,1,0:T(8,128)(2,1)} %get-tuple-element.395), calls=%async_computation.2 | async-start | bytes 1572864 | tf_op jit(solution)/shard_map/cond/branch_1_fun/all_to_all | solution.py:995
  197.1 16.2 %ff_grads.1 = (bf16[4,8,32,1536]{3,2,1,0:T(8,128)(2,1)}, bf16[4,96,1024]{2,1,0:T(8,128)(2,1)}, bf16[128,1024]{1,0:T(8,128)(2,1)}, bf16[512,1024]{1,0:T(8,128)(2,...) custom-call(s32[1]{0:T(128)} %get-tuple-element.396.seat_ref, bf16[768,1024]{1,0:T(8,128)(2,1)} %get-tuple-element.397.refs_0_, ...), custom_call_target="tpu_custom_call" | custom-call | bytes 51660000 | tf_op jit(solution)/shard_map/cond/branch_1_fun/ff_grads/pallas_call | solution.py:552
  213.3 27.5 %conditional.20 = (bf16[4,3,128,512]{3,2,1,0:T(8,128)(2,1)}, bf16[4,3,128,512]{3,2,1,0:T(8,128)(2,1)}, bf16[1024,384]{1,0:T(8,128)(2,1)}, bf16[512,1024]{1,0:T(8,128)(2,1)}, bf16[512,1024]{1,0:T(8,128)(2,1)}) conditional(s32[]{:T(128)} %bitcast.21, () %tuple.114, (s32[1]{0:T(128)}, s32[3]{0:T(128)S(1)}, bf16[8,3,128,128]{3,2,1,0:T(8,128)(2,1)}, ...), branch_computations={%region_16.17_spmd, %region_17.18_spmd} | conditional | bytes 88218096 | solution.py:987
  217.0 20.6 %attn_bwd.1 = (bf16[4,3,128,512]{3,2,1,0:T(8,128)(2,1)}, bf16[4,3,128,512]{3,2,1,0:T(8,128)(2,1)}, bf16[1024,384]{1,0:T(8,128)(2,1)}) custom-call(s32[1]{0:T(128)} %get-tuple-element.421.seat_ref, s32[3]{0:T(128)S(1)} %get-tuple-element.422.len_ref, bf16[8,3,128,128]{3,2,1,0:T(8,128)(2,1)} %get-tuple-element.423.do_ref, ...), custom_call_target="tpu_custom_call" | custom-call | bytes 73800000 | tf_op jit(solution)/shard_map/cond/branch_1_fun/attn_bwd/pallas_call | solution.py:310
  240.7 11.1 %conditional.21 = (bf16[3,128,1280]{2,1,0:T(8,128)(2,1)}, bf16[3,128,1280]{2,1,0:T(8,128)(2,1)}, bf16[3,128,1280]{2,1,0:T(8,128)(2,1)}, bf16[3,128,1280]{2,1,0:T...) conditional(s32[]{:T(128)} %bitcast.21, () %tuple.113, ...), branch_computations={%region_18.19_spmd, %region_19.20_spmd} | conditional | bytes 28935928 | solution.py:987
  242.7 2.8 collective-permute-done.13.b_ref
  245.5 6.4 %back_to_x.1 = (bf16[3,128,1280]{2,1,0:T(8,128)(2,1)}, bf16[3,128,1280]{2,1,0:T(8,128)(2,1)}, bf16[3,128,1280]{2,1,0:T(8,128)(2,1)}, bf16[3,128,1280]{2,1,0:T(8,128)(2,1)}) custom-call(s32[1]{0:T(128)} %get-tuple-element.445.seat_ref, bf16[4,3,128,512]{3,2,1,0:T(8,128)(2,1)} %get-tuple-element.446.a_ref, ...), custom_call_target="tpu_custom_call" | custom-call | bytes 18450000 | tf_op jit(solution)/shard_map/cond/branch_1_fun/back_to_x/pallas_call | solution.py:683
  251.9 39.0 %conditional.22 = (bf16[3,128,1280]{2,1,0:T(8,128)(2,1)}, bf16[3,128,1280]{2,1,0:T(8,128)(2,1)}, bf16[32,32,384]{2,1,0:T(8,128)(2,1)}, bf16[128,1024]{1,0:T(8,12...) conditional(s32[]{:T(128)} %bitcast.21, () %tuple.112, ...), branch_computations={%region_20.21_spmd, %region_21.22_spmd} | conditional | flops 2752512 | bytes 14942384 | solution.py:987
  251.9 5.0 %all-to-all-start.5 = ((bf16[32,32,384]{2,1,0:T(8,128)(2,1)}), bf16[32,32,384]{2,1,0:T(8,128)(2,1)}, u32[]{:S(2)}, u32[]{:S(2)}) async-start(bf16[32,32,384]{2,1,0:T(8,128)(2,1)} %bitcast.13), calls=%async_computation.5 | async-start | bytes 1572864 | tf_op jit(solution)/shard_map/cond/branch_1_fun/all_to_all | solution.py:1000
  260.2 3.0 plane_sums.1
  263.2 2.6 add_convert_fusion
  265.8 23.0 %collective-permute-done.29 = bf16[3,128,1280]{2,1,0:T(8,128)(2,1)} collective-permute-done((bf16[3,128,1280]{2,1,0:T(8,128)(2,1)}, bf16[3,128,1280]{2,1,0:T(8,128)(2,1)}, u32[]{:S(2)}, u32[]{:S(2)}) %collective-permute-start.29) | collective-permute-done | bytes 983072 | tf_op jit(solution)/shard_map/cond/branch_1_fun/ppermute | solution.py:965
  291.8 38.1 %conditional.23 = (bf16[3,128,1280]{2,1,0:T(8,128)(2,1)}, f32[3,128,1024]{2,1,0:T(8,128)}, f32[3,128,1024]{2,1,0:T(8,128)}, f32[32,2816]{1,0:T(8,128)}, f32[32,2...) conditional(s32[]{:T(128)} %bitcast.21, () %tuple.134, ...), branch_computations={%region_23.24_spmd, %region_24.25_spmd} | conditional | bytes 13304648 | solution.py:987
  291.9 2.4 collective-permute-start.16
  294.3 3.5 %all-to-all-start.3 = ((bf16[8,32,1536]{2,1,0:T(8,128)(2,1)}), bf16[8,32,1536]{2,1,0:T(8,128)(2,1)S(1)}, u32[]{:S(2)}, u32[]{:S(2)}) async-start(bf16[8,32,1536]{2,1,0:T(8,128)(2,1)} %bitcast.52), calls=%async_computation.3 | async-start | bytes 1572864 | tf_op jit(solution)/shard_map/cond/branch_1_fun/all_to_all | solution.py:995
  303.7 2.0 projection_grads.1
  305.7 4.4 %token_sums.1 = (f32[3,128,1024]{2,1,0:T(8,128)}, f32[3,128,1024]{2,1,0:T(8,128)}) custom-call(s32[1]{0:T(128)} %get-tuple-element.473.seat_ref, bf16[3,128,1280]{2,1,0:T(8,128)(2,1)} %get-tuple-element.474.refs_0_, bf16[3,128,1280]{2,1,0:T(8,128)(2,1)} %get-tuple-element.475.refs_1_, bf16[3,128,1280]{2,1,0:T(8,128)(2,1)} %get-tuple-element.476.refs_2_), custom_call_target="tpu_custom_call" | custom-call | tf_op jit(solution)/shard_map/cond/branch_1_fun/token_sums/pallas_call | solution.py:809
  310.1 14.3 %collective-permute-done.18.refs_2_ = bf16[128,1024]{1,0:T(8,128)(2,1)} collective-permute-done((bf16[128,1024]{1,0:T(8,128)(2,1)}, bf16[128,1024]{1,0:T(8,128)(2,1)}, u32[]{:S(2)}, u32[]{:S(2)}) %collective-permute-start.18) | collective-permute-done | bytes 262176 | tf_op jit(solution)/shard_map/cond/branch_1_fun/ppermute | solution.py:971
  324.4 2.0 tail_grads.1
  327.3 2.6 pair_grads.1
  329.9 4.2 %token_grads.1 = (f32[3,128,1024]{2,1,0:T(8,128)}, f32[3,128,1024]{2,1,0:T(8,128)}) custom-call(s32[1]{0:T(128)} %bitcast.22.seat_ref, bf16[3,128,1024]{2,1,0:T(8,128)(2,1)S(1)} %copy-done.7, f32[384,1024]{1,0:T(8,128)S(1)} %copy-done, f32[3,128,1024]{2,1,0:T(8,128)} %get-tuple-element.687.dx_ref, ...), custom_call_target="tpu_custom_call", output_to_operand_aliasing={{1}: (5, {})} | custom-call | tf_op jit(solution)/shard_map/token_grads/pallas_call | solution.py:848
  (162 shorter events, 54.1 us)
Async XLA Ops:
  7.2 55.4 %all-gather.6.cloned.1.call-start = ((), (), s32[]{:S(2)}) async-start(), calls=%async_computation.8 | async-start | bytes 1310720 | tf_op jit(solution)/shard_map/all_gather | solution.py:1005
  8.9 126.6 %all-gather.8.cloned.1.call-start = ((), (), s32[]{:S(2)}) async-start(), calls=%async_computation.9 | async-start | bytes 3932160 | tf_op jit(solution)/shard_map/all_gather | solution.py:1025
  15.1 19.9 %all-to-all-start.4 = ((bf16[8,32,1920]{2,1,0:T(8,128)(2,1)}), bf16[8,32,1920]{2,1,0:T(8,128)(2,1)S(1)}, u32[]{:S(2)}, u32[]{:S(2)}) async-start(bf16[8,32,1920]{2,1,0:T(8,128)(2,1)} %pad_maximum_fusion), calls=%async_computation.4 | async-start | bytes 1966080 | tf_op jit(solution)/shard_map/cond/branch_1_fun/all_to_all | solution.py:995
  36.6 254.3 %reduce-scatter.2.cloned.1.call-start = ((), (), s32[]{:S(2)}) async-start(), calls=%async_computation.7 | async-start | bytes 3932160 | tf_op jit(solution)/shard_map/reduce_scatter | solution.py:1127
  36.7 25.8 %collective-permute-start.1 = (bf16[3,128,1536]{2,1,0:T(8,128)(2,1)}, bf16[3,128,1536]{2,1,0:T(8,128)(2,1)}, u32[]{:S(2)}, u32[]{:S(2)}) collective-permute-start(bf16[3,128,1536]{2,1,0:T(8,128)(2,1)} %get-tuple-element.308), channel_id=1, source_target_pairs={{0,16},{4,20},{8,24},{12,28},{16,0},{20,4},{24,8},{28,12},{1,17},{... | collective-permute-start | bytes 3538952 | tf_op jit(solution)/shard_map/cond/branch_1_fun/ppermute | solution.py:965
  37.3 25.2 %collective-permute-start = (bf16[3,128,1280]{2,1,0:T(8,128)(2,1)}, bf16[3,128,1280]{2,1,0:T(8,128)(2,1)}, u32[]{:S(2)}, u32[]{:S(2)}) collective-permute-start(bf16[3,128,1280]{2,1,0:T(8,128)(2,1)} %get-tuple-element.307), channel_id=1, source_target_pairs={{0,8},{4,12},{8,0},{12,4},{16,24},{20,28},{24,16},{28,20},{1,9},{5... | collective-permute-start | bytes 2949128 | tf_op jit(solution)/shard_map/cond/branch_1_fun/ppermute | solution.py:965
  37.9 24.6 %collective-permute-start.2 = (bf16[3,128,1280]{2,1,0:T(8,128)(2,1)S(1)}, bf16[3,128,1280]{2,1,0:T(8,128)(2,1)}, u32[]{:S(2)}, u32[]{:S(2)}) collective-permute-start(bf16[3,128,1280]{2,1,0:T(8,128)(2,1)S(1)} %get-tuple-element.310), channel_id=1, source_target_pairs={{0,4},{4,0},{8,12},{12,8},{16,20},{20,16},{24,28},{28,24},{1,5},{5... | collective-permute-start | bytes 2949128 | tf_op jit(solution)/shard_map/cond/branch_1_fun/ppermute | solution.py:965
  37.9 24.6 %collective-permute-start.3 = (bf16[3,128,1024]{2,1,0:T(8,128)(2,1)S(1)}, bf16[3,128,1024]{2,1,0:T(8,128)(2,1)}, u32[]{:S(2)}, u32[]{:S(2)}) collective-permute-start(bf16[3,128,1024]{2,1,0:T(8,128)(2,1)S(1)} %get-tuple-element.311), channel_id=1, source_target_pairs={{0,4},{4,0},{8,12},{12,8},{16,20},{20,16},{24,28},{28,24},{1,5},{5... | collective-permute-start | bytes 2359304 | tf_op jit(solution)/shard_map/cond/branch_1_fun/ppermute | solution.py:965
  62.6 23.5 %collective-permute-start.23 = (bf16[3,128,1536]{2,1,0:T(8,128)(2,1)}, bf16[3,128,1536]{2,1,0:T(8,128)(2,1)}, u32[]{:S(2)}, u32[]{:S(2)}) collective-permute-start(bf16[3,128,1536]{2,1,0:T(8,128)(2,1)} %get-tuple-element.313), channel_id=1, source_target_pairs={{0,4},{4,0},{8,12},{12,8},{16,20},{20,16},{24,28},{28,24},{1,5},{5... | collective-permute-start | bytes 3538952 | tf_op jit(solution)/shard_map/cond/branch_1_fun/ppermute | solution.py:965
  62.7 23.4 %collective-permute-start.22 = (bf16[3,128,1280]{2,1,0:T(8,128)(2,1)}, bf16[3,128,1280]{2,1,0:T(8,128)(2,1)}, u32[]{:S(2)}, u32[]{:S(2)}) collective-permute-start(bf16[3,128,1280]{2,1,0:T(8,128)(2,1)} %get-tuple-element.312), channel_id=1, source_target_pairs={{0,4},{4,0},{8,12},{12,8},{16,20},{20,16},{24,28},{28,24},{1,5},{5... | collective-permute-start | bytes 2949128 | tf_op jit(solution)/shard_map/cond/branch_1_fun/ppermute | solution.py:965
  63.2 10.3 %collective-permute-start.25 = (bf16[1,128,1024]{2,1,0:T(8,128)(2,1)S(1)}, bf16[1,128,1024]{2,1,0:T(8,128)(2,1)}, u32[]{:S(2)}, u32[]{:S(2)}) collective-permute-start(bf16[1,128,1024]{2,1,0:T(8,128)(2,1)S(1)} %slice.27), channel_id=1, source_target_pairs={{0,8},{4,12},{8,0},{12,4},{16,24},{20,28},{24,16},{28,20},{1,9},{5... | collective-permute-start | bytes 786440 | tf_op jit(solution)/shard_map/cond/branch_1_fun/ppermute | solution.py:965
  67.4 18.7 %collective-permute-start.20 = (bf16[3,128,640]{2,1,0:T(8,128)(2,1)S(1)}, bf16[3,128,640]{2,1,0:T(8,128)(2,1)}, u32[]{:S(2)}, u32[]{:S(2)}) collective-permute-start(bf16[3,128,640]{2,1,0:T(8,128)(2,1)S(1)} %slice.22), channel_id=1, source_target_pairs={{0,16},{4,20},{8,24},{12,28},{16,0},{20,4},{24,8},{28,12},{1,17},{... | collective-permute-start | bytes 1474568 | tf_op jit(solution)/shard_map/cond/branch_1_fun/ppermute | solution.py:965
  69.8 16.3 %collective-permute-start.21 = (bf16[3,128,640]{2,1,0:T(8,128)(2,1)S(1)}, bf16[3,128,640]{2,1,0:T(8,128)(2,1)}, u32[]{:S(2)}, u32[]{:S(2)}) collective-permute-start(bf16[3,128,640]{2,1,0:T(8,128)(2,1)S(1)} %pad_maximum_fusion.1), channel_id=1, source_target_pairs={{0,8},{4,12},{8,0},{12,4},{16,24},{20,28},{24,16},{28,20},{1,9},{5... | collective-permute-start | bytes 1474568 | tf_op jit(solution)/shard_map/cond/branch_1_fun/ppermute | solution.py:965
  73.5 12.6 %collective-permute-start.24 = (bf16[4,32,1024]{2,1,0:T(8,128)(2,1)}, bf16[4,32,1024]{2,1,0:T(8,128)(2,1)}, u32[]{:S(2)}, u32[]{:S(2)}) collective-permute-start(bf16[4,32,1024]{2,1,0:T(8,128)(2,1)} %slice.48), channel_id=1, source_target_pairs={{0,16},{4,20},{8,24},{12,28},{16,0},{20,4},{24,8},{28,12},{1,17},{... | collective-permute-start | bytes 786440 | tf_op jit(solution)/shard_map/cond/branch_1_fun/ppermute | solution.py:965
  86.1 2.1 collective-permute-start.31
  86.2 2.8 collective-permute-start.32
  90.0 26.8 %collective-permute-start.26 = (bf16[4,96,1024]{2,1,0:T(8,128)(2,1)}, bf16[4,96,1024]{2,1,0:T(8,128)(2,1)}, u32[]{:S(2)}, u32[]{:S(2)}) collective-permute-start(bf16[4,96,1024]{2,1,0:T(8,128)(2,1)} %get-tuple-element.337), channel_id=1, source_target_pairs={{0,16},{4,20},{8,24},{12,28},{16,0},{20,4},{24,8},{28,12},{1,17},{... | collective-permute-start | bytes 2359304 | tf_op jit(solution)/shard_map/cond/branch_1_fun/ppermute | solution.py:965
  91.5 23.6 %collective-permute-start.27 = (bf16[2,4,32,1024]{3,2,1,0:T(8,128)(2,1)S(1)}, bf16[2,4,32,1024]{3,2,1,0:T(8,128)(2,1)S(1)}, u32[]{:S(2)}, u32[]{:S(2)}) collective-permute-start(bf16[2,4,32,1024]{3,2,1,0:T(8,128)(2,1)S(1)} %get-tuple-element.753), channel_id=1, source_target_pairs={{0,8},{4,12},{8,0},{12,4},{16,24},{20,28},{24,16},{28,20},{1,9},{5... | collective-permute-start | bytes 1572872 | tf_op jit(solution)/shard_map/cond/branch_1_fun/ppermute | solution.py:965
  92.0 24.8 %collective-permute-start.28 = (bf16[2,128,1024]{2,1,0:T(8,128)(2,1)S(1)}, bf16[2,128,1024]{2,1,0:T(8,128)(2,1)}, u32[]{:S(2)}, u32[]{:S(2)}) collective-permute-start(bf16[2,128,1024]{2,1,0:T(8,128)(2,1)S(1)} %slice.28), channel_id=1, source_target_pairs={{0,8},{4,12},{8,0},{12,4},{16,24},{20,28},{24,16},{28,20},{1,9},{5... | collective-permute-start | bytes 1572872 | tf_op jit(solution)/shard_map/cond/branch_1_fun/ppermute | solution.py:965
  116.8 16.1 %collective-permute-start.4 = (bf16[2,2,4,32,1024]{4,3,2,1,0:T(8,128)(2,1)S(1)}, bf16[2,2,4,32,1024]{4,3,2,1,0:T(8,128)(2,1)}, u32[]{:S(2)}, u32[]{:S(2)}) collective-permute-start(bf16[2,2,4,32,1024]{4,3,2,1,0:T(8,128)(2,1)S(1)} %get-tuple-element.342), channel_id=1, source_target_pairs={{0,4},{4,0},{8,12},{12,8},{16,20},{20,16},{24,28},{28,24},{1,5},{5... | collective-permute-start | bytes 3145736 | tf_op jit(solution)/shard_map/cond/branch_1_fun/ppermute | solution.py:965
  116.8 16.1 %collective-permute-start.5 = (bf16[1024,384]{1,0:T(8,128)(2,1)}, bf16[1024,384]{1,0:T(8,128)(2,1)}, u32[]{:S(2)}, u32[]{:S(2)}) collective-permute-start(bf16[1024,384]{1,0:T(8,128)(2,1)} %get-tuple-element.343), channel_id=1, source_target_pairs={{0,4},{4,0},{8,12},{12,8},{16,20},{20,16},{24,28},{28,24},{1,5},{5... | collective-permute-start | bytes 2359304 | tf_op jit(solution)/shard_map/cond/branch_1_fun/ppermute | solution.py:965
  117.3 15.6 %all-to-all-start = ((bf16[4,3,256,128]{3,2,1,0:T(8,128)(2,1)}), bf16[4,3,256,128]{3,2,1,0:T(8,128)(2,1)}, u32[]{:S(2)}, u32[]{:S(2)}) async-start(bf16[4,3,256,128]{3,2,1,0:T(8,128)(2,1)} %get-tuple-element.341), calls=%async_computation | async-start | bytes 1572864 | tf_op jit(solution)/shard_map/cond/branch_1_fun/all_to_all | solution.py:995
  121.5 2.7 collective-permute-start.7
  121.6 2.6 collective-permute-start.6
  132.9 2.6 collective-permute-start.33
  135.5 22.1 %all-to-all-start.1 = ((bf16[4,3,256,128]{3,2,1,0:T(8,128)(2,1)}), bf16[4,3,256,128]{3,2,1,0:T(8,128)(2,1)}, u32[]{:S(2)}, u32[]{:S(2)}) async-start(bf16[4,3,256,128]{3,2,1,0:T(8,128)(2,1)} %get-tuple-element.367), calls=%async_computation.1 | async-start | bytes 1572864 | tf_op jit(solution)/shard_map/cond/branch_1_fun/all_to_all | solution.py:995
  158.1 5.9 %collective-permute-start.34 = (bf16[4,3,256,128]{3,2,1,0:T(8,128)(2,1)}, bf16[4,3,256,128]{3,2,1,0:T(8,128)(2,1)S(1)}, u32[]{:S(2)}, u32[]{:S(2)}) collective-permute-start(bf16[4,3,256,128]{3,2,1,0:T(8,128)(2,1)} %get-tuple-element.629), channel_id=1, source_target_pairs={{0,4},{4,0},{8,12},{12,8},{16,20},{20,16},{24,28},{28,24},{1,5},{5... | collective-permute-start | bytes 2359304 | tf_op jit(solution)/shard_map/ppermute | solution.py:965
  158.3 2.9 collective-permute-start.35
  158.6 3.1 collective-permute-start.36
  164.0 20.1 %collective-permute-start.8 = (bf16[384,1024]{1,0:T(8,128)(2,1)}, bf16[384,1024]{1,0:T(8,128)(2,1)}, u32[]{:S(2)}, u32[]{:S(2)}) collective-permute-start(bf16[384,1024]{1,0:T(8,128)(2,1)} %get-tuple-element.394), channel_id=1, source_target_pairs={{0,8},{4,12},{8,0},{12,4},{16,24},{20,28},{24,16},{28,20},{1,9},{5... | collective-permute-start | bytes 2359304 | tf_op jit(solution)/shard_map/cond/branch_1_fun/ppermute | solution.py:965
  184.3 2.0 collective-permute-start.37
  184.4 2.5 collective-permute-start.38
  192.3 4.8 %collective-permute-start.10 = (bf16[1,384,1024]{2,1,0:T(8,128)(2,1)}, bf16[1,384,1024]{2,1,0:T(8,128)(2,1)}, u32[]{:S(2)}, u32[]{:S(2)}) collective-permute-start(bf16[1,384,1024]{2,1,0:T(8,128)(2,1)} %get-tuple-element.414), channel_id=1, source_target_pairs={{0,4},{4,0},{8,12},{12,8},{16,20},{20,16},{24,28},{28,24},{1,5},{5... | collective-permute-start | bytes 2359304 | tf_op jit(solution)/shard_map/cond/branch_1_fun/ppermute | solution.py:965
  192.4 4.6 %collective-permute-start.9 = (bf16[384,1024]{1,0:T(8,128)(2,1)}, bf16[384,1024]{1,0:T(8,128)(2,1)}, u32[]{:S(2)}, u32[]{:S(2)}) collective-permute-start(bf16[384,1024]{1,0:T(8,128)(2,1)} %get-tuple-element.412.refs_15_), channel_id=1, source_target_pairs={{0,4},{4,0},{8,12},{12,8},{16,20},{20,16},{24,28},{28,24},{1,5},{5... | collective-permute-start | bytes 2359304 | tf_op jit(solution)/shard_map/cond/branch_1_fun/ppermute | solution.py:965
  192.8 20.5 %all-to-all-start.2 = ((bf16[8,3,128,128]{3,2,1,0:T(8,128)(2,1)}), bf16[8,3,128,128]{3,2,1,0:T(8,128)(2,1)}, u32[]{:S(2)}, u32[]{:S(2)}) async-start(bf16[8,3,128,128]{3,2,1,0:T(8,128)(2,1)} %get-tuple-element.395), calls=%async_computation.2 | async-start | bytes 1572864 | tf_op jit(solution)/shard_map/cond/branch_1_fun/all_to_all | solution.py:995
  213.5 25.8 %collective-permute-start.11 = (bf16[512,1024]{1,0:T(8,128)(2,1)}, bf16[512,1024]{1,0:T(8,128)(2,1)}, u32[]{:S(2)}, u32[]{:S(2)}) collective-permute-start(bf16[512,1024]{1,0:T(8,128)(2,1)} %get-tuple-element.443), channel_id=1, source_target_pairs={{0,8},{4,12},{8,0},{12,4},{16,24},{20,28},{24,16},{28,20},{1,9},{5... | collective-permute-start | bytes 3145736 | tf_op jit(solution)/shard_map/cond/branch_1_fun/ppermute | solution.py:965
  215.5 25.2 %collective-permute-start.12 = (bf16[512,1024]{1,0:T(8,128)(2,1)}, bf16[512,1024]{1,0:T(8,128)(2,1)}, u32[]{:S(2)}, u32[]{:S(2)}) collective-permute-start(bf16[512,1024]{1,0:T(8,128)(2,1)} %get-tuple-element.444), channel_id=1, source_target_pairs={{0,16},{4,20},{8,24},{12,28},{16,0},{20,4},{24,8},{28,12},{1,17},{... | collective-permute-start | bytes 3145736 | tf_op jit(solution)/shard_map/cond/branch_1_fun/ppermute | solution.py:965
  240.7 4.7 %collective-permute-start.13 = (bf16[4,3,128,512]{3,2,1,0:T(8,128)(2,1)}, bf16[4,3,128,512]{3,2,1,0:T(8,128)(2,1)S(1)}, u32[]{:S(2)}, u32[]{:S(2)}) collective-permute-start(bf16[4,3,128,512]{3,2,1,0:T(8,128)(2,1)} %get-tuple-element.447), channel_id=1, source_target_pairs={{0,4},{4,0},{8,12},{12,8},{16,20},{20,16},{24,28},{28,24},{1,5},{5... | collective-permute-start | bytes 4718600 | tf_op jit(solution)/shard_map/cond/branch_1_fun/ppermute | solution.py:965
  240.7 11.1 %collective-permute-start.15 = (bf16[384,1024]{1,0:T(8,128)(2,1)}, bf16[384,1024]{1,0:T(8,128)(2,1)}, u32[]{:S(2)}, u32[]{:S(2)}) collective-permute-start(bf16[384,1024]{1,0:T(8,128)(2,1)} %get-tuple-element.455), channel_id=1, source_target_pairs={{0,4},{4,0},{8,12},{12,8},{16,20},{20,16},{24,28},{28,24},{1,5},{5... | collective-permute-start | bytes 2359304 | tf_op jit(solution)/shard_map/cond/branch_1_fun/ppermute | solution.py:965
  241.2 10.6 %collective-permute-start.14 = (bf16[128,1024]{1,0:T(8,128)(2,1)}, bf16[128,1024]{1,0:T(8,128)(2,1)}, u32[]{:S(2)}, u32[]{:S(2)}) collective-permute-start(bf16[128,1024]{1,0:T(8,128)(2,1)} %get-tuple-element.454), channel_id=1, source_target_pairs={{0,24},{4,28},{8,16},{12,20},{16,8},{20,12},{24,0},{28,4},{1,25},{... | collective-permute-start | bytes 786440 | tf_op jit(solution)/shard_map/cond/branch_1_fun/ppermute | solution.py:965
  251.9 39.0 %all-to-all-start.5 = ((bf16[32,32,384]{2,1,0:T(8,128)(2,1)}), bf16[32,32,384]{2,1,0:T(8,128)(2,1)}, u32[]{:S(2)}, u32[]{:S(2)}) async-start(bf16[32,32,384]{2,1,0:T(8,128)(2,1)} %bitcast.13), calls=%async_computation.5 | async-start | bytes 1572864 | tf_op jit(solution)/shard_map/cond/branch_1_fun/all_to_all | solution.py:1000
  256.9 31.8 %collective-permute-start.29 = (bf16[3,128,1280]{2,1,0:T(8,128)(2,1)}, bf16[3,128,1280]{2,1,0:T(8,128)(2,1)}, u32[]{:S(2)}, u32[]{:S(2)}) collective-permute-start(bf16[3,128,1280]{2,1,0:T(8,128)(2,1)} %get-tuple-element.456), channel_id=1, source_target_pairs={{0,8},{4,12},{8,0},{12,4},{16,24},{20,28},{24,16},{28,20},{1,9},{5... | collective-permute-start | bytes 2949128 | tf_op jit(solution)/shard_map/cond/branch_1_fun/ppermute | solution.py:965
  258.7 30.6 %collective-permute-start.30 = (bf16[3,128,1280]{2,1,0:T(8,128)(2,1)}, bf16[3,128,1280]{2,1,0:T(8,128)(2,1)}, u32[]{:S(2)}, u32[]{:S(2)}) collective-permute-start(bf16[3,128,1280]{2,1,0:T(8,128)(2,1)} %get-tuple-element.457), channel_id=1, source_target_pairs={{0,16},{4,20},{8,24},{12,28},{16,0},{20,4},{24,8},{28,12},{1,17},{... | collective-permute-start | bytes 2949128 | tf_op jit(solution)/shard_map/cond/branch_1_fun/ppermute | solution.py:965
  291.9 38.0 %collective-permute-start.16 = (bf16[3,128,1280]{2,1,0:T(8,128)(2,1)}, bf16[3,128,1280]{2,1,0:T(8,128)(2,1)}, u32[]{:S(2)}, u32[]{:S(2)}) collective-permute-start(bf16[3,128,1280]{2,1,0:T(8,128)(2,1)} %get-tuple-element.472), channel_id=1, source_target_pairs={{0,24},{4,28},{8,16},{12,20},{16,8},{20,12},{24,0},{28,4},{1,25},{... | collective-permute-start | bytes 2949128 | tf_op jit(solution)/shard_map/cond/branch_1_fun/ppermute | solution.py:965
  294.3 32.1 %all-to-all-start.3 = ((bf16[8,32,1536]{2,1,0:T(8,128)(2,1)}), bf16[8,32,1536]{2,1,0:T(8,128)(2,1)S(1)}, u32[]{:S(2)}, u32[]{:S(2)}) async-start(bf16[8,32,1536]{2,1,0:T(8,128)(2,1)} %bitcast.52), calls=%async_computation.3 | async-start | bytes 1572864 | tf_op jit(solution)/shard_map/cond/branch_1_fun/all_to_all | solution.py:995
  297.9 12.2 %collective-permute-start.19 = (bf16[128,1024]{1,0:T(8,128)(2,1)}, bf16[128,1024]{1,0:T(8,128)(2,1)}, u32[]{:S(2)}, u32[]{:S(2)}) collective-permute-start(bf16[128,1024]{1,0:T(8,128)(2,1)} %get-tuple-element.492), channel_id=1, source_target_pairs={{0,3},{1,2},{2,1},{3,0},{4,7},{5,6},{6,5},{7,4},{8,11},{9,10},{10,... | collective-permute-start | bytes 786440 | tf_op jit(solution)/shard_map/cond/branch_1_fun/ppermute | solution.py:971
  299.3 25.0 %collective-permute-start.18 = (bf16[128,1024]{1,0:T(8,128)(2,1)}, bf16[128,1024]{1,0:T(8,128)(2,1)}, u32[]{:S(2)}, u32[]{:S(2)}) collective-permute-start(bf16[128,1024]{1,0:T(8,128)(2,1)} %get-tuple-element.491), channel_id=1, source_target_pairs={{0,2},{1,3},{2,0},{3,1},{4,6},{5,7},{6,4},{7,5},{8,10},{9,11},{10,... | collective-permute-start | bytes 786440 | tf_op jit(solution)/shard_map/cond/branch_1_fun/ppermute | solution.py:971
  300.6 23.8 %collective-permute-start.17 = (bf16[128,1024]{1,0:T(8,128)(2,1)}, bf16[128,1024]{1,0:T(8,128)(2,1)}, u32[]{:S(2)}, u32[]{:S(2)}) collective-permute-start(bf16[128,1024]{1,0:T(8,128)(2,1)} %get-tuple-element.490), channel_id=1, source_target_pairs={{0,1},{1,0},{2,3},{3,2},{4,5},{5,4},{6,7},{7,6},{8,9},{9,8},{10,11... | collective-permute-start | bytes 786440 | tf_op jit(solution)/shard_map/cond/branch_1_fun/ppermute | solution.py:971
  (26 other events, 313.2 us)
Sparse Core Ops, SparseCore 0:
  10.2 30.6 all-gather.5
  42.4 66.3 all-gather.7
  213.4 73.8 reduce-scatter.1

commit v2 on v1

--- a/solution.py
+++ b/solution.py
@@ -651,14 +651,14 @@
     )(*given)
 
 
-def back_to_x(seat, mine, theirs, w_mine, w_theirs):
+def back_to_x(seat, mine, theirs, w_mine, w_theirs, ready):
     count, micro, rows, lanes = mine.shape
     width = w_mine.shape[0]
     wide = lanes // 4
     many = micro * rows
 
     def kernel(seat_ref, a_ref, b_ref, wa, wb, *refs):
-        outs = refs[:count]
+        outs = refs[len(ready) : len(ready) + count]
         buf, sems = refs[-2:]
         core = seat_ref[0] % CORES
         copies = Copies(sems)
@@ -683,7 +683,8 @@
     return pl.pallas_call(
         kernel,
         grid=(1,),
-        in_specs=[pl.BlockSpec(memory_space=pltpu.SMEM)] + [fixed(a.shape) for a in given],
+        in_specs=[pl.BlockSpec(memory_space=pltpu.SMEM)] + [fixed(a.shape) for a in given]
+        + [corner(a) for a in ready],
         out_specs=[anywhere] * count,
         out_shape=[out] * count,
         scratch_shapes=[
@@ -693,7 +694,7 @@
         compiler_params=vmem(32),
         cost_estimate=lasting(5),
         name="back_to_x",
-    )(seat, *given)
+    )(seat, *given, *ready)
 
 
 def plane_sums(level, down, wout, parcels):
@@ -1133,27 +1134,23 @@
             seat_arr, lengths, xs, wqkv.shape, d_o, cosine, sine, qkv, ot, lse, r1, order,
             across + inner, [],
         )
-        return out, [swap(v, m) for v, m in zip(parcels, inner[1:] + across[:1])]
-
-    (e_mine, e_theirs, dwq), landed = together(attend_back, parcels[:spread], d_o, xs)
-
-    def to_x(e_theirs, parcels, fb):
-        both = back_to_x(seat_arr, e_mine, swap(e_theirs, 1), wqkv, wqkv_theirs)
-        return both, [swap(v, m) for v, m in zip(parcels, across[1:])], swap(fb, 1)
-
-    both, more, fb = together(to_x, e_theirs, parcels[spread:], fb)
-    landed = landed + more
-    far, close = both[:spread], both[spread:]
-
-    def first_return(close, far, dwq, down_mine, wout_own, landed):
+        return out, [swap(v, m) for v, m in zip(parcels, inner[1:] + across)]
+
+    (e_mine, e_theirs, dwq), landed = together(attend_back, parcels, d_o, xs)
+
+    def first_return(e_theirs, fb, dwq, down_mine, wout_own, landed):
+        dwq = to_all(dwq.reshape(devices, held, 3 * wide))
+        both = back_to_x(seat_arr, e_mine, swap(e_theirs, 1), wqkv, wqkv_theirs, [])
+        far, close = both[:spread], both[spread:]
         got = [swap(close[j], inner[j]) for j in range(1, spread)] + [swap(far[0], across[0])]
-        dwq = to_all(dwq.reshape(devices, held, 3 * wide))
         tail = plane_sums(level_arr, down_mine, wout_own, landed)
-        output = y + fa.astype(F32) + fb.astype(F32)
+        output = y + fa.astype(F32) + swap(fb, 1).astype(F32)
         output = output + sum(v[:many].astype(F32) for v in landed[: spread - 1])
-        return got, dwq, tail, output.astype(BF16).reshape(tokens.shape)
-
-    got, dwq, tail, output = together(first_return, close, far, dwq, down_mine, wout_own, landed)
+        return [close[0]] + got, far, dwq, tail, output.astype(BF16).reshape(tokens.shape)
+
+    got, far, dwq, tail, output = together(
+        first_return, e_theirs, fb, dwq, down_mine, wout_own, landed
+    )
 
     def second_return(got, far, pair, dwq, tail):
         tail = [tail[0]] + [swap_depth(tail[k], k) for k in range(1, depth)]
@@ -1170,7 +1167,7 @@
         )
 
     rest, (dx, dv), pair_out, projection_out, (down_grad, out_grad_w) = together(
-        second_return, [close[0]] + got, far, pair, dwq, tail
+        second_return, got, far, pair, dwq, tail
     )
     gate_grad, up_grad, gain2_grad = pair_out
     qkv_grad, gain1_grad = projection_out

time: 347 us -> 347 us (level)
    all_to_all x1, waiting for transfers between devices: 1.59 us -> 22.9 us  [to_all(): return lax.all_to_all(value, every, split_axis=0, concat_axis=0, tiled=True)]
    ppermute x36, waiting for transfers between devices: 59 us -> 38.1 us  [swap(): return lax.ppermute(value, 'seq', [(i, i ^ mask) for i in range(seats)])]
  transfers between devices with their start and end apart: 48 -> 48, of which waited for: 21 -> 18; matrix products, arithmetic and copies ran while one was open for 5% -> 5% of each run, Pallas kernels for 35% -> 35%
where the time goes in v2:
time: 347 us; the launch traced here: 340 us
  Pallas kernels  128 us (37%)
  waiting for transfers between devices  96.6 us (28%)
  starting transfers between devices  55 us (16%)
  blocking collectives  24.1 us (7%)
  between operations  14.8 us (4%)
  local copies, waits for them, and re-layouts  11.8 us (3%)
  other arithmetic  8.31 us (2%)
    ppermute x36, waiting for transfers between devices, swap(): return lax.ppermute(value, 'seq', [(i, i ^ mask) for i in range(seats)])  38.1 us
    pallas_call x2, Pallas kernels, feed_forward(): pl.pallas_call(functools.partial(ff_kernel, own, len(ga)), grid=(1,), in_...  34.6 us
    all_gather x1, blocking collectives, first_leg(): lax.all_gather(wqkv, 'dp', axis=1).reshape(width, 3 * wide)  24.1 us
    ppermute x36, starting transfers between devices, swap(): return lax.ppermute(value, 'seq', [(i, i ^ mask) for i in range(seats)])  23.4 us
    all_to_all x1, waiting for transfers between devices, to_all(): return lax.all_to_all(value, every, split_axis=0, concat_axis=0, tiled=True)  22.9 us
    all_to_all x5, starting transfers between devices, to_seats(): lax.all_to_all(value, 'seq', split_axis=0, concat_axis=0, tiled=True, axi...  22 us
    pallas_call x1, Pallas kernels, attn_fwd(): pl.pallas_call(functools.partial(attn_fwd_kernel, order), grid=(micro,),...  21.4 us
    pallas_call x1, Pallas kernels, attn_bwd(): pl.pallas_call(functools.partial(attn_bwd_kernel, order, sent), grid=(mic...  20.6 us
  transfers between devices with their start and end apart: 48, of which 18 were waited for; matrix products, arithmetic and copies ran while one was open for 5% of the time, Pallas kernels for 35%

profile of v2, /device:TPU:0, one launch (start us, length us, event | category | flops | bytes accessed | tf_op | source)
XLA Modules:
  0.0 340.4 jit_solution(18324566817319343675)
XLA Ops:
  10.3 25.4 %conditional.11 = (bf16[8,32,1536]{2,1,0:T(8,128)(2,1)S(1)}, bf16[8,32,384]{2,1,0:T(8,128)(2,1)}, bf16[3,128,1280]{2,1,0:T(8,128)(2,1)S(1)}, bf16[3,128,1536]{2,1,0:T(8,128)(2,1)}, bf16[3,128,1280]{2,1,0:T(8,128)(2,1)}) conditional(s32[]{:T(128)} %bitcast.21, () %tuple.108, (bf16[32,2816]{1,0:T(8,128)(2,1)}, f32[32,1]{0,1:T(1,128)S(1)}, ...), branch_computations={%region_0.1_spmd, %region_1.2_spmd} | conditional | flops 5750784 | bytes 31898080 | solution.py:988
  15.1 5.2 %all-to-all-start.4 = ((bf16[8,32,1920]{2,1,0:T(8,128)(2,1)}), bf16[8,32,1920]{2,1,0:T(8,128)(2,1)S(1)}, u32[]{:S(2)}, u32[]{:S(2)}) async-start(bf16[8,32,1920]{2,1,0:T(8,128)(2,1)} %pad_maximum_fusion), calls=%async_computation.4 | async-start | bytes 1966080 | tf_op jit(solution)/shard_map/cond/branch_1_fun/all_to_all | solution.py:996
  20.2 3.7 %payloads.1 = (bf16[3,128,1280]{2,1,0:T(8,128)(2,1)}, bf16[3,128,1536]{2,1,0:T(8,128)(2,1)}, bf16[3,128,1280]{2,1,0:T(8,128)(2,1)}) custom-call(s32[1]{0:T(128)} %get-tuple-element.295.seat_ref, bf16[3,128,1024]{2,1,0:T(8,128)(2,1)} %get-tuple-element.296.x_ref, bf16[3,128,1024]{2,1,0:T(8,128)(2,1)} %get-tuple-element.685.refs_0_.refs_1_.refs_2_.refs_3_, ...), custom_call_target="tpu_custom_call" | custom-call | bytes 14760000 | tf_op jit(solution)/shard_map/cond/branch_1_fun/payloads/pallas_call | solution.py:593
  23.9 11.0 %all-to-all-done.4 = bf16[8,32,1920]{2,1,0:T(8,128)(2,1)S(1)} async-done(((bf16[8,32,1920]{2,1,0:T(8,128)(2,1)}), bf16[8,32,1920]{2,1,0:T(8,128)(2,1)S(1)}, u32[]{:S(2)}, u32[]{:S(2)}) %all-to-all-start.4) | async-done | bytes 983072 | tf_op jit(solution)/shard_map/cond/branch_1_fun/all_to_all | solution.py:996
  36.7 25.9 %conditional.12 = (bf16[3,128,1280]{2,1,0:T(8,128)(2,1)}, bf16[3,128,1536]{2,1,0:T(8,128)(2,1)}, bf16[1024,384]{1,0:T(8,128)(2,1)}, bf16[3,128,1280]{2,1,0:T(8,128)(2,1)}, bf16[3,128,1024]{2,1,0:T(8,128)(2,1)}) conditional(s32[]{:T(128)} %bitcast.21, () %tuple.110, (bf16[3,128,1280]{2,1,0:T(8,128)(2,1)}, bf16[3,128,1536]{2,1,0:T(8,128)(2,1)}, ...), branch_computations={%region_2.3_spmd, %region_3.4_spmd} | conditional | bytes 16711880 | solution.py:988
  38.5 24.1 %all-gather = bf16[8,128,384]{2,1,0:T(8,128)(2,1)} all-gather(bf16[8,32,384]{2,1,0:T(8,128)(2,1)} %get-tuple-element.303), channel_id=2, replica_groups=mesh['seq'=8,'dp'=4] {'dp'}, dimensions={1}, use_global_device_ids=true | all-gather | bytes 983040 | tf_op jit(solution)/shard_map/cond/branch_1_fun/all_gather | solution.py:1031
  62.7 23.5 %conditional.13 = (bf16[3,128,640]{2,1,0:T(8,128)(2,1)}, bf16[3,128,640]{2,1,0:T(8,128)(2,1)}, bf16[3,128,1280]{2,1,0:T(8,128)(2,1)}, bf16[3,128,1536]{2,1,0:T(8...) conditional(s32[]{:T(128)} %bitcast.21, () %tuple.113, ...), branch_computations={%region_4.5_spmd, %region_5.6_spmd} | conditional | flops 983040 | bytes 24445260 | solution.py:988
  63.3 3.0 collective-permute-start.23
  70.7 2.8 collective-permute-done.23
  74.5 11.6 %collective-permute-done.22 = bf16[4,32,1024]{2,1,0:T(8,128)(2,1)} collective-permute-done((bf16[4,32,1024]{2,1,0:T(8,128)(2,1)}, bf16[4,32,1024]{2,1,0:T(8,128)(2,1)}, u32[]{:S(2)}, u32[]{:S(2)}) %collective-permute-start.22) | collective-permute-done | bytes 262176 | tf_op jit(solution)/shard_map/cond/branch_1_fun/ppermute | solution.py:966
  89.8 27.0 %conditional.14 = (bf16[3,1024,384]{2,1,0:T(8,128)(2,1)}, f32[3,128,1024]{2,1,0:T(8,128)}, bf16[4,3,256,128]{3,2,1,0:T(8,128)(2,1)}, bf16[4,3,256,128]{3,2,1,0:T...) conditional(s32[]{:T(128)} %bitcast.21, () %tuple.116, ...), branch_computations={%region_6.7_spmd, %region_7.8_spmd} | conditional | flops 786432 | bytes 89791032 | solution.py:988
  93.7 21.4 %attn_fwd.1 = (bf16[3,1024,384]{2,1,0:T(8,128)(2,1)}, f32[3,128,1024]{2,1,0:T(8,128)}, bf16[4,3,256,128]{3,2,1,0:T(8,128)(2,1)}, bf16[4,3,256,128]{3,2,1,0:T(8,1...) custom-call(s32[1]{0:T(128)} %get-tuple-element.310.seat_ref, s32[3]{0:T(128)S(1)} %get-tuple-element.311.len_ref, ...), custom_call_target="tpu_custom_call" | custom-call | bytes 73800000 | tf_op jit(solution)/shard_map/cond/branch_1_fun/attn_fwd/pallas_call | solution.py:188
  116.8 16.1 %conditional.15 = (bf16[4,3,256,128]{3,2,1,0:T(8,128)(2,1)}, bf16[2,2,4,32,1024]{4,3,2,1,0:T(8,128)(2,1)}, bf16[1024,384]{1,0:T(8,128)(2,1)}, bf16[1,128,1024]{2,1,0:T(8,128)(2,1)}, bf16[2,128,1024]{2,1,0:T(8,128)(2,1)}) conditional(s32[]{:T(128)} %bitcast.21, () %tuple.115, (bf16[4,3,256,128]{3,2,1,0:T(8,128)(2,1)}, ...), branch_computations={%region_8.9_spmd, %region_9.10_spmd} | conditional | bytes 12845288 | solution.py:988
  117.3 4.2 %all-to-all-start = ((bf16[4,3,256,128]{3,2,1,0:T(8,128)(2,1)}), bf16[4,3,256,128]{3,2,1,0:T(8,128)(2,1)}, u32[]{:S(2)}, u32[]{:S(2)}) async-start(bf16[4,3,256,128]{3,2,1,0:T(8,128)(2,1)} %get-tuple-element.335), calls=%async_computation | async-start | bytes 1572864 | tf_op jit(solution)/shard_map/cond/branch_1_fun/all_to_all | solution.py:996
  122.1 2.1 collective-permute-done.6
  124.2 8.7 %all-to-all-done = bf16[4,3,256,128]{3,2,1,0:T(8,128)(2,1)} async-done(((bf16[4,3,256,128]{3,2,1,0:T(8,128)(2,1)}), bf16[4,3,256,128]{3,2,1,0:T(8,128)(2,1)}, u32[]{:S(2)}, u32[]{:S(2)}) %all-to-all-start) | async-done | bytes 786464 | tf_op jit(solution)/shard_map/cond/branch_1_fun/all_to_all | solution.py:996
  132.9 2.6 collective-permute-done.33
  135.5 22.5 %conditional.16 = (bf16[384,1024]{1,0:T(8,128)(2,1)}, bf16[192,1024]{1,0:T(8,128)(2,1)}, bf16[192,1024]{1,0:T(8,128)(2,1)}, bf16[768,1024]{1,0:T(8,128)(2,1)}, b...) conditional(s32[]{:T(128)} %bitcast.21, () %tuple.112, ...), branch_computations={%region_10.11_spmd, %region_11.12_spmd} | conditional | bytes 61399408 | solution.py:988
  135.5 4.2 %all-to-all-start.1 = ((bf16[4,3,256,128]{3,2,1,0:T(8,128)(2,1)}), bf16[4,3,256,128]{3,2,1,0:T(8,128)(2,1)}, u32[]{:S(2)}, u32[]{:S(2)}) async-start(bf16[4,3,256,128]{3,2,1,0:T(8,128)(2,1)} %get-tuple-element.361), calls=%async_computation.1 | async-start | bytes 1572864 | tf_op jit(solution)/shard_map/cond/branch_1_fun/all_to_all | solution.py:996
  139.7 17.9 %ff_near.1 = (bf16[384,1024]{1,0:T(8,128)(2,1)}, bf16[192,1024]{1,0:T(8,128)(2,1)}, bf16[192,1024]{1,0:T(8,128)(2,1)}, bf16[384,1024]{1,0:T(8,128)(2,1)}, bf16[3...) custom-call(s32[1]{0:T(128)} %get-tuple-element.340.seat_ref, ...), custom_call_target="tpu_custom_call" | custom-call | bytes 59040000 | tf_op jit(solution)/shard_map/cond/branch_1_fun/ff_near/pallas_call | solution.py:465
  158.8 2.4 collective-permute-done.35.refs_0_
  161.7 2.2 add_parts.1
  164.0 20.3 %conditional.17 = (bf16[384,1024]{1,0:T(8,128)(2,1)}, bf16[192,1024]{1,0:T(8,128)(2,1)}, bf16[192,1024]{1,0:T(8,128)(2,1)}, bf16[384,1024]{1,0:T(8,128)(2,1)}, b...) conditional(s32[]{:T(128)} %bitcast.21, () %tuple.107, ...), branch_computations={%region_12.13_spmd, %region_13.14_spmd} | conditional | bytes 72671712 | solution.py:988
  164.0 2.0 collective-permute-start.8
  166.0 16.7 %ff_own.1 = (bf16[384,1024]{1,0:T(8,128)(2,1)}, bf16[192,1024]{1,0:T(8,128)(2,1)}, bf16[192,1024]{1,0:T(8,128)(2,1)}, bf16[384,1024]{1,0:T(8,128)(2,1)}, bf16[38...) custom-call(s32[1]{0:T(128)} %get-tuple-element.364.seat_ref, ...), custom_call_target="tpu_custom_call" | custom-call | bytes 59040000 | tf_op jit(solution)/shard_map/cond/branch_1_fun/ff_own/pallas_call | solution.py:465
  186.9 5.4 %middle_back.1 = (f32[384,1024]{1,0:T(8,128)}, bf16[384,1024]{1,0:T(8,128)(2,1)}, bf16[8,3,128,128]{3,2,1,0:T(8,128)(2,1)}) custom-call(f32[384,1024]{1,0:T(8,128)} %get-tuple-element.622.y_ref, bf16[3,128,1024]{2,1,0:T(8,128)(2,1)} %g_ref.1, bf16[1024,1024]{1,0:T(8,128)(2,1)} %get-tuple-element.623.w_ref, bf16[384,1024]{1,0:T(8,128)(2,1)} %get-tuple-element.624.refs_0_, ...), custom_call_target="tpu_custom_call" | custom-call | tf_op jit(solution)/shard_map/middle_back/pallas_call | solution.py:636
  192.3 20.8 %conditional.18 = (bf16[8,3,128,128]{3,2,1,0:T(8,128)(2,1)}, bf16[4,8,32,1536]{3,2,1,0:T(8,128)(2,1)}, bf16[4,96,1024]{2,1,0:T(8,128)(2,1)}, bf16[128,1024]{1,0:...) conditional(s32[]{:T(128)} %bitcast.21, () %tuple.106, ...), branch_computations={%region_14.15_spmd, %region_15.16_spmd} | conditional | bytes 63456676 | solution.py:988
  192.8 4.2 %all-to-all-start.2 = ((bf16[8,3,128,128]{3,2,1,0:T(8,128)(2,1)}), bf16[8,3,128,128]{3,2,1,0:T(8,128)(2,1)}, u32[]{:S(2)}, u32[]{:S(2)}) async-start(bf16[8,3,128,128]{3,2,1,0:T(8,128)(2,1)} %get-tuple-element.389), calls=%async_computation.2 | async-start | bytes 1572864 | tf_op jit(solution)/shard_map/cond/branch_1_fun/all_to_all | solution.py:996
  197.0 16.1 %ff_grads.1 = (bf16[4,8,32,1536]{3,2,1,0:T(8,128)(2,1)}, bf16[4,96,1024]{2,1,0:T(8,128)(2,1)}, bf16[128,1024]{1,0:T(8,128)(2,1)}, bf16[512,1024]{1,0:T(8,128)(2,...) custom-call(s32[1]{0:T(128)} %get-tuple-element.390.seat_ref, bf16[768,1024]{1,0:T(8,128)(2,1)} %get-tuple-element.391.refs_0_, ...), custom_call_target="tpu_custom_call" | custom-call | bytes 51660000 | tf_op jit(solution)/shard_map/cond/branch_1_fun/ff_grads/pallas_call | solution.py:552
  213.1 33.1 %conditional.19 = (bf16[4,3,128,512]{3,2,1,0:T(8,128)(2,1)}, bf16[4,3,128,512]{3,2,1,0:T(8,128)(2,1)}, bf16[1024,384]{1,0:T(8,128)(2,1)}, bf16[512,1024]{1,0:T(8...) conditional(s32[]{:T(128)} %bitcast.21, () %tuple.105, (s32[1]{0:T(128)}, s32[3]{0:T(128)S(1)}, ...), branch_computations={%region_16.17_spmd, %region_17.18_spmd} | conditional | bytes 89266720 | solution.py:988
  216.9 20.6 %attn_bwd.1 = (bf16[4,3,128,512]{3,2,1,0:T(8,128)(2,1)}, bf16[4,3,128,512]{3,2,1,0:T(8,128)(2,1)}, bf16[1024,384]{1,0:T(8,128)(2,1)}) custom-call(s32[1]{0:T(128)} %get-tuple-element.415.seat_ref, s32[3]{0:T(128)S(1)} %get-tuple-element.416.len_ref, bf16[8,3,128,128]{3,2,1,0:T(8,128)(2,1)} %get-tuple-element.417.do_ref, ...), custom_call_target="tpu_custom_call" | custom-call | bytes 73800000 | tf_op jit(solution)/shard_map/cond/branch_1_fun/attn_bwd/pallas_call | solution.py:310
  237.6 8.4 %collective-permute-done.13 = bf16[128,1024]{1,0:T(8,128)(2,1)} collective-permute-done((bf16[128,1024]{1,0:T(8,128)(2,1)}, bf16[128,1024]{1,0:T(8,128)(2,1)}, u32[]{:S(2)}, u32[]{:S(2)}) %collective-permute-start.13) | collective-permute-done | bytes 262176 | tf_op jit(solution)/shard_map/cond/branch_1_fun/ppermute | solution.py:966
  246.2 43.5 %conditional.20 = (bf16[3,128,1280]{2,1,0:T(8,128)(2,1)S(1)}, bf16[3,128,1280]{2,1,0:T(8,128)(2,1)}, bf16[3,128,1280]{2,1,0:T(8,128)(2,1)}, bf16[3,128,1280]{2,1...) conditional(s32[]{:T(128)} %bitcast.21, () %tuple.104, ...), branch_computations={%region_18.19_spmd, %region_19.20_spmd} | conditional | flops 2752512 | bytes 46761852 | solution.py:988
  246.2 5.1 %all-to-all-start.5 = ((bf16[32,32,384]{2,1,0:T(8,128)(2,1)}), bf16[32,32,384]{2,1,0:T(8,128)(2,1)}, u32[]{:S(2)}, u32[]{:S(2)}) async-start(bf16[32,32,384]{2,1,0:T(8,128)(2,1)} %bitcast.13), calls=%async_computation.5 | async-start | bytes 1572864 | tf_op jit(solution)/shard_map/cond/branch_1_fun/all_to_all | solution.py:1001
  251.6 6.4 %back_to_x.1 = (bf16[3,128,1280]{2,1,0:T(8,128)(2,1)}, bf16[3,128,1280]{2,1,0:T(8,128)(2,1)}, bf16[3,128,1280]{2,1,0:T(8,128)(2,1)}, bf16[3,128,1280]{2,1,0:T(8,128)(2,1)}) custom-call(s32[1]{0:T(128)} %get-tuple-element.440.seat_ref, bf16[4,3,128,512]{3,2,1,0:T(8,128)(2,1)} %get-tuple-element.441.a_ref, ...), custom_call_target="tpu_custom_call" | custom-call | bytes 18450000 | tf_op jit(solution)/shard_map/cond/branch_1_fun/back_to_x/pallas_call | solution.py:683
  261.2 3.1 plane_sums.1
  264.3 2.4 add_convert_fusion
  266.7 22.9 %all-to-all-done.5 = bf16[32,32,384]{2,1,0:T(8,128)(2,1)} async-done(((bf16[32,32,384]{2,1,0:T(8,128)(2,1)}), bf16[32,32,384]{2,1,0:T(8,128)(2,1)}, u32[]{:S(2)}, u32[]{:S(2)}) %all-to-all-start.5) | async-done | bytes 786464 | tf_op jit(solution)/shard_map/cond/branch_1_fun/all_to_all | solution.py:1001
  290.5 38.9 %conditional.21 = (bf16[3,128,1280]{2,1,0:T(8,128)(2,1)}, f32[3,128,1024]{2,1,0:T(8,128)}, f32[3,128,1024]{2,1,0:T(8,128)}, f32[32,2816]{1,0:T(8,128)}, f32[32,2...) conditional(s32[]{:T(128)} %bitcast.21, () %tuple.124, ...), branch_computations={%region_21.22_spmd, %region_22.23_spmd} | conditional | bytes 10158892 | solution.py:988
  290.5 2.4 collective-permute-start.14
  292.9 4.2 %all-to-all-start.3 = ((bf16[8,32,1536]{2,1,0:T(8,128)(2,1)}), bf16[8,32,1536]{2,1,0:T(8,128)(2,1)}, u32[]{:S(2)}, u32[]{:S(2)}) async-start(bf16[8,32,1536]{2,1,0:T(8,128)(2,1)} %bitcast.51), calls=%async_computation.3 | async-start | bytes 1572864 | tf_op jit(solution)/shard_map/cond/branch_1_fun/all_to_all | solution.py:996
  297.1 2.2 collective-permute-start.17
  303.0 2.0 projection_grads.1
  305.0 3.9 %token_sums.1 = (f32[3,128,1024]{2,1,0:T(8,128)}, f32[3,128,1024]{2,1,0:T(8,128)}) custom-call(s32[1]{0:T(128)} %get-tuple-element.464.seat_ref, bf16[3,128,1280]{2,1,0:T(8,128)(2,1)S(1)} %get-tuple-element.465.refs_0_, bf16[3,128,1280]{2,1,0:T(8,128)(2,1)} %get-tuple-element.466.refs_1_, bf16[3,128,1280]{2,1,0:T(8,128)(2,1)} %get-tuple-element.467.refs_2_), custom_call_target="tpu_custom_call" | custom-call | tf_op jit(solution)/shard_map/cond/branch_1_fun/token_sums/pallas_call | solution.py:810
  308.9 15.8 %collective-permute-done.16.refs_2_ = bf16[128,1024]{1,0:T(8,128)(2,1)} collective-permute-done((bf16[128,1024]{1,0:T(8,128)(2,1)}, bf16[128,1024]{1,0:T(8,128)(2,1)}, u32[]{:S(2)}, u32[]{:S(2)}) %collective-permute-start.16) | collective-permute-done | bytes 262176 | tf_op jit(solution)/shard_map/cond/branch_1_fun/ppermute | solution.py:972
  324.7 2.0 tail_grads.1
  326.8 2.7 pair_grads.1
  329.4 4.2 %token_grads.1 = (f32[3,128,1024]{2,1,0:T(8,128)}, f32[3,128,1024]{2,1,0:T(8,128)}) custom-call(s32[1]{0:T(128)} %bitcast.22.seat_ref, bf16[3,128,1024]{2,1,0:T(8,128)(2,1)S(1)} %copy-done.8, f32[384,1024]{1,0:T(8,128)S(1)} %copy-done, f32[3,128,1024]{2,1,0:T(8,128)} %get-tuple-element.672.dx_ref, ...), custom_call_target="tpu_custom_call", output_to_operand_aliasing={{1}: (5, {})} | custom-call | tf_op jit(solution)/shard_map/token_grads/pallas_call | solution.py:849
  (159 shorter events, 44.2 us)
Async XLA Ops:
  7.2 55.5 %all-gather.6.cloned.1.call-start = ((), (), s32[]{:S(2)}) async-start(), calls=%async_computation.8 | async-start | bytes 1310720 | tf_op jit(solution)/shard_map/all_gather | solution.py:1006
  8.9 126.6 %all-gather.8.cloned.1.call-start = ((), (), s32[]{:S(2)}) async-start(), calls=%async_computation.9 | async-start | bytes 3932160 | tf_op jit(solution)/shard_map/all_gather | solution.py:1026
  15.1 19.9 %all-to-all-start.4 = ((bf16[8,32,1920]{2,1,0:T(8,128)(2,1)}), bf16[8,32,1920]{2,1,0:T(8,128)(2,1)S(1)}, u32[]{:S(2)}, u32[]{:S(2)}) async-start(bf16[8,32,1920]{2,1,0:T(8,128)(2,1)} %pad_maximum_fusion), calls=%async_computation.4 | async-start | bytes 1966080 | tf_op jit(solution)/shard_map/cond/branch_1_fun/all_to_all | solution.py:996
  36.7 253.0 %reduce-scatter.2.cloned.1.call-start = ((), (), s32[]{:S(2)}) async-start(), calls=%async_computation.7 | async-start | bytes 3932160 | tf_op jit(solution)/shard_map/reduce_scatter | solution.py:1128
  36.7 25.9 %collective-permute-start.1 = (bf16[3,128,1536]{2,1,0:T(8,128)(2,1)}, bf16[3,128,1536]{2,1,0:T(8,128)(2,1)}, u32[]{:S(2)}, u32[]{:S(2)}) collective-permute-start(bf16[3,128,1536]{2,1,0:T(8,128)(2,1)} %get-tuple-element.302), channel_id=1, source_target_pairs={{0,16},{4,20},{8,24},{12,28},{16,0},{20,4},{24,8},{28,12},{1,17},{... | collective-permute-start | bytes 3538952 | tf_op jit(solution)/shard_map/cond/branch_1_fun/ppermute | solution.py:966
  37.4 25.2 %collective-permute-start = (bf16[3,128,1280]{2,1,0:T(8,128)(2,1)}, bf16[3,128,1280]{2,1,0:T(8,128)(2,1)}, u32[]{:S(2)}, u32[]{:S(2)}) collective-permute-start(bf16[3,128,1280]{2,1,0:T(8,128)(2,1)} %get-tuple-element.301), channel_id=1, source_target_pairs={{0,8},{4,12},{8,0},{12,4},{16,24},{20,28},{24,16},{28,20},{1,9},{5... | collective-permute-start | bytes 2949128 | tf_op jit(solution)/shard_map/cond/branch_1_fun/ppermute | solution.py:966
  38.0 24.6 %collective-permute-start.2 = (bf16[3,128,1280]{2,1,0:T(8,128)(2,1)S(1)}, bf16[3,128,1280]{2,1,0:T(8,128)(2,1)}, u32[]{:S(2)}, u32[]{:S(2)}) collective-permute-start(bf16[3,128,1280]{2,1,0:T(8,128)(2,1)S(1)} %get-tuple-element.304), channel_id=1, source_target_pairs={{0,4},{4,0},{8,12},{12,8},{16,20},{20,16},{24,28},{28,24},{1,5},{5... | collective-permute-start | bytes 2949128 | tf_op jit(solution)/shard_map/cond/branch_1_fun/ppermute | solution.py:966
  38.0 24.6 %collective-permute-start.3 = (bf16[3,128,1024]{2,1,0:T(8,128)(2,1)S(1)}, bf16[3,128,1024]{2,1,0:T(8,128)(2,1)}, u32[]{:S(2)}, u32[]{:S(2)}) collective-permute-start(bf16[3,128,1024]{2,1,0:T(8,128)(2,1)S(1)} %get-tuple-element.305), channel_id=1, source_target_pairs={{0,4},{4,0},{8,12},{12,8},{16,20},{20,16},{24,28},{28,24},{1,5},{5... | collective-permute-start | bytes 2359304 | tf_op jit(solution)/shard_map/cond/branch_1_fun/ppermute | solution.py:966
  62.7 23.5 %collective-permute-start.21 = (bf16[3,128,1536]{2,1,0:T(8,128)(2,1)}, bf16[3,128,1536]{2,1,0:T(8,128)(2,1)}, u32[]{:S(2)}, u32[]{:S(2)}) collective-permute-start(bf16[3,128,1536]{2,1,0:T(8,128)(2,1)} %get-tuple-element.307), channel_id=1, source_target_pairs={{0,4},{4,0},{8,12},{12,8},{16,20},{20,16},{24,28},{28,24},{1,5},{5... | collective-permute-start | bytes 3538952 | tf_op jit(solution)/shard_map/cond/branch_1_fun/ppermute | solution.py:966
  62.8 23.4 %collective-permute-start.20 = (bf16[3,128,1280]{2,1,0:T(8,128)(2,1)}, bf16[3,128,1280]{2,1,0:T(8,128)(2,1)}, u32[]{:S(2)}, u32[]{:S(2)}) collective-permute-start(bf16[3,128,1280]{2,1,0:T(8,128)(2,1)} %get-tuple-element.306), channel_id=1, source_target_pairs={{0,4},{4,0},{8,12},{12,8},{16,20},{20,16},{24,28},{28,24},{1,5},{5... | collective-permute-start | bytes 2949128 | tf_op jit(solution)/shard_map/cond/branch_1_fun/ppermute | solution.py:966
  63.3 10.3 %collective-permute-start.23 = (bf16[1,128,1024]{2,1,0:T(8,128)(2,1)S(1)}, bf16[1,128,1024]{2,1,0:T(8,128)(2,1)}, u32[]{:S(2)}, u32[]{:S(2)}) collective-permute-start(bf16[1,128,1024]{2,1,0:T(8,128)(2,1)S(1)} %slice.27), channel_id=1, source_target_pairs={{0,8},{4,12},{8,0},{12,4},{16,24},{20,28},{24,16},{28,20},{1,9},{5... | collective-permute-start | bytes 786440 | tf_op jit(solution)/shard_map/cond/branch_1_fun/ppermute | solution.py:966
  67.4 18.7 %collective-permute-start.18 = (bf16[3,128,640]{2,1,0:T(8,128)(2,1)S(1)}, bf16[3,128,640]{2,1,0:T(8,128)(2,1)}, u32[]{:S(2)}, u32[]{:S(2)}) collective-permute-start(bf16[3,128,640]{2,1,0:T(8,128)(2,1)S(1)} %slice.22), channel_id=1, source_target_pairs={{0,16},{4,20},{8,24},{12,28},{16,0},{20,4},{24,8},{28,12},{1,17},{... | collective-permute-start | bytes 1474568 | tf_op jit(solution)/shard_map/cond/branch_1_fun/ppermute | solution.py:966
  69.9 16.3 %collective-permute-start.19 = (bf16[3,128,640]{2,1,0:T(8,128)(2,1)S(1)}, bf16[3,128,640]{2,1,0:T(8,128)(2,1)}, u32[]{:S(2)}, u32[]{:S(2)}) collective-permute-start(bf16[3,128,640]{2,1,0:T(8,128)(2,1)S(1)} %pad_maximum_fusion.1), channel_id=1, source_target_pairs={{0,8},{4,12},{8,0},{12,4},{16,24},{20,28},{24,16},{28,20},{1,9},{5... | collective-permute-start | bytes 1474568 | tf_op jit(solution)/shard_map/cond/branch_1_fun/ppermute | solution.py:966
  73.6 12.6 %collective-permute-start.22 = (bf16[4,32,1024]{2,1,0:T(8,128)(2,1)}, bf16[4,32,1024]{2,1,0:T(8,128)(2,1)}, u32[]{:S(2)}, u32[]{:S(2)}) collective-permute-start(bf16[4,32,1024]{2,1,0:T(8,128)(2,1)} %slice.47), channel_id=1, source_target_pairs={{0,16},{4,20},{8,24},{12,28},{16,0},{20,4},{24,8},{28,12},{1,17},{... | collective-permute-start | bytes 786440 | tf_op jit(solution)/shard_map/cond/branch_1_fun/ppermute | solution.py:966
  86.2 2.1 collective-permute-start.31
  86.2 2.8 collective-permute-start.32
  90.0 26.8 %collective-permute-start.24 = (bf16[4,96,1024]{2,1,0:T(8,128)(2,1)}, bf16[4,96,1024]{2,1,0:T(8,128)(2,1)}, u32[]{:S(2)}, u32[]{:S(2)}) collective-permute-start(bf16[4,96,1024]{2,1,0:T(8,128)(2,1)} %get-tuple-element.331), channel_id=1, source_target_pairs={{0,16},{4,20},{8,24},{12,28},{16,0},{20,4},{24,8},{28,12},{1,17},{... | collective-permute-start | bytes 2359304 | tf_op jit(solution)/shard_map/cond/branch_1_fun/ppermute | solution.py:966
  91.5 23.6 %collective-permute-start.25 = (bf16[2,4,32,1024]{3,2,1,0:T(8,128)(2,1)S(1)}, bf16[2,4,32,1024]{3,2,1,0:T(8,128)(2,1)S(1)}, u32[]{:S(2)}, u32[]{:S(2)}) collective-permute-start(bf16[2,4,32,1024]{3,2,1,0:T(8,128)(2,1)S(1)} %get-tuple-element.738), channel_id=1, source_target_pairs={{0,8},{4,12},{8,0},{12,4},{16,24},{20,28},{24,16},{28,20},{1,9},{5... | collective-permute-start | bytes 1572872 | tf_op jit(solution)/shard_map/cond/branch_1_fun/ppermute | solution.py:966
  92.0 24.8 %collective-permute-start.26 = (bf16[2,128,1024]{2,1,0:T(8,128)(2,1)S(1)}, bf16[2,128,1024]{2,1,0:T(8,128)(2,1)}, u32[]{:S(2)}, u32[]{:S(2)}) collective-permute-start(bf16[2,128,1024]{2,1,0:T(8,128)(2,1)S(1)} %slice.28), channel_id=1, source_target_pairs={{0,8},{4,12},{8,0},{12,4},{16,24},{20,28},{24,16},{28,20},{1,9},{5... | collective-permute-start | bytes 1572872 | tf_op jit(solution)/shard_map/cond/branch_1_fun/ppermute | solution.py:966
  116.8 16.1 %collective-permute-start.4 = (bf16[2,2,4,32,1024]{4,3,2,1,0:T(8,128)(2,1)S(1)}, bf16[2,2,4,32,1024]{4,3,2,1,0:T(8,128)(2,1)}, u32[]{:S(2)}, u32[]{:S(2)}) collective-permute-start(bf16[2,2,4,32,1024]{4,3,2,1,0:T(8,128)(2,1)S(1)} %get-tuple-element.336), channel_id=1, source_target_pairs={{0,4},{4,0},{8,12},{12,8},{16,20},{20,16},{24,28},{28,24},{1,5},{5... | collective-permute-start | bytes 3145736 | tf_op jit(solution)/shard_map/cond/branch_1_fun/ppermute | solution.py:966
  116.8 16.1 %collective-permute-start.5 = (bf16[1024,384]{1,0:T(8,128)(2,1)}, bf16[1024,384]{1,0:T(8,128)(2,1)}, u32[]{:S(2)}, u32[]{:S(2)}) collective-permute-start(bf16[1024,384]{1,0:T(8,128)(2,1)} %get-tuple-element.337), channel_id=1, source_target_pairs={{0,4},{4,0},{8,12},{12,8},{16,20},{20,16},{24,28},{28,24},{1,5},{5... | collective-permute-start | bytes 2359304 | tf_op jit(solution)/shard_map/cond/branch_1_fun/ppermute | solution.py:966
  117.3 15.6 %all-to-all-start = ((bf16[4,3,256,128]{3,2,1,0:T(8,128)(2,1)}), bf16[4,3,256,128]{3,2,1,0:T(8,128)(2,1)}, u32[]{:S(2)}, u32[]{:S(2)}) async-start(bf16[4,3,256,128]{3,2,1,0:T(8,128)(2,1)} %get-tuple-element.335), calls=%async_computation | async-start | bytes 1572864 | tf_op jit(solution)/shard_map/cond/branch_1_fun/all_to_all | solution.py:996
  121.5 2.7 collective-permute-start.7
  121.6 2.6 collective-permute-start.6
  132.9 2.6 collective-permute-start.33
  135.5 22.1 %all-to-all-start.1 = ((bf16[4,3,256,128]{3,2,1,0:T(8,128)(2,1)}), bf16[4,3,256,128]{3,2,1,0:T(8,128)(2,1)}, u32[]{:S(2)}, u32[]{:S(2)}) async-start(bf16[4,3,256,128]{3,2,1,0:T(8,128)(2,1)} %get-tuple-element.361), calls=%async_computation.1 | async-start | bytes 1572864 | tf_op jit(solution)/shard_map/cond/branch_1_fun/all_to_all | solution.py:996
  158.1 5.9 %collective-permute-start.34 = (bf16[4,3,256,128]{3,2,1,0:T(8,128)(2,1)}, bf16[4,3,256,128]{3,2,1,0:T(8,128)(2,1)S(1)}, u32[]{:S(2)}, u32[]{:S(2)}) collective-permute-start(bf16[4,3,256,128]{3,2,1,0:T(8,128)(2,1)} %get-tuple-element.617), channel_id=1, source_target_pairs={{0,4},{4,0},{8,12},{12,8},{16,20},{20,16},{24,28},{28,24},{1,5},{5... | collective-permute-start | bytes 2359304 | tf_op jit(solution)/shard_map/ppermute | solution.py:966
  158.3 2.9 collective-permute-start.35
  158.6 3.1 collective-permute-start.36
  164.0 20.1 %collective-permute-start.8 = (bf16[384,1024]{1,0:T(8,128)(2,1)}, bf16[384,1024]{1,0:T(8,128)(2,1)}, u32[]{:S(2)}, u32[]{:S(2)}) collective-permute-start(bf16[384,1024]{1,0:T(8,128)(2,1)} %get-tuple-element.388), channel_id=1, source_target_pairs={{0,8},{4,12},{8,0},{12,4},{16,24},{20,28},{24,16},{28,20},{1,9},{5... | collective-permute-start | bytes 2359304 | tf_op jit(solution)/shard_map/cond/branch_1_fun/ppermute | solution.py:966
  184.3 2.0 collective-permute-start.37
  184.4 2.5 collective-permute-start.38
  192.3 4.7 %collective-permute-start.10 = (bf16[1,384,1024]{2,1,0:T(8,128)(2,1)}, bf16[1,384,1024]{2,1,0:T(8,128)(2,1)}, u32[]{:S(2)}, u32[]{:S(2)}) collective-permute-start(bf16[1,384,1024]{2,1,0:T(8,128)(2,1)} %get-tuple-element.408), channel_id=1, source_target_pairs={{0,4},{4,0},{8,12},{12,8},{16,20},{20,16},{24,28},{28,24},{1,5},{5... | collective-permute-start | bytes 2359304 | tf_op jit(solution)/shard_map/cond/branch_1_fun/ppermute | solution.py:966
  192.4 4.6 %collective-permute-start.9 = (bf16[384,1024]{1,0:T(8,128)(2,1)}, bf16[384,1024]{1,0:T(8,128)(2,1)}, u32[]{:S(2)}, u32[]{:S(2)}) collective-permute-start(bf16[384,1024]{1,0:T(8,128)(2,1)} %get-tuple-element.406.refs_15_), channel_id=1, source_target_pairs={{0,4},{4,0},{8,12},{12,8},{16,20},{20,16},{24,28},{28,24},{1,5},{5... | collective-permute-start | bytes 2359304 | tf_op jit(solution)/shard_map/cond/branch_1_fun/ppermute | solution.py:966
  192.8 20.3 %all-to-all-start.2 = ((bf16[8,3,128,128]{3,2,1,0:T(8,128)(2,1)}), bf16[8,3,128,128]{3,2,1,0:T(8,128)(2,1)}, u32[]{:S(2)}, u32[]{:S(2)}) async-start(bf16[8,3,128,128]{3,2,1,0:T(8,128)(2,1)} %get-tuple-element.389), calls=%async_computation.2 | async-start | bytes 1572864 | tf_op jit(solution)/shard_map/cond/branch_1_fun/all_to_all | solution.py:996
  213.4 32.7 %collective-permute-start.11 = (bf16[512,1024]{1,0:T(8,128)(2,1)}, bf16[512,1024]{1,0:T(8,128)(2,1)}, u32[]{:S(2)}, u32[]{:S(2)}) collective-permute-start(bf16[512,1024]{1,0:T(8,128)(2,1)} %get-tuple-element.437), channel_id=1, source_target_pairs={{0,8},{4,12},{8,0},{12,4},{16,24},{20,28},{24,16},{28,20},{1,9},{5... | collective-permute-start | bytes 3145736 | tf_op jit(solution)/shard_map/cond/branch_1_fun/ppermute | solution.py:966
  215.3 30.9 %collective-permute-start.12 = (bf16[512,1024]{1,0:T(8,128)(2,1)}, bf16[512,1024]{1,0:T(8,128)(2,1)}, u32[]{:S(2)}, u32[]{:S(2)}) collective-permute-start(bf16[512,1024]{1,0:T(8,128)(2,1)} %get-tuple-element.438), channel_id=1, source_target_pairs={{0,16},{4,20},{8,24},{12,28},{16,0},{20,4},{24,8},{28,12},{1,17},{... | collective-permute-start | bytes 3145736 | tf_op jit(solution)/shard_map/cond/branch_1_fun/ppermute | solution.py:966
  216.8 29.2 %collective-permute-start.13 = (bf16[128,1024]{1,0:T(8,128)(2,1)}, bf16[128,1024]{1,0:T(8,128)(2,1)}, u32[]{:S(2)}, u32[]{:S(2)}) collective-permute-start(bf16[128,1024]{1,0:T(8,128)(2,1)} %get-tuple-element.439), channel_id=1, source_target_pairs={{0,24},{4,28},{8,16},{12,20},{16,8},{20,12},{24,0},{28,4},{1,25},{... | collective-permute-start | bytes 786440 | tf_op jit(solution)/shard_map/cond/branch_1_fun/ppermute | solution.py:966
  246.2 5.4 %collective-permute-start.27 = (bf16[4,3,128,512]{3,2,1,0:T(8,128)(2,1)}, bf16[4,3,128,512]{3,2,1,0:T(8,128)(2,1)S(1)}, u32[]{:S(2)}, u32[]{:S(2)}) collective-permute-start(bf16[4,3,128,512]{3,2,1,0:T(8,128)(2,1)} %get-tuple-element.442), channel_id=1, source_target_pairs={{0,4},{4,0},{8,12},{12,8},{16,20},{20,16},{24,28},{28,24},{1,5},{5... | collective-permute-start | bytes 4718600 | tf_op jit(solution)/shard_map/cond/branch_1_fun/ppermute | solution.py:966
  246.2 43.4 %all-to-all-start.5 = ((bf16[32,32,384]{2,1,0:T(8,128)(2,1)}), bf16[32,32,384]{2,1,0:T(8,128)(2,1)}, u32[]{:S(2)}, u32[]{:S(2)}) async-start(bf16[32,32,384]{2,1,0:T(8,128)(2,1)} %bitcast.13), calls=%async_computation.5 | async-start | bytes 1572864 | tf_op jit(solution)/shard_map/cond/branch_1_fun/all_to_all | solution.py:1001
  251.3 12.9 %collective-permute-start.30 = (bf16[384,1024]{1,0:T(8,128)(2,1)}, bf16[384,1024]{1,0:T(8,128)(2,1)S(1)}, u32[]{:S(2)}, u32[]{:S(2)}) collective-permute-start(bf16[384,1024]{1,0:T(8,128)(2,1)} %get-tuple-element.462), channel_id=1, source_target_pairs={{0,4},{4,0},{8,12},{12,8},{16,20},{20,16},{24,28},{28,24},{1,5},{5... | collective-permute-start | bytes 2359304 | tf_op jit(solution)/shard_map/cond/branch_1_fun/ppermute | solution.py:966
  258.0 31.7 %collective-permute-start.28 = (bf16[3,128,1280]{2,1,0:T(8,128)(2,1)}, bf16[3,128,1280]{2,1,0:T(8,128)(2,1)}, u32[]{:S(2)}, u32[]{:S(2)}) collective-permute-start(bf16[3,128,1280]{2,1,0:T(8,128)(2,1)} %get-tuple-element.446), channel_id=1, source_target_pairs={{0,8},{4,12},{8,0},{12,4},{16,24},{20,28},{24,16},{28,20},{1,9},{5... | collective-permute-start | bytes 2949128 | tf_op jit(solution)/shard_map/cond/branch_1_fun/ppermute | solution.py:966
  259.7 29.9 %collective-permute-start.29 = (bf16[3,128,1280]{2,1,0:T(8,128)(2,1)}, bf16[3,128,1280]{2,1,0:T(8,128)(2,1)}, u32[]{:S(2)}, u32[]{:S(2)}) collective-permute-start(bf16[3,128,1280]{2,1,0:T(8,128)(2,1)} %get-tuple-element.447), channel_id=1, source_target_pairs={{0,16},{4,20},{8,24},{12,28},{16,0},{20,4},{24,8},{28,12},{1,17},{... | collective-permute-start | bytes 2949128 | tf_op jit(solution)/shard_map/cond/branch_1_fun/ppermute | solution.py:966
  290.5 38.9 %collective-permute-start.14 = (bf16[3,128,1280]{2,1,0:T(8,128)(2,1)}, bf16[3,128,1280]{2,1,0:T(8,128)(2,1)}, u32[]{:S(2)}, u32[]{:S(2)}) collective-permute-start(bf16[3,128,1280]{2,1,0:T(8,128)(2,1)} %get-tuple-element.463), channel_id=1, source_target_pairs={{0,24},{4,28},{8,16},{12,20},{16,8},{20,12},{24,0},{28,4},{1,25},{... | collective-permute-start | bytes 2949128 | tf_op jit(solution)/shard_map/cond/branch_1_fun/ppermute | solution.py:966
  292.9 33.8 %all-to-all-start.3 = ((bf16[8,32,1536]{2,1,0:T(8,128)(2,1)}), bf16[8,32,1536]{2,1,0:T(8,128)(2,1)}, u32[]{:S(2)}, u32[]{:S(2)}) async-start(bf16[8,32,1536]{2,1,0:T(8,128)(2,1)} %bitcast.51), calls=%async_computation.3 | async-start | bytes 1572864 | tf_op jit(solution)/shard_map/cond/branch_1_fun/all_to_all | solution.py:996
  297.1 11.7 %collective-permute-start.17 = (bf16[128,1024]{1,0:T(8,128)(2,1)}, bf16[128,1024]{1,0:T(8,128)(2,1)}, u32[]{:S(2)}, u32[]{:S(2)}) collective-permute-start(bf16[128,1024]{1,0:T(8,128)(2,1)} %get-tuple-element.483), channel_id=1, source_target_pairs={{0,3},{1,2},{2,1},{3,0},{4,7},{5,6},{6,5},{7,4},{8,11},{9,10},{10,... | collective-permute-start | bytes 786440 | tf_op jit(solution)/shard_map/cond/branch_1_fun/ppermute | solution.py:972
  299.4 25.3 %collective-permute-start.16 = (bf16[128,1024]{1,0:T(8,128)(2,1)}, bf16[128,1024]{1,0:T(8,128)(2,1)}, u32[]{:S(2)}, u32[]{:S(2)}) collective-permute-start(bf16[128,1024]{1,0:T(8,128)(2,1)} %get-tuple-element.482), channel_id=1, source_target_pairs={{0,2},{1,3},{2,0},{3,1},{4,6},{5,7},{6,4},{7,5},{8,10},{9,11},{10,... | collective-permute-start | bytes 786440 | tf_op jit(solution)/shard_map/cond/branch_1_fun/ppermute | solution.py:972
  301.2 23.5 %collective-permute-start.15 = (bf16[128,1024]{1,0:T(8,128)(2,1)}, bf16[128,1024]{1,0:T(8,128)(2,1)}, u32[]{:S(2)}, u32[]{:S(2)}) collective-permute-start(bf16[128,1024]{1,0:T(8,128)(2,1)} %get-tuple-element.481), channel_id=1, source_target_pairs={{0,1},{1,0},{2,3},{3,2},{4,5},{5,4},{6,7},{7,6},{8,9},{9,8},{10,11... | collective-permute-start | bytes 786440 | tf_op jit(solution)/shard_map/cond/branch_1_fun/ppermute | solution.py:972
  (25 other events, 304.1 us)
Sparse Core Ops, SparseCore 0:
  10.2 30.6 all-gather.5
  42.4 66.3 all-gather.7
  213.2 74.3 reduce-scatter.1
